TPU v7x, 128 devices: a whole 4x4x4 slice. The times are simulated.
128 devices in a mesh: dp: 4 (over x_hi, core), section: 4 (over z), tensor: 8 (over x_lo, y).
Axes of the slice: x: 4 (x_hi: 2, x_lo: 2; x = x_hi * 2 + x_lo), y: 4, z: 4, core: 2. Of those that a mesh axis runs over, the one named last changes fastest.
Arguments:
- embeds: bfloat16 [8, 128, 4096], P('dp', None, 'tensor'), may hold values from -6 to 6
- source: int32 [8], replicated, may hold values from 0 to 7, each once
- lengths: int32 [8], replicated, may hold values from 32 to 128, as said below
- bounds: int32 [8, 4], replicated, may hold values from 0 to 127, as said below
- targets: int32 [8, 4], replicated, may hold values from 0 to 127
- w_query: bfloat16 [4, 4096, 4096], P('section', None, 'tensor'), may hold values from -0.09375 to 0.09375
- w_key: bfloat16 [4, 4096, 1024], P('section', None, 'tensor'), may hold values from -0.09375 to 0.09375
- w_value: bfloat16 [4, 4096, 1024], P('section', None, 'tensor'), may hold values from -0.09375 to 0.09375
- w_out: bfloat16 [4, 4096, 4096], P('section', 'tensor'), may hold values from -0.09375 to 0.09375
- w_class: bfloat16 [4096, 128], P('tensor'), may hold values from -0.09375 to 0.09375
Outputs:
- grad_query: float32 [4, 4096, 4096], P('section', 'dp', 'tensor')
- grad_key: float32 [4, 4096, 1024], P('section', 'dp', 'tensor')
- grad_value: float32 [4, 4096, 1024], P('section', 'dp', 'tensor')
- grad_out: float32 [4, 4096, 4096], P('section', 'tensor', 'dp')
Inputs may be any that keep to these rules, and one draw needn't show every extreme that they name: `lengths`: a trace's length is at least 32; some trace has exactly 128 tokens. `bounds`: within a trace the step ends rise strictly and the last is its length minus one. `source`: each trace fills exactly one slot.
All inputs are finite; a program needn't handle non-finite values.
Results may differ from a plain program's by a relative error of at most 0.04.
Values may be sent and summed in bfloat16 or wider, within the bound.
No kernel may reach another device: no remote copies, remote signals or barrier semaphores. Data moves between devices by JAX's collectives and lax.ppermute only.
A program may use at most 320 MiB of HBM per device.

v0:
```python
import jax
import jax.numpy as jnp
from jax import lax
from jax.sharding import PartitionSpec as P

HEAD_DIM = 128


EPS = 1e-06
LOSS_SCALE = 16384.0


def passed_along(x, axis, by):
    peers = lax.axis_size(axis)
    pairs = [(i, i + by) for i in range(peers) if 0 <= i + by < peers]
    return lax.ppermute(x, axis, pairs)


def visible(lens, width):
    posq = jnp.arange(width, dtype=jnp.int32)[:, None]
    posk = jnp.arange(width, dtype=jnp.int32)[None, :]
    allowed = (posk <= posq)[None] & (posk[None] < lens[:, None, None])
    return allowed.astype(jnp.float32)


def norm_rows(full):
    xf = full.astype(jnp.float32)
    scale = lax.rsqrt(jnp.mean(xf * xf, axis=-1, keepdims=True) + EPS)
    return (xf * scale).astype(jnp.bfloat16)


def project(normed, wq, wk, wv):
    query = jnp.dot(normed, wq, preferred_element_type=jnp.float32).astype(jnp.bfloat16)
    key_rows = jnp.dot(normed, wk, preferred_element_type=jnp.float32).astype(jnp.bfloat16)
    value_rows = jnp.dot(normed, wv, preferred_element_type=jnp.float32).astype(jnp.bfloat16)
    return (query, key_rows, value_rows)


def attend(query, key_rows, value_rows, keep):
    ntr = keep.shape[0]
    width = keep.shape[1]
    kvh = key_rows.shape[1] // HEAD_DIM
    qh = query.shape[1] // HEAD_DIM
    q5 = query.reshape(ntr, width, kvh, qh // kvh, HEAD_DIM).astype(jnp.float32)
    k4 = key_rows.reshape(ntr, width, kvh, HEAD_DIM).astype(jnp.float32)
    v4 = value_rows.reshape(ntr, width, kvh, HEAD_DIM).astype(jnp.float32)
    scores = jnp.einsum("tqgrd,tkgd->tgrqk", q5, k4) / jnp.sqrt(jnp.float32(HEAD_DIM))
    expo = jnp.exp(scores) * keep[:, None, None]
    weights = (expo / jnp.sum(expo, axis=-1, keepdims=True)).astype(jnp.bfloat16)
    attended = jnp.einsum("tgrqk,tkgd->tqgrd", weights.astype(jnp.float32), v4)
    return attended.astype(jnp.bfloat16).reshape(ntr * width, qh * HEAD_DIM)


def local_layer(full, wq, wk, wv, wo, keep):
    normed = norm_rows(full)
    query, key_rows, value_rows = project(normed, wq, wk, wv)
    attended = attend(query, key_rows, value_rows, keep)
    return jnp.dot(attended, wo, preferred_element_type=jnp.float32)


def pick_rows(ids, table):
    count = table.shape[0]
    match = ids[..., None] == jnp.arange(count, dtype=jnp.int32)
    if table.ndim == 1:
        return jnp.sum(jnp.where(match, table, 0), axis=-1)
    return jnp.sum(jnp.where(match[..., None], table[None], 0), axis=-2)


def on_device(embeds, source, lengths, bounds, targets, w_query, w_key, w_value, w_out, w_class):
    ndp = lax.axis_size("dp")
    nst = lax.axis_size("section")
    mine_rep = lax.axis_index("dp")
    section_at = lax.axis_index("section")
    ntr = embeds.shape[0]
    width = embeds.shape[1]
    dsh = embeds.shape[2]
    total = source.shape[0]
    flat = embeds.reshape(ntr, width * dsh)
    owner = source - mine_rep * ntr
    select = (owner[:, None] == jnp.arange(ntr, dtype=jnp.int32)[None, :]).astype(jnp.bfloat16)
    outgoing = jnp.dot(select, flat, preferred_element_type=jnp.float32).astype(jnp.bfloat16)
    arrived = lax.all_to_all(
        outgoing.reshape(total, width, dsh), "dp", split_axis=0, concat_axis=0, tiled=True
    )
    taken = jnp.sum(arrived.reshape(ndp, ntr, width, dsh).astype(jnp.float32), axis=0).astype(
        jnp.bfloat16
    )
    wanted_ids = lax.dynamic_slice_in_dim(source, mine_rep * ntr, ntr)
    lens = pick_rows(wanted_ids, lengths)
    bnd = pick_rows(wanted_ids, bounds)
    tgt = pick_rows(wanted_ids, targets).reshape(-1)
    keep = visible(lens, width)
    rows_rep = ntr * width
    wq = w_query[0]
    wk = w_key[0]
    wv = w_value[0]
    wo = w_out[0]
    current = taken.reshape(rows_rep, dsh)
    full_width = dsh * lax.axis_size("tensor")
    saved = jnp.zeros((rows_rep, full_width), jnp.bfloat16)

    def forward_part(full):
        return local_layer(full, wq, wk, wv, wo, keep)

    def forward_none(full):
        return jnp.zeros((rows_rep, full.shape[1]), jnp.float32)

    for turn in range(nst):
        full = lax.all_gather(current, "tensor", axis=1, tiled=True)
        term = lax.cond(section_at == turn, forward_part, forward_none, full)
        share = lax.psum_scatter(
            term.astype(jnp.bfloat16), "tensor", scatter_dimension=1, tiled=True
        ).astype(jnp.float32)
        saved = jnp.where(section_at == turn, full, saved)
        current = (current.astype(jnp.float32) + share).astype(jnp.bfloat16)
        if turn + 1 < nst:
            current = passed_along(current, "section", 1)
    index = (jnp.arange(ntr, dtype=jnp.int32)[:, None] * width + bnd).reshape(-1)
    rows = current[index]
    part_z = jnp.dot(rows, w_class, preferred_element_type=jnp.float32)
    rows_f = rows.astype(jnp.float32)
    part_sq = jnp.sum(rows_f * rows_f, axis=1)
    zeta, sumsq = lax.psum((part_z, part_sq), "tensor")
    rstd = lax.rsqrt(sumsq / full_width + EPS)
    logits = zeta * rstd[:, None]
    expo = jnp.exp(logits)
    prob = expo / jnp.sum(expo, axis=1, keepdims=True)
    onehot = (tgt[:, None] == jnp.arange(logits.shape[1], dtype=jnp.int32)[None, :]).astype(
        jnp.float32
    )
    tokens_total = jnp.sum(lens).astype(jnp.float32)
    dlog = LOSS_SCALE / tokens_total * (prob - onehot)
    dzeta = dlog * rstd[:, None]
    drstd = jnp.sum(dlog * zeta, axis=1)
    dmean = drstd * -0.5 * rstd * rstd * rstd
    drows = jnp.dot(dzeta, w_class.astype(jnp.float32).T, precision=lax.Precision.HIGHEST)
    drows = drows + dmean[:, None] * 2.0 * rows_f / full_width
    grad = jnp.zeros((rows_rep, dsh), jnp.float32).at[index].set(drows).astype(jnp.bfloat16)

    def backward_part(gfull):
        _, pull = jax.vjp(
            lambda xx, a, b, c, d: local_layer(xx, a, b, c, d, keep), saved, wq, wk, wv, wo
        )
        return pull(gfull.astype(jnp.float32))

    def backward_none(gfull):
        return (
            jnp.zeros(saved.shape, saved.dtype),
            jnp.zeros(wq.shape, wq.dtype),
            jnp.zeros(wk.shape, wk.dtype),
            jnp.zeros(wv.shape, wv.dtype),
            jnp.zeros(wo.shape, wo.dtype),
        )

    acc_q = jnp.zeros(wq.shape, jnp.float32)
    acc_k = jnp.zeros(wk.shape, jnp.float32)
    acc_v = jnp.zeros(wv.shape, jnp.float32)
    acc_o = jnp.zeros(wo.shape, jnp.float32)
    for turn in reversed(range(nst)):
        gfull = lax.all_gather(grad, "tensor", axis=1, tiled=True)
        dx, dq, dk, dv, do = lax.cond(section_at == turn, backward_part, backward_none, gfull)
        acc_q = acc_q + dq.astype(jnp.float32)
        acc_k = acc_k + dk.astype(jnp.float32)
        acc_v = acc_v + dv.astype(jnp.float32)
        acc_o = acc_o + do.astype(jnp.float32)
        dshare = lax.psum_scatter(
            dx.astype(jnp.float32).astype(jnp.bfloat16), "tensor", scatter_dimension=1, tiled=True
        ).astype(jnp.float32)
        grad = (grad.astype(jnp.float32) + dshare).astype(jnp.bfloat16)
        if turn > 0:
            grad = passed_along(grad, "section", -1)
    sum_q, sum_k, sum_v, sum_o = (
        lax.psum_scatter(acc_q.astype(jnp.bfloat16), "dp", scatter_dimension=0, tiled=True).astype(
            jnp.float32
        ),
        lax.psum_scatter(acc_k.astype(jnp.bfloat16), "dp", scatter_dimension=0, tiled=True).astype(
            jnp.float32
        ),
        lax.psum_scatter(acc_v.astype(jnp.bfloat16), "dp", scatter_dimension=0, tiled=True).astype(
            jnp.float32
        ),
        lax.psum_scatter(acc_o.astype(jnp.bfloat16), "dp", scatter_dimension=1, tiled=True).astype(
            jnp.float32
        ),
    )
    return (sum_q[None], sum_k[None], sum_v[None], sum_o[None])


def solution(mesh):
    placed = (
        P("dp", None, "tensor"),
        P(),
        P(),
        P(),
        P(),
        P("section", None, "tensor"),
        P("section", None, "tensor"),
        P("section", None, "tensor"),
        P("section", "tensor", None),
        P("tensor", None),
    )
    return jax.shard_map(
        on_device,
        mesh=mesh,
        in_specs=placed,
        out_specs=(
            P("section", "dp", "tensor"),
            P("section", "dp", "tensor"),
            P("section", "dp", "tensor"),
            P("section", "tensor", "dp"),
        ),
        check_vma=False,
    )
```

profile of v0, /device:TPU:1, one launch (start us, length us, event | category | flops | bytes accessed | tf_op | source)
XLA Modules:
  0.0 1124.4 jit_solution(3976962974276138444)
XLA Ops:
  10.0 20.7 %all_to_all.5 = bf16[8,128,512]{2,1,0:T(8,128)(2,1)S(1)} all-to-all(bf16[8,128,512]{2,1,0:T(8,128)(2,1)S(1)} %copy.203), channel_id=1, replica_groups=mesh['dp'=4,'section'=4,'tensor'=8] {'dp'}, dimensions={0} | all-to-all | bytes 2097152 | tf_op jit(solution)/shard_map/all_to_all | solution.py:82
  32.6 35.7 %all-gather.9.cloned.1.call-done = bf16[256,4096]{1,0:T(8,128)(2,1)} async-done(((bf16[256,512]{1,0:T(8,128)(2,1)}), bf16[256,4096]{1,0:T(8,128)(2,1)}) %all-gather.9.cloned.1.call-update) | async-done | bytes 2097168 | tf_op jit(solution)/shard_map/all_gather | solution.py:109
  68.3 11.3 %conditional.8 = (bf16[256,4096]{1,0:T(8,128)(2,1)}) conditional(s32[]{:T(128)} %convert_element_type.704, () %tuple.97, (bf16[256,4096]{1,0:T(8,128)(2,1)}, bf16[4096,128]{1,0:T(8,128)(2,1)S(1)}, bf16[4096,128]{1,0:T(8,128)(2,1)S(1)}, bf16[4096,512]{1,0:T(8,128)(2,1)}, f32[2,128,128]{1,2,0:T(8,128)S(1)}, ...), branch_computations={%region_2.3_spmd, %region_3.0_spmd} | conditional | flops 2765028608 | bytes 49690688 | solution.py:110
  74.9 4.8 fusion.6
  79.7 39.6 %reduce-scatter.12.cloned.1.call-done = bf16[256,512]{1,0:T(8,128)(2,1)} async-done(((bf16[256,4096]{1,0:T(8,128)(2,1)}), bf16[256,512]{1,0:T(8,128)(2,1)}) %reduce-scatter.12.cloned.1.call-update) | async-done | bytes 262160 | tf_op jit(solution)/shard_map/reduce_scatter | solution.py:111
  120.3 3.2 collective-permute-start
  123.5 3.3 collective-permute-done
  127.6 42.0 %all-gather.11.cloned.1.call-done = bf16[256,4096]{1,0:T(8,128)(2,1)} async-done(((bf16[256,512]{1,0:T(8,128)(2,1)}), bf16[256,4096]{1,0:T(8,128)(2,1)}) %all-gather.11.cloned.1.call-update) | async-done | bytes 2097168 | tf_op jit(solution)/shard_map/all_gather | solution.py:109
  171.2 50.5 %reduce-scatter.14.cloned.1.call-done = bf16[256,512]{1,0:T(8,128)(2,1)} async-done(((bf16[256,4096]{1,0:T(8,128)(2,1)}), bf16[256,512]{1,0:T(8,128)(2,1)}) %reduce-scatter.14.cloned.1.call-update) | async-done | bytes 262160 | tf_op jit(solution)/shard_map/reduce_scatter | solution.py:111
  222.7 3.1 collective-permute-start.1
  225.8 3.3 collective-permute-done.1
  229.9 42.1 %all-gather.13.cloned.1.call-done = bf16[256,4096]{1,0:T(8,128)(2,1)} async-done(((bf16[256,512]{1,0:T(8,128)(2,1)}), bf16[256,4096]{1,0:T(8,128)(2,1)}) %all-gather.13.cloned.1.call-update) | async-done | bytes 2097168 | tf_op jit(solution)/shard_map/all_gather | solution.py:109
  273.7 52.0 %reduce-scatter.16.cloned.1.call-done = bf16[256,512]{1,0:T(8,128)(2,1)} async-done(((bf16[256,4096]{1,0:T(8,128)(2,1)}), bf16[256,512]{1,0:T(8,128)(2,1)}) %reduce-scatter.16.cloned.1.call-update) | async-done | bytes 262160 | tf_op jit(solution)/shard_map/reduce_scatter | solution.py:111
  326.8 3.1 collective-permute-start.2
  329.9 3.3 collective-permute-done.2
  333.9 42.1 %all-gather.15.cloned.1.call-done = bf16[256,4096]{1,0:T(8,128)(2,1)} async-done(((bf16[256,512]{1,0:T(8,128)(2,1)}), bf16[256,4096]{1,0:T(8,128)(2,1)}) %all-gather.15.cloned.1.call-update) | async-done | bytes 2097168 | tf_op jit(solution)/shard_map/all_gather | solution.py:109
  378.9 51.4 %reduce-scatter.18.cloned.1.call-done = bf16[256,512]{1,0:T(8,128)(2,1)} async-done(((bf16[256,4096]{1,0:T(8,128)(2,1)}), bf16[256,512]{1,0:T(8,128)(2,1)}) %reduce-scatter.18.cloned.1.call-update) | async-done | bytes 262160 | tf_op jit(solution)/shard_map/reduce_scatter | solution.py:111
  432.2 14.6 %all-reduce = (f32[8,128]{1,0:T(8,128)S(1)}, f32[8]{0:T(128)S(1)}) all-reduce(f32[8,128]{1,0:T(8,128)S(1)} %fusion.230, f32[8]{0:T(128)S(1)} %fusion.215), channel_id=1, replica_groups=mesh['dp'=4,'section'=4,'tensor'=8] {'tensor'}, use_global_device_ids=true, to_apply=%region_24.25 | all-reduce | flops 1032 | bytes 8256 | tf_op jit(solution)/shard_map/psum | solution.py:123
  451.1 40.9 %all-gather.17.cloned.1.call-done = bf16[256,4096]{1,0:T(8,128)(2,1)} async-done(((bf16[256,512]{1,0:T(8,128)(2,1)}), bf16[256,4096]{1,0:T(8,128)(2,1)}) %all-gather.17.cloned.1.call-update) | async-done | bytes 2097168 | tf_op jit(solution)/shard_map/all_gather | solution.py:160
  492.0 24.4 %conditional.12 = (bf16[256,4096]{1,0:T(8,128)(2,1)}, f32[4096,512]{1,0:T(8,128)}, f32[4096,128]{1,0:T(8,128)}, f32[4096,128]{1,0:T(8,128)}, f32[512,4096]{1,0:T(8,128)}) conditional(s32[]{:T(128)} %convert_element_type.700, () %tuple.96, (bf16[256,4096]{1,0:T(8,128)(2,1)}, bf16[512,4096]{1,0:T(8,128)(2,1)}, bf16[256,4096]{1,0:T(8,128)(2,1)S(1)}, ...), branch_computations={%region_31.32_spmd, %region_32.37_spmd} | conditional | flops 7233341952 | bytes 124583184 | solution.py:161
  496.6 4.2 broadcast.466
  500.8 4.3 broadcast.464
  516.5 72.0 %reduce-scatter.20.cloned.1.call-done = bf16[256,512]{1,0:T(8,128)(2,1)} async-done(((bf16[256,4096]{1,0:T(8,128)(2,1)}), bf16[256,512]{1,0:T(8,128)(2,1)}) %reduce-scatter.20.cloned.1.call-update) | async-done | bytes 262160 | tf_op jit(solution)/shard_map/reduce_scatter | solution.py:166
  591.0 5.9 collective-permute-done.3
  597.0 41.5 %all-gather.19.cloned.1.call-done = bf16[256,4096]{1,0:T(8,128)(2,1)} async-done(((bf16[256,512]{1,0:T(8,128)(2,1)}), bf16[256,4096]{1,0:T(8,128)(2,1)}) %all-gather.19.cloned.1.call-update) | async-done | bytes 2097168 | tf_op jit(solution)/shard_map/all_gather | solution.py:160
  638.4 13.5 %conditional.13 = (bf16[256,4096]{1,0:T(8,128)(2,1)}, f32[4096,512]{1,0:T(8,128)}, f32[4096,128]{1,0:T(8,128)}, f32[4096,128]{1,0:T(8,128)}, f32[512,4096]{1,0:T(8,128)}) conditional(s32[]{:T(128)} %convert_element_type.715, () %tuple.106, (bf16[256,4096]{1,0:T(8,128)(2,1)}, bf16[512,4096]{1,0:T(8,128)(2,1)}, bf16[256,4096]{1,0:T(8,128)(2,1)S(1)}, ...), branch_computations={%region_38.39_spmd, %region_39.44_spmd} | conditional | flops 7233341952 | bytes 124583184 | solution.py:161
  643.0 4.3 broadcast.476
  647.2 4.3 broadcast.474
  652.0 73.3 %reduce-scatter.22.cloned.1.call-done = bf16[256,512]{1,0:T(8,128)(2,1)} async-done(((bf16[256,4096]{1,0:T(8,128)(2,1)}), bf16[256,512]{1,0:T(8,128)(2,1)}) %reduce-scatter.22.cloned.1.call-update) | async-done | bytes 262160 | tf_op jit(solution)/shard_map/reduce_scatter | solution.py:166
  727.8 5.9 collective-permute-done.4
  733.7 41.3 %all-gather.21.cloned.1.call-done = bf16[256,4096]{1,0:T(8,128)(2,1)} async-done(((bf16[256,512]{1,0:T(8,128)(2,1)}), bf16[256,4096]{1,0:T(8,128)(2,1)}) %all-gather.21.cloned.1.call-update) | async-done | bytes 2097168 | tf_op jit(solution)/shard_map/all_gather | solution.py:160
  775.1 13.2 %conditional.14 = (bf16[256,4096]{1,0:T(8,128)(2,1)}, f32[4096,512]{1,0:T(8,128)}, f32[4096,128]{1,0:T(8,128)}, f32[4096,128]{1,0:T(8,128)}, f32[512,4096]{1,0:T(8,128)}) conditional(s32[]{:T(128)} %convert_element_type.710, () %tuple.108, (bf16[256,4096]{1,0:T(8,128)(2,1)}, bf16[512,4096]{1,0:T(8,128)(2,1)}, bf16[256,4096]{1,0:T(8,128)(2,1)S(1)}, ...), branch_computations={%region_45.46_spmd, %region_46.51_spmd} | conditional | flops 7233341952 | bytes 124583184 | solution.py:161
  779.6 4.3 broadcast.486
  783.8 4.3 broadcast.484
  788.4 71.7 %reduce-scatter.24.cloned.1.call-done = bf16[256,512]{1,0:T(8,128)(2,1)} async-done(((bf16[256,4096]{1,0:T(8,128)(2,1)}), bf16[256,512]{1,0:T(8,128)(2,1)}) %reduce-scatter.24.cloned.1.call-update) | async-done | bytes 262160 | tf_op jit(solution)/shard_map/reduce_scatter | solution.py:166
  862.5 5.9 collective-permute-done.5
  868.5 41.4 %all-gather.23.cloned.1.call-done = bf16[256,4096]{1,0:T(8,128)(2,1)} async-done(((bf16[256,512]{1,0:T(8,128)(2,1)}), bf16[256,4096]{1,0:T(8,128)(2,1)}) %all-gather.23.cloned.1.call-update) | async-done | bytes 2097168 | tf_op jit(solution)/shard_map/all_gather | solution.py:160
  909.8 25.3 %conditional.15 = (f32[4096,512]{1,0:T(8,128)}, f32[4096,128]{1,0:T(8,128)}, f32[4096,128]{1,0:T(8,128)}, f32[512,4096]{1,0:T(8,128)}) conditional(s32[]{:T(128)} %convert_element_type.704, () %tuple.110, (bf16[256,4096]{1,0:T(8,128)(2,1)S(1)}, bf16[256,4096]{1,0:T(8,128)(2,1)}, bf16[512,4096]{1,0:T(8,128)(2,1)}, bf16[4096,128]{1,0:T(8,128)(2,1)S(1)}, ...), branch_computations={%region_52.53_spmd, %region_53.57_spmd} | conditional | flops 5605950464 | bytes 90629240 | solution.py:161
  914.6 4.1 convolution_convert_fusion.66
  925.8 4.6 fusion.180
  930.4 4.5 fusion.179
  935.1 4.8 add_convert_fusion.2
  940.0 4.8 add_convert_fusion.3
  944.9 14.6 %add_convert_fusion = bf16[512,4096]{1,0:T(8,128)(2,1)} fusion(f32[512,4096]{1,0:T(8,128)} %get-tuple-element.225, f32[512,4096]{1,0:T(8,128)} %get-tuple-element.224, f32[512,4096]{1,0:T(8,128)} %get-tuple-element.222, f32[512,4096]{1,0:T(8,128)} %get-tuple-element.223), kind=kLoop, calls=%fused_computation.320 | loop fusion | flops 8388608 | bytes 37748736 | tf_op jit(solution)/shard_map/convert_element_type | solution.py:182
  959.6 14.6 %add_convert_fusion.1 = bf16[4096,512]{1,0:T(8,128)(2,1)} fusion(f32[4096,512]{1,0:T(8,128)} %get-tuple-element.213, f32[4096,512]{1,0:T(8,128)} %get-tuple-element.211, f32[4096,512]{1,0:T(8,128)} %get-tuple-element.207, f32[4096,512]{1,0:T(8,128)} %get-tuple-element.209), kind=kLoop, calls=%fused_computation.321 | loop fusion | flops 8388608 | bytes 37748736 | tf_op jit(solution)/shard_map/convert_element_type | solution.py:173
  976.0 31.7 %reduce-scatter.28.cloned.1.call-done = bf16[1024,128]{1,0:T(8,128)(2,1)} async-done(((bf16[4096,128]{1,0:T(8,128)(2,1)}), bf16[1024,128]{1,0:T(8,128)(2,1)}) %reduce-scatter.28.cloned.1.call-update) | async-done | bytes 262160 | tf_op jit(solution)/shard_map/reduce_scatter | solution.py:176
  1009.5 51.6 %reduce-scatter.32.cloned.1.call-done = bf16[512,1024]{1,0:T(8,128)(2,1)} async-done(((bf16[512,4096]{1,0:T(8,128)(2,1)}), bf16[512,1024]{1,0:T(8,128)(2,1)}) %reduce-scatter.32.cloned.1.call-update) | async-done | bytes 1048592 | tf_op jit(solution)/shard_map/reduce_scatter | solution.py:182
  1063.9 50.9 %reduce-scatter.26.cloned.1.call-done = bf16[1024,512]{1,0:T(8,128)(2,1)} async-done(((bf16[4096,512]{1,0:T(8,128)(2,1)}), bf16[1024,512]{1,0:T(8,128)(2,1)}) %reduce-scatter.26.cloned.1.call-update) | async-done | bytes 1048592 | tf_op jit(solution)/shard_map/reduce_scatter | solution.py:173
  (168 shorter events, 73.9 us)
Async XLA Ops:
  7.2 424.9 %copy-start = (bf16[512,128]{1,0:T(8,128)(2,1)S(1)}, bf16[512,128]{1,0:T(8,128)(2,1)}, u32[]{:S(2)}) copy-start(bf16[512,128]{1,0:T(8,128)(2,1)} %param.35) | copy-start | bytes 393220
  7.2 61.1 %all-gather.9.cloned.1.call-start = ((), (), s32[]{:S(2)}) async-start(), calls=%async_computation.12 | async-start | bytes 2359296 | tf_op jit(solution)/shard_map/all_gather | solution.py:109
  9.9 21.7 %copy-start.50 = (s32[8]{0:T(128)S(1)}, s32[8]{0:T(128)}, u32[]{:S(2)}) copy-start(s32[8]{0:T(128)} %param.27) | copy-start | bytes 100
  9.9 21.8 %copy-start.49 = (s32[8]{0:T(128)S(1)}, s32[8]{0:T(128)}, u32[]{:S(2)}) copy-start(s32[8]{0:T(128)} %param.28) | copy-start | bytes 100
  10.0 58.4 %copy-start.10 = (bf16[1,4096,128]{2,1,0:T(8,128)(2,1)S(1)}, bf16[1,4096,128]{2,1,0:T(8,128)(2,1)}, u32[]{:S(2)}) copy-start(bf16[1,4096,128]{2,1,0:T(8,128)(2,1)} %param.33) | copy-start | bytes 3145732
  10.0 58.4 %copy-start.11 = (bf16[1,4096,128]{2,1,0:T(8,128)(2,1)S(1)}, bf16[1,4096,128]{2,1,0:T(8,128)(2,1)}, u32[]{:S(2)}) copy-start(bf16[1,4096,128]{2,1,0:T(8,128)(2,1)} %param.32) | copy-start | bytes 3145732
  31.6 87.7 %reduce-scatter.12.cloned.1.call-start = ((), (), s32[]{:S(2)}) async-start(), calls=%async_computation.13 | async-start | bytes 2359296 | tf_op jit(solution)/shard_map/reduce_scatter | solution.py:111
  68.3 2.2 copy-start.20
  70.6 2.2 copy-start.2
  79.7 39.7 %copy-start.28 = (bf16[2,128,512]{2,1,0:T(8,128)(2,1)S(1)}, bf16[2,128,512]{2,1,0:T(8,128)(2,1)}, u32[]{:S(2)}) copy-start(bf16[2,128,512]{2,1,0:T(8,128)(2,1)} %reduce_sum.312) | copy-start | bytes 786436
  79.7 89.9 %all-gather.11.cloned.1.call-start = ((), (), s32[]{:S(2)}) async-start(), calls=%async_computation.14 | async-start | bytes 2359296 | tf_op jit(solution)/shard_map/all_gather | solution.py:109
  120.3 6.5 collective-permute-start
  126.8 0.7 copy-start.34
  127.5 94.1 %reduce-scatter.14.cloned.1.call-start = ((), (), s32[]{:S(2)}) async-start(), calls=%async_computation.15 | async-start | bytes 2359296 | tf_op jit(solution)/shard_map/reduce_scatter | solution.py:111
  171.1 50.5 %copy-start.35 = (bf16[256,512]{1,0:T(8,128)(2,1)S(1)}, bf16[256,512]{1,0:T(8,128)(2,1)}, u32[]{:S(2)}) copy-start(bf16[256,512]{1,0:T(8,128)(2,1)} %copy-done.34) | copy-start | bytes 786436
  171.1 100.8 %all-gather.13.cloned.1.call-start = ((), (), s32[]{:S(2)}) async-start(), calls=%async_computation.16 | async-start | bytes 2359296 | tf_op jit(solution)/shard_map/all_gather | solution.py:109
  222.7 6.4 collective-permute-start.1
  229.1 0.7 copy-start.36
  229.8 95.9 %reduce-scatter.16.cloned.1.call-start = ((), (), s32[]{:S(2)}) async-start(), calls=%async_computation.17 | async-start | bytes 2359296 | tf_op jit(solution)/shard_map/reduce_scatter | solution.py:111
  273.6 52.1 %copy-start.37 = (bf16[256,512]{1,0:T(8,128)(2,1)S(1)}, bf16[256,512]{1,0:T(8,128)(2,1)}, u32[]{:S(2)}) copy-start(bf16[256,512]{1,0:T(8,128)(2,1)} %copy-done.36) | copy-start | bytes 786436
  273.7 102.3 %all-gather.15.cloned.1.call-start = ((), (), s32[]{:S(2)}) async-start(), calls=%async_computation.18 | async-start | bytes 2359296 | tf_op jit(solution)/shard_map/all_gather | solution.py:109
  326.8 6.4 collective-permute-start.2
  333.2 0.7 copy-start.33
  333.9 96.4 %reduce-scatter.18.cloned.1.call-start = ((), (), s32[]{:S(2)}) async-start(), calls=%async_computation.19 | async-start | bytes 2359296 | tf_op jit(solution)/shard_map/reduce_scatter | solution.py:111
  376.3 1.3 copy-start.19
  376.3 2.1 copy-start.47
  376.3 2.1 copy-start.48
  377.6 114.4 %all-gather.17.cloned.1.call-start = ((), (), s32[]{:S(2)}) async-start(), calls=%async_computation.20 | async-start | bytes 2359296 | tf_op jit(solution)/shard_map/all_gather | solution.py:160
  448.2 0.9 copy-start.24
  449.1 139.4 %reduce-scatter.20.cloned.1.call-start = ((), (), s32[]{:S(2)}) async-start(), calls=%async_computation.21 | async-start | bytes 2359296 | tf_op jit(solution)/shard_map/reduce_scatter | solution.py:166
  516.5 122.0 %all-gather.19.cloned.1.call-start = ((), (), s32[]{:S(2)}) async-start(), calls=%async_computation.22 | async-start | bytes 2359296 | tf_op jit(solution)/shard_map/all_gather | solution.py:160
  589.7 7.2 collective-permute-start.3
  596.9 128.4 %reduce-scatter.22.cloned.1.call-start = ((), (), s32[]{:S(2)}) async-start(), calls=%async_computation.23 | async-start | bytes 2359296 | tf_op jit(solution)/shard_map/reduce_scatter | solution.py:166
  652.0 123.1 %all-gather.21.cloned.1.call-start = ((), (), s32[]{:S(2)}) async-start(), calls=%async_computation.24 | async-start | bytes 2359296 | tf_op jit(solution)/shard_map/all_gather | solution.py:160
  726.5 7.2 collective-permute-start.4
  733.7 126.4 %reduce-scatter.24.cloned.1.call-start = ((), (), s32[]{:S(2)}) async-start(), calls=%async_computation.25 | async-start | bytes 2359296 | tf_op jit(solution)/shard_map/reduce_scatter | solution.py:166
  788.3 121.5 %all-gather.23.cloned.1.call-start = ((), (), s32[]{:S(2)}) async-start(), calls=%async_computation.26 | async-start | bytes 2359296 | tf_op jit(solution)/shard_map/all_gather | solution.py:160
  861.2 7.2 collective-permute-start.5
  868.4 105.8 %reduce-scatter.30.cloned.1.call-start = ((), (), s32[]{:S(2)}) async-start(), calls=%async_computation.29 | async-start | bytes 1310720 | tf_op jit(solution)/shard_map/reduce_scatter | solution.py:179
  909.8 1.2 copy-start.18
  911.1 2.2 copy-start.9
  925.8 4.6 copy-start.32
  940.0 67.8 %reduce-scatter.28.cloned.1.call-start = ((), (), s32[]{:S(2)}) async-start(), calls=%async_computation.28 | async-start | bytes 1310720 | tf_op jit(solution)/shard_map/reduce_scatter | solution.py:176
  944.9 116.2 %reduce-scatter.32.cloned.1.call-start = ((), (), s32[]{:S(2)}) async-start(), calls=%async_computation.30 | async-start | bytes 5242880 | tf_op jit(solution)/shard_map/reduce_scatter | solution.py:182
  959.5 155.3 %reduce-scatter.26.cloned.1.call-start = ((), (), s32[]{:S(2)}) async-start(), calls=%async_computation.27 | async-start | bytes 5242880 | tf_op jit(solution)/shard_map/reduce_scatter | solution.py:173
  1061.1 56.5 %copy-start.1 = (bf16[512,128]{1,0:T(8,128)(2,1)S(1)}, bf16[512,128]{1,0:T(8,128)(2,1)}, u32[]{:S(2)}) copy-start(bf16[512,128]{1,0:T(8,128)(2,1)} %param.35) | copy-start | bytes 393220
Sparse Core Ops, SparseCore 0:
  31.7 36.5 all-gather.8
  79.8 39.4 reduce-scatter.11
  127.6 41.8 all-gather.10
  172.4 49.2 reduce-scatter.13
  229.9 41.9 all-gather.12
  274.7 50.9 reduce-scatter.15
  334.0 41.9 all-gather.14
  379.0 51.2 reduce-scatter.17
  449.2 42.8 all-gather.16
  516.6 71.8 reduce-scatter.19
  597.0 41.3 all-gather.18
  652.1 73.2 reduce-scatter.21
  733.8 41.1 all-gather.20
  788.4 71.5 reduce-scatter.23
  868.5 41.2 all-gather.22
  940.1 33.6 reduce-scatter.29
  976.5 31.1 reduce-scatter.27
  1010.2 50.8 reduce-scatter.31
  1063.9 50.8 reduce-scatter.25
where the time goes:
time: 1130 us; the launch traced here: 1120 us
  waiting for transfers between devices  899 us (80%)
  other arithmetic  64.4 us (6%)
  local copies, waits for them, and re-layouts  52.2 us (5%)
  blocking collectives  35.3 us (3%)
  matrix products  31.4 us (3%)
  between operations  15.3 us (1%)
  starting transfers between devices  14 us (1%)
  loops' own time  12.4 us (1%)
    reduce_scatter x3, waiting for transfers between devices, on_device(): lax.psum_scatter(dx.astype(jnp.float32).astype(jnp.bfloat16), 'tensor', s...  217 us
    reduce_scatter x4, waiting for transfers between devices, on_device(): lax.psum_scatter(term.astype(jnp.bfloat16), 'tensor', scatter_dimension=1...  193 us
    all_gather x4, waiting for transfers between devices, on_device(): gfull = lax.all_gather(grad, 'tensor', axis=1, tiled=True)  165 us
    all_gather x4, waiting for transfers between devices, on_device(): full = lax.all_gather(current, 'tensor', axis=1, tiled=True)  162 us
    reduce_scatter x1, waiting for transfers between devices, on_device(): lax.psum_scatter(acc_o.astype(jnp.bfloat16), 'dp', scatter_dimension=1, t...  51.6 us
    reduce_scatter x1, waiting for transfers between devices, on_device(): lax.psum_scatter(acc_q.astype(jnp.bfloat16), 'dp', scatter_dimension=0, t...  50.9 us
    another operation x20, local copies, waits for them, and re-layouts  42.7 us
    reduce_scatter x1, waiting for transfers between devices, on_device(): lax.psum_scatter(acc_k.astype(jnp.bfloat16), 'dp', scatter_dimension=0, t...  31.7 us
  transfers between devices with their start and end apart: 25, of which 24 were waited for; matrix products, arithmetic and copies ran while one was open for 4% of the time, Pallas kernels for 0%

commit v1 on v0

v1 whole, which is shorter than its diff:
```python
import jax
import jax.numpy as jnp
from jax import lax
from jax.sharding import PartitionSpec as P

HEAD_DIM = 128
EPS = 1e-06
LOSS_SCALE = 16384.0
F32 = jnp.float32
BF16 = jnp.bfloat16


def dot(a, b):
    return jnp.dot(a, b, preferred_element_type=F32)


def dot_nt(a, b):
    return lax.dot_general(a, b, (((1,), (1,)), ((), ())), preferred_element_type=F32)


def dot_tn(a, b):
    return lax.dot_general(a, b, (((0,), (0,)), ((), ())), preferred_element_type=F32)


def passed_along(x, axis, by):
    peers = lax.axis_size(axis)
    pairs = [(i, i + by) for i in range(peers) if 0 <= i + by < peers]
    return lax.ppermute(x, axis, pairs)


def swapped(x, axis, mask):
    return lax.ppermute(x, axis, [(i, i ^ mask) for i in range(lax.axis_size(axis))])


def exchange(blocks):
    return lax.all_to_all(blocks, "tensor", split_axis=0, concat_axis=0, tiled=True)


def gathered(cur):
    peers = lax.axis_size("tensor")
    got = exchange(jnp.broadcast_to(cur[None], (peers,) + cur.shape))
    return joined(got)


def joined(blocks):
    return blocks.transpose(1, 0, 2).reshape(blocks.shape[1], -1)


def cut(whole):
    peers = lax.axis_size("tensor")
    return whole.reshape(whole.shape[0], peers, -1).transpose(1, 0, 2)


def heads_down(x):
    rows = x.shape[0]
    return x.reshape(rows, -1, HEAD_DIM).transpose(1, 0, 2).reshape(-1, HEAD_DIM)


def heads_across(x, rows):
    return x.reshape(-1, rows, HEAD_DIM).transpose(1, 0, 2).reshape(rows, -1)


def visible(length, width):
    posq = jnp.arange(width, dtype=jnp.int32)[:, None]
    posk = jnp.arange(width, dtype=jnp.int32)[None, :]
    return ((posk <= posq) & (posk < length)).astype(F32)


def forward(full, wq, wk, wv, keep):
    xf = full.astype(F32)
    scale = lax.rsqrt(jnp.mean(xf * xf, axis=-1, keepdims=True) + EPS)
    h = (xf * scale).astype(BF16)
    rows = full.shape[0]
    q = heads_down(dot(h, wq).astype(BF16))
    k = dot(h, wk).astype(BF16)
    v = dot(h, wv).astype(BF16)
    scores = dot_nt(q, k) / jnp.sqrt(F32(HEAD_DIM))
    expo = (jnp.exp(scores).reshape(-1, rows, rows) * keep[None]).reshape(scores.shape)
    weights = (expo / jnp.sum(expo, axis=-1, keepdims=True)).astype(BF16)
    o = heads_across(dot(weights, v).astype(BF16), rows)
    return dict(x=full, scale=scale, h=h, q=q, k=k, v=v, w=weights, o=o)


def backward_heads(g, kept, wo):
    rows = g.shape[0]
    do = heads_down(dot_nt(g, wo).astype(BF16))
    wf = kept["w"].astype(F32)
    dw = dot_nt(do, kept["v"])
    ds = wf * (dw - jnp.sum(dw * wf, axis=-1, keepdims=True)) / jnp.sqrt(F32(HEAD_DIM))
    ds = ds.astype(BF16)
    dq = heads_across(dot(ds, kept["k"]).astype(BF16), rows)
    dk = dot_tn(ds, kept["q"]).astype(BF16)
    dv = dot_tn(kept["w"], do).astype(BF16)
    return dq, dk, dv


def backward_input(dq, dk, dv, kept, wq, wk, wv):
    dh = dot_nt(dq, wq) + dot_nt(dk, wk) + dot_nt(dv, wv)
    hf = kept["x"].astype(F32) * kept["scale"]
    return (kept["scale"] * (dh - hf * jnp.mean(dh * hf, axis=-1, keepdims=True))).astype(BF16)


def step_end_grad(rows, w_class, tgt, tokens_total):
    width = rows.shape[1]
    zeta = dot(rows, w_class)
    rf = rows.astype(F32)
    rstd = lax.rsqrt(jnp.sum(rf * rf, axis=1) / width + EPS)
    logits = zeta * rstd[:, None]
    expo = jnp.exp(logits)
    prob = expo / jnp.sum(expo, axis=1, keepdims=True)
    onehot = (tgt[:, None] == jnp.arange(logits.shape[1], dtype=jnp.int32)[None, :]).astype(F32)
    dlog = LOSS_SCALE / tokens_total * (prob - onehot)
    dzeta = dlog * rstd[:, None]
    dmean = jnp.sum(dlog * zeta, axis=1) * -0.5 * rstd * rstd * rstd
    drows = jnp.dot(dzeta, w_class.astype(F32).T, precision=lax.Precision.HIGHEST)
    drows = drows + dmean[:, None] * 2.0 * rf / width
    return drows.astype(BF16)


def among_replicas(x):
    return [x] + [swapped(x, "dp", k) for k in (1, 2, 3)]


def quarters_among_replicas(x, mine_rep):
    ndp = lax.axis_size("dp")
    size = x.shape[1] // ndp
    take = lambda who: lax.dynamic_slice_in_dim(x, who * size, size, axis=1)
    return [take(mine_rep)] + [swapped(take(mine_rep ^ k), "dp", k) for k in (1, 2, 3)]


def by_section(section_at, choices):
    out = choices[-1]
    for s in reversed(range(len(choices) - 1)):
        out = jnp.where(section_at == s, choices[s], out)
    return out


def on_device(embeds, source, lengths, bounds, targets, w_query, w_key, w_value, w_out, w_class):
    nst = lax.axis_size("section")
    peers = lax.axis_size("tensor")
    rep = lax.axis_index("dp")
    section_at = lax.axis_index("section")
    tensor_at = lax.axis_index("tensor")
    ntr, width, dsh = embeds.shape
    wq, wk, wv, wo = w_query[0], w_key[0], w_value[0], w_out[0]
    w_class = lax.all_gather(w_class, "tensor", axis=0, tiled=True)

    hi, core = rep // 2, rep % 2
    slots = source.reshape(2, 2, ntr) - rep * ntr

    def mine_for(col):
        owner = lax.dynamic_slice_in_dim(slots, col, 1, axis=1)[:, 0]
        out = jnp.zeros((2, ntr, width, dsh), BF16)
        for n in range(ntr):
            out = jnp.where((owner == n)[:, :, None, None], embeds[n][None, None], out)
        return out

    both = mine_for(core) + swapped(mine_for(1 - core), "dp", 1)
    own = lax.dynamic_slice_in_dim(both, hi, 1, axis=0)[0]
    away = lax.dynamic_slice_in_dim(both, 1 - hi, 1, axis=0)[0]
    first = [own[j] + swapped(away[j], "dp", 2) for j in range(ntr)]

    wanted = lax.dynamic_slice_in_dim(source, rep * ntr, ntr)
    lens = lengths[wanted]
    bnd = bounds[wanted]
    tgt = targets[wanted]
    tokens_total = jnp.sum(lens).astype(F32)
    keeps = [visible(lens[j], width) for j in range(ntr)]
    picks = [
        (bnd[j][:, None] == jnp.arange(width, dtype=jnp.int32)[None, :]).astype(BF16)
        for j in range(ntr)
    ]
    nstep = bnd.shape[1]

    def ends_to_all(part_rows):
        flat = part_rows.reshape(1, nstep * peers, dsh)
        return jnp.broadcast_to(flat, (peers, nstep * peers, dsh))

    def ends_sum(got):
        return jnp.sum(got.astype(F32), axis=0).reshape(nstep, peers * dsh)

    kept = []
    arriving = None
    for turn in range(nst):
        cur = first[turn] if turn < ntr else jnp.zeros((width, dsh), BF16)
        if arriving is not None:
            cur = jnp.where(section_at == 0, cur, arriving)
        keep = jnp.where(section_at == turn, keeps[0], keeps[1])
        now = forward(gathered(cur), wq, wk, wv, keep)
        kept.append(now)
        part = dot(now["o"], wo).astype(BF16)
        blocks = cut(part)
        if turn == nst - 1:
            ends = dot(picks[0], part).astype(BF16)
            blocks = jnp.concatenate([blocks, ends_to_all(ends)], axis=1)
        got = exchange(blocks)
        share = jnp.sum(got[:, :width].astype(F32), axis=0)
        arriving = passed_along((cur.astype(F32) + share).astype(BF16), "section", 1)

    def end_cotangent(which, parts, full):
        rows = dot(picks[which], full) + parts
        grad = step_end_grad(rows.astype(BF16), w_class, tgt[which], tokens_total)
        return dot_tn(picks[which], grad).astype(BF16)

    taken = {}
    g_top = end_cotangent(0, ends_sum(got[:, width:]), kept[-1]["x"])
    dq, dk, dv = backward_heads(g_top, kept[nst - 1], wo)
    dx = backward_input(dq, dk, dv, kept[nst - 1], wq, wk, wv)
    taken[nst] = (dq, dk, dv, g_top)
    own_cols = lambda whole: lax.dynamic_slice_in_dim(whole, tensor_at * dsh, dsh, axis=1)
    grad = own_cols(g_top)
    now = forward(gathered(arriving), wq, wk, wv, keeps[1])
    kept.append(now)
    ends = dot(dot(picks[1], now["o"]).astype(BF16), wo).astype(BF16)
    got = exchange(jnp.concatenate([cut(dx), ends_to_all(ends)], axis=1))
    g_top = end_cotangent(1, ends_sum(got[:, width:]), now["x"])

    for turn in range(nst + 1, 2 * nst + 1):
        share = jnp.sum(got[:, :width].astype(F32), axis=0)
        grad = passed_along((grad.astype(F32) + share).astype(BF16), "section", -1)
        g_full = gathered(grad)
        if turn == nst + 1:
            g_full = jnp.where(section_at == nst - 1, g_top, g_full)
            grad = jnp.where(section_at == nst - 1, own_cols(g_top), grad)
        late = 2 * nst + 1 - turn
        early = late - 2
        if early < 0:
            old = kept[late]
        else:
            old = {
                name: jnp.where(section_at == early, kept[early][name], kept[late][name])
                for name in kept[late]
            }
        dq, dk, dv = backward_heads(g_full, old, wo)
        taken[turn] = (dq, dk, dv, g_full)
        if turn < 2 * nst:
            dx = backward_input(dq, dk, dv, old, wq, wk, wv)
            got = exchange(cut(dx))

    h_rows, o_rows, g_rows, d_rows = [], [], [], []
    for which in range(ntr):
        h = by_section(section_at, [kept[s + which]["h"] for s in range(nst)])
        o = by_section(section_at, [kept[s + which]["o"] for s in range(nst)])
        back = [taken[2 * nst - 1 - s + which] for s in range(nst)]
        cots = by_section(section_at, [jnp.concatenate(b[:3], axis=1) for b in back])
        g = by_section(section_at, [b[3] for b in back])
        h_rows += quarters_among_replicas(h, rep)
        o_rows += among_replicas(o)
        d_rows += among_replicas(cots)
        g_rows += quarters_among_replicas(g, rep)
    h_rows, o_rows, g_rows, d_rows = (
        jnp.concatenate(part, axis=0) for part in (h_rows, o_rows, g_rows, d_rows)
    )
    qcol, kcol = wq.shape[1], wk.shape[1]
    grad_q = dot_tn(h_rows, d_rows[:, :qcol])
    grad_k = dot_tn(h_rows, d_rows[:, qcol : qcol + kcol])
    grad_v = dot_tn(h_rows, d_rows[:, qcol + kcol :])
    grad_o = dot_tn(o_rows, g_rows)
    return (grad_q[None], grad_k[None], grad_v[None], grad_o[None])


def solution(mesh):
    placed = (
        P("dp", None, "tensor"),
        P(),
        P(),
        P(),
        P(),
        P("section", None, "tensor"),
        P("section", None, "tensor"),
        P("section", None, "tensor"),
        P("section", "tensor", None),
        P("tensor", None),
    )
    return jax.shard_map(
        on_device,
        mesh=mesh,
        in_specs=placed,
        out_specs=(
            P("section", "dp", "tensor"),
            P("section", "dp", "tensor"),
            P("section", "dp", "tensor"),
            P("section", "tensor", "dp"),
        ),
        check_vma=False,
    )
```

time: 1130 us -> 677 us (0.60)
  waiting for transfers between devices: 899 us -> 188 us
  starting transfers between devices: 14 us -> 128 us
  matrix products: 31.4 us -> 121 us
  local copies, waits for them, and re-layouts: 52.2 us -> 102 us
  blocking collectives: 35.3 us -> 58.7 us
  other arithmetic: 64.4 us -> 50.7 us
  loops' own time: 12.4 us -> 0 us
    reduce_scatter x11 -> x0, waiting for transfers between devices: 545 us -> none  [the longest x3 217 us: on_device(): lax.psum_scatter(dx.astype(jnp.float32).astype(jnp.bfloat16), 'tensor', s...]
    all_gather x8 -> x1, waiting for transfers between devices: 327 us -> 0.01 us  [on_device(): w_class = lax.all_gather(w_class, 'tensor', axis=0, tiled=True)]
    all_to_all x0 -> x14, waiting for transfers between devices: none -> 117 us  [exchange(): lax.all_to_all(blocks, 'tensor', split_axis=0, concat_axis=0, tiled=True)]
    dot_general x23 -> x80, matrix products: 31.4 us -> 121 us  [the longest x35 51.8 us: dot(): return jnp.dot(a, b, preferred_element_type=F32)]
    all_to_all x0 -> x14, starting transfers between devices: none -> 72 us  [exchange(): lax.all_to_all(blocks, 'tensor', split_axis=0, concat_axis=0, tiled=True)]
    ppermute x0 -> x27, waiting for transfers between devices: none -> 54.1 us  [swapped(): lax.ppermute(x, axis, [(i, i ^ mask) for i in range(lax.axis_size(axis))])]
    another operation x20 -> x0, local copies, waits for them, and re-layouts: 42.7 us -> none
    all_to_all x1 -> x3, blocking collectives: 20.7 us -> 58.7 us  [exchange(): lax.all_to_all(blocks, 'tensor', split_axis=0, concat_axis=0, tiled=True)]
  transfers between devices with their start and end apart: 25 -> 50, of which waited for: 24 -> 27; matrix products, arithmetic and copies ran while one was open for 4% -> 19% of each run, Pallas kernels for 0% -> 0%
where the time goes in v1:
time: 677 us; the launch traced here: 666 us
  waiting for transfers between devices  188 us (28%)
  starting transfers between devices  128 us (19%)
  matrix products  121 us (18%)
  local copies, waits for them, and re-layouts  102 us (15%)
  blocking collectives  58.7 us (9%)
  other arithmetic  50.7 us (7%)
  between operations  17.7 us (3%)
    all_to_all x14, waiting for transfers between devices, exchange(): lax.all_to_all(blocks, 'tensor', split_axis=0, concat_axis=0, tiled=True)  117 us
    all_to_all x14, starting transfers between devices, exchange(): lax.all_to_all(blocks, 'tensor', split_axis=0, concat_axis=0, tiled=True)  72 us
    all_to_all x3, blocking collectives, exchange(): lax.all_to_all(blocks, 'tensor', split_axis=0, concat_axis=0, tiled=True)  58.7 us
    ppermute x27, waiting for transfers between devices, swapped(): lax.ppermute(x, axis, [(i, i ^ mask) for i in range(lax.axis_size(axis))])  54.1 us
    dot_general x35, matrix products, dot(): return jnp.dot(a, b, preferred_element_type=F32)  51.8 us
    dot_general x27, matrix products, dot_nt(): lax.dot_general(a, b, (((1,), (1,)), ((), ())), preferred_element_type=F32)  42.1 us
    ppermute x27, starting transfers between devices, swapped(): lax.ppermute(x, axis, [(i, i ^ mask) for i in range(lax.axis_size(axis))])  36.4 us
    unnamed x288, local copies, waits for them, and re-layouts  28.1 us
  transfers between devices with their start and end apart: 50, of which 27 were waited for; matrix products, arithmetic and copies ran while one was open for 19% of the time, Pallas kernels for 0%

profile of v1, /device:TPU:1, one launch (start us, length us, event | category | flops | bytes accessed | tf_op | source)
XLA Modules:
  0.0 665.8 jit_solution(15085470870656958993)
XLA Ops:
  20.4 5.2 all-to-all-start
  29.8 9.8 %all-to-all-done = bf16[8,128,512]{2,1,0:T(8,128)(2,1)S(1)} async-done(((bf16[8,128,512]{2,1,0:T(8,128)(2,1)}), bf16[8,128,512]{2,1,0:T(8,128)(2,1)S(1)}, u32[]{:S(2)}, u32[]{:S(2)}) %all-to-all-start) | async-done | bytes 1048608 | tf_op jit(solution)/shard_map/all_to_all | solution.py:36
  50.9 4.6 all-to-all-start.1
  58.0 12.4 %all-to-all-done.1 = bf16[8,128,512]{2,1,0:T(8,128)(2,1)S(1)} async-done(((bf16[8,128,512]{2,1,0:T(8,128)(2,1)}), bf16[8,128,512]{2,1,0:T(8,128)(2,1)S(1)}, u32[]{:S(2)}, u32[]{:S(2)}) %all-to-all-start.1) | async-done | bytes 1048608 | tf_op jit(solution)/shard_map/all_to_all | solution.py:36
  78.1 4.3 all-to-all-start.2
  82.5 12.5 %all-to-all-done.2 = bf16[8,128,512]{2,1,0:T(8,128)(2,1)} async-done(((bf16[8,128,512]{2,1,0:T(8,128)(2,1)}), bf16[8,128,512]{2,1,0:T(8,128)(2,1)}, u32[]{:S(2)}, u32[]{:S(2)}) %all-to-all-start.2) | async-done | bytes 1048608 | tf_op jit(solution)/shard_map/all_to_all | solution.py:36
  106.1 20.1 %all_to_all.85 = bf16[8,128,512]{2,1,0:T(8,128)(2,1)S(1)} all-to-all(bf16[8,128,512]{2,1,0:T(8,128)(2,1)S(1)} %bitcast.580), channel_id=1, replica_groups=mesh['dp'=4,'section'=4,'tensor'=8] {'tensor'}, dimensions={0} | all-to-all | bytes 2097152 | tf_op jit(solution)/shard_map/all_to_all | solution.py:36
  126.4 3.8 collective-permute-start.4
  133.2 4.5 all-to-all-start.4
  137.8 10.5 %all-to-all-done.4 = bf16[8,128,512]{2,1,0:T(8,128)(2,1)} async-done(((bf16[8,128,512]{2,1,0:T(8,128)(2,1)}), bf16[8,128,512]{2,1,0:T(8,128)(2,1)}, u32[]{:S(2)}, u32[]{:S(2)}) %all-to-all-start.4) | async-done | bytes 1048608 | tf_op jit(solution)/shard_map/all_to_all | solution.py:36
  159.5 20.7 %all_to_all.86 = bf16[8,128,512]{2,1,0:T(8,128)(2,1)S(1)} all-to-all(bf16[8,128,512]{2,1,0:T(8,128)(2,1)S(1)} %bitcast.581), channel_id=1, replica_groups=mesh['dp'=4,'section'=4,'tensor'=8] {'tensor'}, dimensions={0} | all-to-all | bytes 2097152 | tf_op jit(solution)/shard_map/all_to_all | solution.py:36
  180.4 3.8 collective-permute-start.5
  187.8 4.3 all-to-all-start.6
  194.2 7.8 %all-to-all-done.6 = bf16[8,128,512]{2,1,0:T(8,128)(2,1)} async-done(((bf16[8,128,512]{2,1,0:T(8,128)(2,1)}), bf16[8,128,512]{2,1,0:T(8,128)(2,1)}, u32[]{:S(2)}, u32[]{:S(2)}) %all-to-all-start.6) | async-done | bytes 1048608 | tf_op jit(solution)/shard_map/all_to_all | solution.py:36
  218.6 8.6 %all-to-all-start.7 = ((bf16[8,160,512]{2,1,0:T(8,128)(2,1)}), bf16[8,160,512]{2,1,0:T(8,128)(2,1)}, u32[]{:S(2)}, u32[]{:S(2)}) async-start(bf16[8,160,512]{2,1,0:T(8,128)(2,1)} %pad_maximum_fusion), calls=%async_computation.7 | async-start | bytes 2621440 | tf_op jit(solution)/shard_map/all_to_all | solution.py:36
  231.9 15.1 %all-to-all-done.7 = bf16[8,160,512]{2,1,0:T(8,128)(2,1)} async-done(((bf16[8,160,512]{2,1,0:T(8,128)(2,1)}), bf16[8,160,512]{2,1,0:T(8,128)(2,1)}, u32[]{:S(2)}, u32[]{:S(2)}) %all-to-all-start.7) | async-done | bytes 1310752 | tf_op jit(solution)/shard_map/all_to_all | solution.py:36
  259.5 4.2 fusion.100
  267.6 3.8 fusion.27
  279.3 4.3 all-to-all-start.8
  286.8 9.4 %all-to-all-done.8 = bf16[8,128,512]{2,1,0:T(8,128)(2,1)} async-done(((bf16[8,128,512]{2,1,0:T(8,128)(2,1)}), bf16[8,128,512]{2,1,0:T(8,128)(2,1)}, u32[]{:S(2)}, u32[]{:S(2)}) %all-to-all-start.8) | async-done | bytes 1048608 | tf_op jit(solution)/shard_map/all_to_all | solution.py:36
  322.8 6.0 all-to-all-start.9
  333.5 13.1 %all-to-all-done.9 = bf16[8,160,512]{2,1,0:T(8,128)(2,1)} async-done(((bf16[8,160,512]{2,1,0:T(8,128)(2,1)}), bf16[8,160,512]{2,1,0:T(8,128)(2,1)}, u32[]{:S(2)}, u32[]{:S(2)}) %all-to-all-start.9) | async-done | bytes 1310752 | tf_op jit(solution)/shard_map/all_to_all | solution.py:36
  358.5 4.4 all-to-all-start.10
  369.8 8.1 %all-to-all-done.10 = bf16[8,128,512]{2,1,0:T(8,128)(2,1)} async-done(((bf16[8,128,512]{2,1,0:T(8,128)(2,1)}), bf16[8,128,512]{2,1,0:T(8,128)(2,1)}, u32[]{:S(2)}, u32[]{:S(2)}) %all-to-all-start.10) | async-done | bytes 1048608 | tf_op jit(solution)/shard_map/all_to_all | solution.py:36
  393.5 17.9 %all_to_all.87 = bf16[8,128,512]{2,1,0:T(8,128)(2,1)S(1)} all-to-all(bf16[8,128,512]{2,1,0:T(8,128)(2,1)S(1)} %bitcast.583), channel_id=1, replica_groups=mesh['dp'=4,'section'=4,'tensor'=8] {'tensor'}, dimensions={0} | all-to-all | bytes 2097152 | tf_op jit(solution)/shard_map/all_to_all | solution.py:36
  413.8 5.3 collective-permute-done.14
  420.9 4.3 all-to-all-start.12
  427.5 8.2 %all-to-all-done.12 = bf16[8,128,512]{2,1,0:T(8,128)(2,1)} async-done(((bf16[8,128,512]{2,1,0:T(8,128)(2,1)}), bf16[8,128,512]{2,1,0:T(8,128)(2,1)}, u32[]{:S(2)}, u32[]{:S(2)}) %all-to-all-start.12) | async-done | bytes 1048608 | tf_op jit(solution)/shard_map/all_to_all | solution.py:36
  437.1 4.2 fusion.94
  445.2 3.7 fusion.21
  452.8 7.3 %all-to-all-start.13 = ((bf16[8,128,512]{2,1,0:T(8,128)(2,1)}), bf16[8,128,512]{2,1,0:T(8,128)(2,1)}, u32[]{:S(2)}, u32[]{:S(2)}) async-start(bf16[8,128,512]{2,1,0:T(8,128)(2,1)} %bitcast.576), calls=%async_computation.13 | async-start | bytes 2097152 | tf_op jit(solution)/shard_map/all_to_all | solution.py:36
  487.9 5.3 all-to-all-start.14
  493.2 5.0 fusion.106
  498.2 9.9 %all-to-all-done.14 = bf16[8,128,512]{2,1,0:T(8,128)(2,1)} async-done(((bf16[8,128,512]{2,1,0:T(8,128)(2,1)}), bf16[8,128,512]{2,1,0:T(8,128)(2,1)}, u32[]{:S(2)}, u32[]{:S(2)}) %all-to-all-start.14) | async-done | bytes 1048608 | tf_op jit(solution)/shard_map/all_to_all | solution.py:36
  509.5 4.2 fusion.91
  515.3 3.7 fusion.19
  523.3 4.3 all-to-all-start.15
  541.4 4.9 collective-permute-done.7
  547.0 8.0 %collective-permute-done.8 = bf16[128,1024]{1,0:T(8,128)(2,1)S(1)} collective-permute-done((bf16[128,1024]{1,0:T(8,128)(2,1)}, bf16[128,1024]{1,0:T(8,128)(2,1)S(1)}, u32[]{:S(2)}, u32[]{:S(2)}) %collective-permute-start.8) | collective-permute-done | bytes 262176 | tf_op jit(solution)/shard_map/ppermute | solution.py:32
  565.8 4.8 all-to-all-start.16
  579.9 12.1 %collective-permute-done.12 = bf16[128,1024]{1,0:T(8,128)(2,1)S(1)} collective-permute-done((bf16[128,1024]{1,0:T(8,128)(2,1)S(1)}, bf16[128,1024]{1,0:T(8,128)(2,1)S(1)}, u32[]{:S(2)}, u32[]{:S(2)}) %collective-permute-start.12) | collective-permute-done | bytes 262176 | tf_op jit(solution)/shard_map/ppermute | solution.py:32
  594.5 5.1 collective-permute-done.18
  601.4 3.8 fusion.88
  622.0 4.4 collective-permute-done.22
  627.2 3.9 convolution_bitcast_fusion.1
  631.1 5.6 collective-permute-done.31
  648.4 6.2 collective-permute-done.34
  654.6 3.8 convolution_bitcast_fusion
  (596 shorter events, 301.0 us)
Async XLA Ops:
  13.1 6.2 collective-permute-start.1
  20.4 19.3 %all-to-all-start = ((bf16[8,128,512]{2,1,0:T(8,128)(2,1)}), bf16[8,128,512]{2,1,0:T(8,128)(2,1)S(1)}, u32[]{:S(2)}, u32[]{:S(2)}) async-start(bf16[8,128,512]{2,1,0:T(8,128)(2,1)} %broadcast_in_dim.90), calls=%async_computation | async-start | bytes 2097152 | tf_op jit(solution)/shard_map/all_to_all | solution.py:36
  50.9 19.5 %all-to-all-start.1 = ((bf16[8,128,512]{2,1,0:T(8,128)(2,1)}), bf16[8,128,512]{2,1,0:T(8,128)(2,1)S(1)}, u32[]{:S(2)}, u32[]{:S(2)}) async-start(bf16[8,128,512]{2,1,0:T(8,128)(2,1)} %bitcast.578), calls=%async_computation.1 | async-start | bytes 2097152 | tf_op jit(solution)/shard_map/all_to_all | solution.py:36
  55.5 18.7 %collective-permute-start.2 = (bf16[128,512]{1,0:T(8,128)(2,1)S(1)}, bf16[128,512]{1,0:T(8,128)(2,1)S(1)}, u32[]{:S(2)}, u32[]{:S(2)}) collective-permute-start(bf16[128,512]{1,0:T(8,128)(2,1)S(1)} %copy-done.102), channel_id=1, source_target_pairs={{0,64},{32,96},{64,0},{96,32},{1,65},{33,97},{65,1},{97,33},{2,66}... | collective-permute-start | bytes 393224 | tf_op jit(solution)/shard_map/ppermute | solution.py:32
  70.6 5.5 collective-permute-start.3
  78.1 16.9 %all-to-all-start.2 = ((bf16[8,128,512]{2,1,0:T(8,128)(2,1)}), bf16[8,128,512]{2,1,0:T(8,128)(2,1)}, u32[]{:S(2)}, u32[]{:S(2)}) async-start(bf16[8,128,512]{2,1,0:T(8,128)(2,1)} %broadcast_in_dim.92), calls=%async_computation.2 | async-start | bytes 2097152 | tf_op jit(solution)/shard_map/all_to_all | solution.py:36
  126.4 5.7 collective-permute-start.4
  133.2 15.0 %all-to-all-start.4 = ((bf16[8,128,512]{2,1,0:T(8,128)(2,1)}), bf16[8,128,512]{2,1,0:T(8,128)(2,1)}, u32[]{:S(2)}, u32[]{:S(2)}) async-start(bf16[8,128,512]{2,1,0:T(8,128)(2,1)} %broadcast_in_dim.93), calls=%async_computation.4 | async-start | bytes 2097152 | tf_op jit(solution)/shard_map/all_to_all | solution.py:36
  180.4 5.7 collective-permute-start.5
  187.8 14.2 %all-to-all-start.6 = ((bf16[8,128,512]{2,1,0:T(8,128)(2,1)}), bf16[8,128,512]{2,1,0:T(8,128)(2,1)}, u32[]{:S(2)}, u32[]{:S(2)}) async-start(bf16[8,128,512]{2,1,0:T(8,128)(2,1)} %broadcast_in_dim.94), calls=%async_computation.6 | async-start | bytes 2097152 | tf_op jit(solution)/shard_map/all_to_all | solution.py:36
  192.1 60.9 %all-gather.2.cloned.1.call-start = ((), (), s32[]{:S(2)}) async-start(), calls=%async_computation.17 | async-start | bytes 1179648 | tf_op jit(solution)/shard_map/all_gather | solution.py:146
  218.6 28.4 %all-to-all-start.7 = ((bf16[8,160,512]{2,1,0:T(8,128)(2,1)}), bf16[8,160,512]{2,1,0:T(8,128)(2,1)}, u32[]{:S(2)}, u32[]{:S(2)}) async-start(bf16[8,160,512]{2,1,0:T(8,128)(2,1)} %pad_maximum_fusion), calls=%async_computation.7 | async-start | bytes 2621440 | tf_op jit(solution)/shard_map/all_to_all | solution.py:36
  279.3 16.9 %all-to-all-start.8 = ((bf16[8,128,512]{2,1,0:T(8,128)(2,1)}), bf16[8,128,512]{2,1,0:T(8,128)(2,1)}, u32[]{:S(2)}, u32[]{:S(2)}) async-start(bf16[8,128,512]{2,1,0:T(8,128)(2,1)} %broadcast_in_dim.97), calls=%async_computation.8 | async-start | bytes 2097152 | tf_op jit(solution)/shard_map/all_to_all | solution.py:36
  322.8 23.8 %all-to-all-start.9 = ((bf16[8,160,512]{2,1,0:T(8,128)(2,1)}), bf16[8,160,512]{2,1,0:T(8,128)(2,1)}, u32[]{:S(2)}, u32[]{:S(2)}) async-start(bf16[8,160,512]{2,1,0:T(8,128)(2,1)} %pad_maximum_fusion.1), calls=%async_computation.9 | async-start | bytes 2621440 | tf_op jit(solution)/shard_map/all_to_all | solution.py:36
  349.6 7.8 %collective-permute-start.13 = (bf16[128,512]{1,0:T(8,128)(2,1)}, bf16[128,512]{1,0:T(8,128)(2,1)S(1)}, u32[]{:S(2)}, u32[]{:S(2)}) collective-permute-start(bf16[128,512]{1,0:T(8,128)(2,1)} %add_convert_fusion.3), channel_id=1, source_target_pairs={{8,0},{16,8},{24,16},{9,1},{17,9},{25,17},{10,2},{18,10},{26,18},{... | collective-permute-start | bytes 393224 | tf_op jit(solution)/shard_map/ppermute | solution.py:28
  358.5 19.4 %all-to-all-start.10 = ((bf16[8,128,512]{2,1,0:T(8,128)(2,1)}), bf16[8,128,512]{2,1,0:T(8,128)(2,1)}, u32[]{:S(2)}, u32[]{:S(2)}) async-start(bf16[8,128,512]{2,1,0:T(8,128)(2,1)} %broadcast_in_dim.100), calls=%async_computation.10 | async-start | bytes 2097152 | tf_op jit(solution)/shard_map/all_to_all | solution.py:36
  412.5 6.6 collective-permute-start.14
  420.9 14.8 %all-to-all-start.12 = ((bf16[8,128,512]{2,1,0:T(8,128)(2,1)}), bf16[8,128,512]{2,1,0:T(8,128)(2,1)}, u32[]{:S(2)}, u32[]{:S(2)}) async-start(bf16[8,128,512]{2,1,0:T(8,128)(2,1)} %broadcast_in_dim.101), calls=%async_computation.12 | async-start | bytes 2097152 | tf_op jit(solution)/shard_map/all_to_all | solution.py:36
  452.8 23.6 %all-to-all-start.13 = ((bf16[8,128,512]{2,1,0:T(8,128)(2,1)}), bf16[8,128,512]{2,1,0:T(8,128)(2,1)}, u32[]{:S(2)}, u32[]{:S(2)}) async-start(bf16[8,128,512]{2,1,0:T(8,128)(2,1)} %bitcast.576), calls=%async_computation.13 | async-start | bytes 2097152 | tf_op jit(solution)/shard_map/all_to_all | solution.py:36
  470.9 9.1 %collective-permute-start.23 = (bf16[128,512]{1,0:T(8,128)(2,1)}, bf16[128,512]{1,0:T(8,128)(2,1)}, u32[]{:S(2)}, u32[]{:S(2)}) collective-permute-start(bf16[128,512]{1,0:T(8,128)(2,1)} %get-tuple-element.7), channel_id=1, source_target_pairs={{0,32},{32,0},{64,96},{96,64},{1,33},{33,1},{65,97},{97,65},{2,34}... | collective-permute-start | bytes 393224 | tf_op jit(solution)/shard_map/ppermute | solution.py:32
  473.0 8.6 %collective-permute-start.24 = (bf16[128,512]{1,0:T(8,128)(2,1)}, bf16[128,512]{1,0:T(8,128)(2,1)}, u32[]{:S(2)}, u32[]{:S(2)}) collective-permute-start(bf16[128,512]{1,0:T(8,128)(2,1)} %get-tuple-element.7), channel_id=1, source_target_pairs={{0,64},{32,96},{64,0},{96,32},{1,65},{33,97},{65,1},{97,33},{2,66}... | collective-permute-start | bytes 393224 | tf_op jit(solution)/shard_map/ppermute | solution.py:32
  476.1 53.4 %collective-permute-start.25 = (bf16[128,512]{1,0:T(8,128)(2,1)}, bf16[128,512]{1,0:T(8,128)(2,1)}, u32[]{:S(2)}, u32[]{:S(2)}) collective-permute-start(bf16[128,512]{1,0:T(8,128)(2,1)} %get-tuple-element.7), channel_id=1, source_target_pairs={{0,96},{32,64},{64,32},{96,0},{1,97},{33,65},{65,33},{97,1},{2,98}... | collective-permute-start | bytes 393224 | tf_op jit(solution)/shard_map/ppermute | solution.py:32
  478.7 7.4 %collective-permute-start.15 = (bf16[128,512]{1,0:T(8,128)(2,1)S(1)}, bf16[128,512]{1,0:T(8,128)(2,1)S(1)}, u32[]{:S(2)}, u32[]{:S(2)}) collective-permute-start(bf16[128,512]{1,0:T(8,128)(2,1)S(1)} %add_convert_fusion.1), channel_id=1, source_target_pairs={{8,0},{16,8},{24,16},{9,1},{17,9},{25,17},{10,2},{18,10},{26,18},{... | collective-permute-start | bytes 393224 | tf_op jit(solution)/shard_map/ppermute | solution.py:28
  487.9 20.2 %all-to-all-start.14 = ((bf16[8,128,512]{2,1,0:T(8,128)(2,1)}), bf16[8,128,512]{2,1,0:T(8,128)(2,1)}, u32[]{:S(2)}, u32[]{:S(2)}) async-start(bf16[8,128,512]{2,1,0:T(8,128)(2,1)} %broadcast_in_dim.102), calls=%async_computation.14 | async-start | bytes 2097152 | tf_op jit(solution)/shard_map/all_to_all | solution.py:36
  523.3 33.4 %all-to-all-start.15 = ((bf16[8,128,512]{2,1,0:T(8,128)(2,1)}), bf16[8,128,512]{2,1,0:T(8,128)(2,1)}, u32[]{:S(2)}, u32[]{:S(2)}) async-start(bf16[8,128,512]{2,1,0:T(8,128)(2,1)} %bitcast.510), calls=%async_computation.15 | async-start | bytes 2097152 | tf_op jit(solution)/shard_map/all_to_all | solution.py:36
  528.6 10.9 %collective-permute-start.6 = (bf16[128,1024]{1,0:T(8,128)(2,1)}, bf16[128,1024]{1,0:T(8,128)(2,1)S(1)}, u32[]{:S(2)}, u32[]{:S(2)}) collective-permute-start(bf16[128,1024]{1,0:T(8,128)(2,1)} %get-tuple-element.36), channel_id=1, source_target_pairs={{0,32},{32,0},{64,96},{96,64},{1,33},{33,1},{65,97},{97,65},{2,34}... | collective-permute-start | bytes 786440 | tf_op jit(solution)/shard_map/ppermute | solution.py:32
  532.1 14.2 %collective-permute-start.7 = (bf16[128,1024]{1,0:T(8,128)(2,1)}, bf16[128,1024]{1,0:T(8,128)(2,1)S(1)}, u32[]{:S(2)}, u32[]{:S(2)}) collective-permute-start(bf16[128,1024]{1,0:T(8,128)(2,1)} %get-tuple-element.35), channel_id=1, source_target_pairs={{0,64},{32,96},{64,0},{96,32},{1,65},{33,97},{65,1},{97,33},{2,66}... | collective-permute-start | bytes 786440 | tf_op jit(solution)/shard_map/ppermute | solution.py:32
  534.4 20.5 %collective-permute-start.8 = (bf16[128,1024]{1,0:T(8,128)(2,1)}, bf16[128,1024]{1,0:T(8,128)(2,1)S(1)}, u32[]{:S(2)}, u32[]{:S(2)}) collective-permute-start(bf16[128,1024]{1,0:T(8,128)(2,1)} %get-tuple-element.34), channel_id=1, source_target_pairs={{0,96},{32,64},{64,32},{96,0},{1,97},{33,65},{65,33},{97,1},{2,98}... | collective-permute-start | bytes 786440 | tf_op jit(solution)/shard_map/ppermute | solution.py:32
  537.0 22.6 %collective-permute-start.26 = (bf16[128,512]{1,0:T(8,128)(2,1)}, bf16[128,512]{1,0:T(8,128)(2,1)}, u32[]{:S(2)}, u32[]{:S(2)}) collective-permute-start(bf16[128,512]{1,0:T(8,128)(2,1)} %get-tuple-element.5), channel_id=1, source_target_pairs={{0,32},{32,0},{64,96},{96,64},{1,33},{33,1},{65,97},{97,65},{2,34}... | collective-permute-start | bytes 393224 | tf_op jit(solution)/shard_map/ppermute | solution.py:32
  537.2 23.9 %collective-permute-start.27 = (bf16[128,512]{1,0:T(8,128)(2,1)}, bf16[128,512]{1,0:T(8,128)(2,1)S(1)}, u32[]{:S(2)}, u32[]{:S(2)}) collective-permute-start(bf16[128,512]{1,0:T(8,128)(2,1)} %get-tuple-element.5), channel_id=1, source_target_pairs={{0,64},{32,96},{64,0},{96,32},{1,65},{33,97},{65,1},{97,33},{2,66}... | collective-permute-start | bytes 393224 | tf_op jit(solution)/shard_map/ppermute | solution.py:32
  539.5 31.1 %collective-permute-start.28 = (bf16[128,512]{1,0:T(8,128)(2,1)}, bf16[128,512]{1,0:T(8,128)(2,1)}, u32[]{:S(2)}, u32[]{:S(2)}) collective-permute-start(bf16[128,512]{1,0:T(8,128)(2,1)} %get-tuple-element.5), channel_id=1, source_target_pairs={{0,96},{32,64},{64,32},{96,0},{1,97},{33,65},{65,33},{97,1},{2,98}... | collective-permute-start | bytes 393224 | tf_op jit(solution)/shard_map/ppermute | solution.py:32
  556.7 18.6 %collective-permute-start.10 = (bf16[128,1024]{1,0:T(8,128)(2,1)}, bf16[128,1024]{1,0:T(8,128)(2,1)S(1)}, u32[]{:S(2)}, u32[]{:S(2)}) collective-permute-start(bf16[128,1024]{1,0:T(8,128)(2,1)} %get-tuple-element.32), channel_id=1, source_target_pairs={{0,32},{32,0},{64,96},{96,64},{1,33},{33,1},{65,97},{97,65},{2,34}... | collective-permute-start | bytes 786440 | tf_op jit(solution)/shard_map/ppermute | solution.py:32
  558.1 6.6 collective-permute-start.19
  561.9 15.0 %collective-permute-start.11 = (bf16[128,1024]{1,0:T(8,128)(2,1)}, bf16[128,1024]{1,0:T(8,128)(2,1)}, u32[]{:S(2)}, u32[]{:S(2)}) collective-permute-start(bf16[128,1024]{1,0:T(8,128)(2,1)} %get-tuple-element.31), channel_id=1, source_target_pairs={{0,64},{32,96},{64,0},{96,32},{1,65},{33,97},{65,1},{97,33},{2,66}... | collective-permute-start | bytes 786440 | tf_op jit(solution)/shard_map/ppermute | solution.py:32
  565.8 34.6 %all-to-all-start.16 = ((bf16[8,128,512]{2,1,0:T(8,128)(2,1)}), bf16[8,128,512]{2,1,0:T(8,128)(2,1)S(1)}, u32[]{:S(2)}, u32[]{:S(2)}) async-start(bf16[8,128,512]{2,1,0:T(8,128)(2,1)} %broadcast_in_dim.103), calls=%async_computation.16 | async-start | bytes 2097152 | tf_op jit(solution)/shard_map/all_to_all | solution.py:36
  572.1 19.9 %collective-permute-start.12 = (bf16[128,1024]{1,0:T(8,128)(2,1)S(1)}, bf16[128,1024]{1,0:T(8,128)(2,1)S(1)}, u32[]{:S(2)}, u32[]{:S(2)}) collective-permute-start(bf16[128,1024]{1,0:T(8,128)(2,1)S(1)} %copy-done.90), channel_id=1, source_target_pairs={{0,96},{32,64},{64,32},{96,0},{1,97},{33,65},{65,33},{97,1},{2,98}... | collective-permute-start | bytes 786440 | tf_op jit(solution)/shard_map/ppermute | solution.py:32
  576.9 16.1 %collective-permute-start.16 = (bf16[128,768]{0,1:T(8,128)(2,1)S(1)}, bf16[128,768]{0,1:T(8,128)(2,1)S(1)}, u32[]{:S(2)}, u32[]{:S(2)}) collective-permute-start(bf16[128,768]{0,1:T(8,128)(2,1)S(1)} %get-tuple-element.11), channel_id=1, source_target_pairs={{0,32},{32,0},{64,96},{96,64},{1,33},{33,1},{65,97},{97,65},{2,34}... | collective-permute-start | bytes 589832 | tf_op jit(solution)/shard_map/ppermute | solution.py:32
  578.5 15.2 %collective-permute-start.17 = (bf16[128,768]{0,1:T(8,128)(2,1)S(1)}, bf16[128,768]{0,1:T(8,128)(2,1)S(1)}, u32[]{:S(2)}, u32[]{:S(2)}) collective-permute-start(bf16[128,768]{0,1:T(8,128)(2,1)S(1)} %get-tuple-element.11), channel_id=1, source_target_pairs={{0,64},{32,96},{64,0},{96,32},{1,65},{33,97},{65,1},{97,33},{2,66}... | collective-permute-start | bytes 589832 | tf_op jit(solution)/shard_map/ppermute | solution.py:32
  592.8 6.8 %collective-permute-start.18 = (bf16[128,768]{0,1:T(8,128)(2,1)S(1)}, bf16[128,768]{0,1:T(8,128)(2,1)S(1)}, u32[]{:S(2)}, u32[]{:S(2)}) collective-permute-start(bf16[128,768]{0,1:T(8,128)(2,1)S(1)} %get-tuple-element.11), channel_id=1, source_target_pairs={{0,96},{32,64},{64,32},{96,0},{1,97},{33,65},{65,33},{97,1},{2,98}... | collective-permute-start | bytes 589832 | tf_op jit(solution)/shard_map/ppermute | solution.py:32
  610.9 7.7 %collective-permute-start.20 = (bf16[128,768]{0,1:T(8,128)(2,1)S(1)}, bf16[128,768]{0,1:T(8,128)(2,1)S(1)}, u32[]{:S(2)}, u32[]{:S(2)}) collective-permute-start(bf16[128,768]{0,1:T(8,128)(2,1)S(1)} %get-tuple-element.9), channel_id=1, source_target_pairs={{0,32},{32,0},{64,96},{96,64},{1,33},{33,1},{65,97},{97,65},{2,34}... | collective-permute-start | bytes 589832 | tf_op jit(solution)/shard_map/ppermute | solution.py:32
  613.1 8.2 %collective-permute-start.21 = (bf16[128,768]{0,1:T(8,128)(2,1)S(1)}, bf16[128,768]{0,1:T(8,128)(2,1)S(1)}, u32[]{:S(2)}, u32[]{:S(2)}) collective-permute-start(bf16[128,768]{0,1:T(8,128)(2,1)S(1)} %get-tuple-element.9), channel_id=1, source_target_pairs={{0,64},{32,96},{64,0},{96,32},{1,65},{33,97},{65,1},{97,33},{2,66}... | collective-permute-start | bytes 589832 | tf_op jit(solution)/shard_map/ppermute | solution.py:32
  614.7 11.7 %collective-permute-start.22 = (bf16[128,768]{0,1:T(8,128)(2,1)S(1)}, bf16[128,768]{0,1:T(8,128)(2,1)S(1)}, u32[]{:S(2)}, u32[]{:S(2)}) collective-permute-start(bf16[128,768]{0,1:T(8,128)(2,1)S(1)} %get-tuple-element.9), channel_id=1, source_target_pairs={{0,96},{32,64},{64,32},{96,0},{1,97},{33,65},{65,33},{97,1},{2,98}... | collective-permute-start | bytes 589832 | tf_op jit(solution)/shard_map/ppermute | solution.py:32
  616.9 14.2 %collective-permute-start.29 = (bf16[128,1024]{1,0:T(8,128)(2,1)S(1)}, bf16[128,1024]{1,0:T(8,128)(2,1)S(1)}, u32[]{:S(2)}, u32[]{:S(2)}) collective-permute-start(bf16[128,1024]{1,0:T(8,128)(2,1)S(1)} %get-tuple-element.28), channel_id=1, source_target_pairs={{0,32},{32,0},{64,96},{96,64},{1,33},{33,1},{65,97},{97,65},{2,34}... | collective-permute-start | bytes 786440 | tf_op jit(solution)/shard_map/ppermute | solution.py:32
  617.0 14.1 %collective-permute-start.30 = (bf16[128,1024]{1,0:T(8,128)(2,1)S(1)}, bf16[128,1024]{1,0:T(8,128)(2,1)S(1)}, u32[]{:S(2)}, u32[]{:S(2)}) collective-permute-start(bf16[128,1024]{1,0:T(8,128)(2,1)S(1)} %get-tuple-element.27), channel_id=1, source_target_pairs={{0,64},{32,96},{64,0},{96,32},{1,65},{33,97},{65,1},{97,33},{2,66}... | collective-permute-start | bytes 786440 | tf_op jit(solution)/shard_map/ppermute | solution.py:32
  618.6 18.1 %collective-permute-start.31 = (bf16[128,1024]{1,0:T(8,128)(2,1)S(1)}, bf16[128,1024]{1,0:T(8,128)(2,1)S(1)}, u32[]{:S(2)}, u32[]{:S(2)}) collective-permute-start(bf16[128,1024]{1,0:T(8,128)(2,1)S(1)} %get-tuple-element.26), channel_id=1, source_target_pairs={{0,96},{32,64},{64,32},{96,0},{1,97},{33,65},{65,33},{97,1},{2,98}... | collective-permute-start | bytes 786440 | tf_op jit(solution)/shard_map/ppermute | solution.py:32
  636.9 8.7 %collective-permute-start.32 = (bf16[128,1024]{1,0:T(8,128)(2,1)S(1)}, bf16[128,1024]{1,0:T(8,128)(2,1)S(1)}, u32[]{:S(2)}, u32[]{:S(2)}) collective-permute-start(bf16[128,1024]{1,0:T(8,128)(2,1)S(1)} %get-tuple-element.24), channel_id=1, source_target_pairs={{0,32},{32,0},{64,96},{96,64},{1,33},{33,1},{65,97},{97,65},{2,34}... | collective-permute-start | bytes 786440 | tf_op jit(solution)/shard_map/ppermute | solution.py:32
  639.5 8.9 %collective-permute-start.33 = (bf16[128,1024]{1,0:T(8,128)(2,1)S(1)}, bf16[128,1024]{1,0:T(8,128)(2,1)S(1)}, u32[]{:S(2)}, u32[]{:S(2)}) collective-permute-start(bf16[128,1024]{1,0:T(8,128)(2,1)S(1)} %get-tuple-element.23), channel_id=1, source_target_pairs={{0,64},{32,96},{64,0},{96,32},{1,65},{33,97},{65,1},{97,33},{2,66}... | collective-permute-start | bytes 786440 | tf_op jit(solution)/shard_map/ppermute | solution.py:32
  641.0 13.6 %collective-permute-start.34 = (bf16[128,1024]{1,0:T(8,128)(2,1)S(1)}, bf16[128,1024]{1,0:T(8,128)(2,1)S(1)}, u32[]{:S(2)}, u32[]{:S(2)}) collective-permute-start(bf16[128,1024]{1,0:T(8,128)(2,1)S(1)} %get-tuple-element.22), channel_id=1, source_target_pairs={{0,96},{32,64},{64,32},{96,0},{1,97},{33,65},{65,33},{97,1},{2,98}... | collective-permute-start | bytes 786440 | tf_op jit(solution)/shard_map/ppermute | solution.py:32
  (134 other events, 954.9 us)
Sparse Core Ops, SparseCore 0:
  194.6 44.5 all-gather.1

commit v2 on v1

v2 whole, which is shorter than its diff:
```python
import functools

import jax
import jax.numpy as jnp
from jax import lax
from jax.experimental import pallas as pl
from jax.experimental.pallas import tpu as pltpu
from jax.sharding import PartitionSpec as P

HEAD_DIM = 128
EPS = 1e-06
LOSS_SCALE = 16384.0
SCORE_SCALE = 1.0 / HEAD_DIM**0.5
F32 = jnp.float32
BF16 = jnp.bfloat16
VMEM_LIMIT = 48 * 1024 * 1024


def dot(a, b):
    return jnp.dot(a, b, preferred_element_type=F32)


def dot_nt(a, b):
    return lax.dot_general(a, b, (((1,), (1,)), ((), ())), preferred_element_type=F32)


def dot_tn(a, b):
    return lax.dot_general(a, b, (((0,), (0,)), ((), ())), preferred_element_type=F32)


def in_vmem():
    return pl.BlockSpec(memory_space=pltpu.VMEM)


def in_smem():
    return pl.BlockSpec(memory_space=pltpu.SMEM)


def anywhere():
    return pl.BlockSpec(memory_space=pl.ANY)


def kernel_params():
    return pltpu.CompilerParams(vmem_limit_bytes=VMEM_LIMIT)


def forward_kernel(len_ref, x_ref, wq_ref, wk_ref, wv_ref, wo_ref, part_ref, h_ref, scale_ref, pack_ref, o_ref):
    nblk, rows, dsh = x_ref.shape
    qh = wq_ref.shape[1] // HEAD_DIM
    sq = jnp.zeros((rows, 1), F32)
    for j in range(nblk):
        xf = x_ref[j].astype(F32)
        sq = sq + jnp.sum(xf * xf, axis=1, keepdims=True)
    scale = lax.rsqrt(sq / (nblk * dsh) + EPS)
    scale_ref[...] = jnp.broadcast_to(scale, scale_ref.shape)
    q = jnp.zeros((rows, wq_ref.shape[1]), F32)
    k = jnp.zeros((rows, HEAD_DIM), F32)
    v = jnp.zeros((rows, HEAD_DIM), F32)
    for j in range(nblk):
        h = (x_ref[j].astype(F32) * scale).astype(BF16)
        h_ref[j] = h
        at = pl.ds(j * dsh, dsh)
        q = q + dot(h, wq_ref[at, :])
        k = k + dot(h, wk_ref[at, :])
        v = v + dot(h, wv_ref[at, :])
    q = q.astype(BF16)
    k = k.astype(BF16)
    v = v.astype(BF16)
    top = qh * rows
    pack_ref[pl.ds(2 * top, rows), :] = k
    pack_ref[pl.ds(2 * top + rows, rows), :] = v
    posq = lax.broadcasted_iota(jnp.int32, (rows, rows), 0)
    posk = lax.broadcasted_iota(jnp.int32, (rows, rows), 1)
    keep = ((posk <= posq) & (posk < len_ref[0])).astype(F32)
    for n in range(qh):
        qn = q[:, n * HEAD_DIM : (n + 1) * HEAD_DIM]
        pack_ref[pl.ds(n * rows, rows), :] = qn
        expo = jnp.exp(dot_nt(qn, k) * SCORE_SCALE) * keep
        weights = (expo / jnp.sum(expo, axis=1, keepdims=True)).astype(BF16)
        pack_ref[pl.ds(top + n * rows, rows), :] = weights
        o_ref[:, pl.ds(n * HEAD_DIM, HEAD_DIM)] = dot(weights, v).astype(BF16)
    o = o_ref[...]
    for j in range(nblk):
        part_ref[j] = dot(o, wo_ref[:, pl.ds(j * dsh, dsh)]).astype(BF16)


def forward(length, x, wq, wk, wv, wo):
    nblk, rows, dsh = x.shape
    qcol = wq.shape[1]
    packed = 2 * qcol // HEAD_DIM * rows + 2 * rows
    out = pl.pallas_call(
        forward_kernel,
        out_shape=(
            jax.ShapeDtypeStruct(x.shape, BF16),
            jax.ShapeDtypeStruct(x.shape, BF16),
            jax.ShapeDtypeStruct((rows, HEAD_DIM), F32),
            jax.ShapeDtypeStruct((packed, HEAD_DIM), BF16),
            jax.ShapeDtypeStruct((rows, qcol), BF16),
        ),
        in_specs=[in_smem()] + [in_vmem()] * 5,
        out_specs=tuple([in_vmem()] * 5),
        compiler_params=kernel_params(),
        cost_estimate=pl.CostEstimate(
            flops=2 * rows * nblk * dsh * (2 * qcol + 2 * HEAD_DIM),
            bytes_accessed=4 * nblk * dsh * (qcol + HEAD_DIM),
            transcendentals=rows * rows * qcol // HEAD_DIM,
        ),
        name="forward_layer",
    )(length.reshape(1), x, wq, wk, wv, wo)
    return dict(zip(("part", "h", "scale", "pack", "o"), out))


def backward_kernel(
    with_input, flag_ref, g_ref, pack0_ref, pack1_ref, h0_ref, h1_ref, scale0_ref, scale1_ref,
    wq_ref, wk_ref, wv_ref, wo_ref, *rest
):
    if with_input:
        d_ref, dx_ref, pack_ref, h_ref, scale_ref, dh_ref, sems = rest
    else:
        d_ref, pack_ref, sems = rest
    nblk, rows, dsh = g_ref.shape
    qcol = wq_ref.shape[1]
    qh = qcol // HEAD_DIM
    top = qh * rows
    pairs = [(pack0_ref, pack1_ref, pack_ref)]
    if with_input:
        pairs += [(h0_ref, h1_ref, h_ref), (scale0_ref, scale1_ref, scale_ref)]
    for at, (one, two, to) in enumerate(pairs):

        @pl.when(flag_ref[0] == 0)
        def _(one=one, to=to, at=at):
            pltpu.make_async_copy(one, to, sems.at[at]).start()

        @pl.when(flag_ref[0] != 0)
        def _(two=two, to=to, at=at):
            pltpu.make_async_copy(two, to, sems.at[at]).start()

    do = jnp.zeros((rows, qcol), F32)
    for j in range(nblk):
        do = do + dot_nt(g_ref[j], wo_ref[:, pl.ds(j * dsh, dsh)])
    do = do.astype(BF16)
    pltpu.make_async_copy(pack0_ref, pack_ref, sems.at[0]).wait()
    k = pack_ref[pl.ds(2 * top, rows), :]
    v = pack_ref[pl.ds(2 * top + rows, rows), :]
    dk = jnp.zeros((rows, HEAD_DIM), F32)
    dv = jnp.zeros((rows, HEAD_DIM), F32)
    for n in range(qh):
        cols = slice(n * HEAD_DIM, (n + 1) * HEAD_DIM)
        qn = pack_ref[pl.ds(n * rows, rows), :]
        weights = pack_ref[pl.ds(top + n * rows, rows), :]
        don = do[:, cols]
        wf = weights.astype(F32)
        dw = dot_nt(don, v)
        ds = wf * (dw - jnp.sum(dw * wf, axis=1, keepdims=True)) * SCORE_SCALE
        ds = ds.astype(BF16)
        d_ref[:, cols] = dot(ds, k).astype(BF16)
        dk = dk + dot_tn(ds, qn)
        dv = dv + dot_tn(weights, don)
    d_ref[:, qcol : qcol + HEAD_DIM] = dk.astype(BF16)
    d_ref[:, qcol + HEAD_DIM :] = dv.astype(BF16)
    if not with_input:
        return
    pltpu.make_async_copy(h0_ref, h_ref, sems.at[1]).wait()
    pltpu.make_async_copy(scale0_ref, scale_ref, sems.at[2]).wait()
    dq = d_ref[:, :qcol]
    dk = dk.astype(BF16)
    dv = dv.astype(BF16)
    inner = jnp.zeros((rows, 1), F32)
    for j in range(nblk):
        at = pl.ds(j * dsh, dsh)
        dh = dot_nt(dq, wq_ref[at, :]) + dot_nt(dk, wk_ref[at, :]) + dot_nt(dv, wv_ref[at, :])
        dh_ref[j] = dh
        inner = inner + jnp.sum(dh * h_ref[j].astype(F32), axis=1, keepdims=True)
    inner = inner / (nblk * dsh)
    scale = scale_ref[:, :1]
    for j in range(nblk):
        dx_ref[j] = (scale * (dh_ref[j] - h_ref[j].astype(F32) * inner)).astype(BF16)


def backward(flag, g, one, two, weights, with_input):
    nblk, rows, dsh = g.shape
    wq, wk, wv, wo = weights
    qcol = wq.shape[1]
    out_shape = [jax.ShapeDtypeStruct((rows, qcol + 2 * HEAD_DIM), BF16)]
    scratch = [pltpu.VMEM(one["pack"].shape, BF16)]
    if with_input:
        out_shape.append(jax.ShapeDtypeStruct(g.shape, BF16))
        scratch += [
            pltpu.VMEM(g.shape, BF16),
            pltpu.VMEM(one["scale"].shape, F32),
            pltpu.VMEM(g.shape, F32),
        ]
    scratch.append(pltpu.SemaphoreType.DMA((3,)))
    return pl.pallas_call(
        functools.partial(backward_kernel, with_input),
        out_shape=tuple(out_shape),
        in_specs=[in_smem(), in_vmem()] + [anywhere()] * 6 + [in_vmem()] * 4,
        out_specs=tuple([in_vmem()] * len(out_shape)),
        scratch_shapes=scratch,
        compiler_params=kernel_params(),
        cost_estimate=pl.CostEstimate(
            flops=2 * rows * nblk * dsh * (2 * qcol + 2 * HEAD_DIM),
            bytes_accessed=4 * nblk * dsh * (qcol + HEAD_DIM),
            transcendentals=0,
        ),
        name="backward_layer" if with_input else "backward_heads",
    )(
        flag.astype(jnp.int32).reshape(1), g, one["pack"], two["pack"], one["h"], two["h"],
        one["scale"], two["scale"], wq, wk, wv, wo,
    )


def qkv_grad_kernel(n, *refs):
    h_refs, d_refs = refs[:n], refs[n : 2 * n]
    gq_ref, gk_ref, gv_ref, h_all, d_all = refs[2 * n :]
    rows = d_refs[0].shape[0]
    nblk, _, dsh = h_refs[0].shape
    qcol = gq_ref.shape[1]
    for i in range(n):
        at = pl.ds(i * rows, rows)
        d_all[at, :] = d_refs[i][...]
        for b in range(nblk):
            h_all[at, pl.ds(b * dsh, dsh)] = h_refs[i][b]
    for c in range(nblk * dsh // 256):
        cols = pl.ds(c * 256, 256)
        got = dot_tn(h_all[:, cols], d_all[...])
        gq_ref[cols, :] = got[:, :qcol]
        gk_ref[cols, :] = got[:, qcol : qcol + HEAD_DIM]
        gv_ref[cols, :] = got[:, qcol + HEAD_DIM :]


def qkv_grad(h, d):
    n = len(h)
    rows, dcol = d[0].shape
    nblk, _, dsh = h[0].shape
    width = nblk * dsh
    return pl.pallas_call(
        functools.partial(qkv_grad_kernel, n),
        out_shape=(
            jax.ShapeDtypeStruct((width, dcol - 2 * HEAD_DIM), F32),
            jax.ShapeDtypeStruct((width, HEAD_DIM), F32),
            jax.ShapeDtypeStruct((width, HEAD_DIM), F32),
        ),
        in_specs=[in_vmem()] * (2 * n),
        out_specs=tuple([in_vmem()] * 3),
        scratch_shapes=[pltpu.VMEM((n * rows, width), BF16), pltpu.VMEM((n * rows, dcol), BF16)],
        compiler_params=kernel_params(),
        name="qkv_grad",
    )(*h, *d)


def out_grad_kernel(n, *refs):
    o_refs, g_refs = refs[:n], refs[n : 2 * n]
    go_ref, o_all, g_all = refs[2 * n :]
    rows, qcol = o_refs[0].shape
    nblk, _, dsh = g_refs[0].shape
    for i in range(n):
        at = pl.ds(i * rows, rows)
        o_all[at, :] = o_refs[i][...]
        for b in range(nblk):
            g_all[at, pl.ds(b * dsh, dsh)] = g_refs[i][b]
    for c in range(qcol // 256):
        cols = pl.ds(c * 256, 256)
        go_ref[cols, :] = dot_tn(o_all[:, cols], g_all[...])


def out_grad(o, g):
    n = len(o)
    rows, qcol = o[0].shape
    nblk, _, dsh = g[0].shape
    width = nblk * dsh
    return pl.pallas_call(
        functools.partial(out_grad_kernel, n),
        out_shape=jax.ShapeDtypeStruct((qcol, width), F32),
        in_specs=[in_vmem()] * (2 * n),
        out_specs=in_vmem(),
        scratch_shapes=[pltpu.VMEM((n * rows, qcol), BF16), pltpu.VMEM((n * rows, width), BF16)],
        compiler_params=kernel_params(),
        name="out_grad",
    )(*o, *g)


def passed_along(x, axis, by):
    peers = lax.axis_size(axis)
    pairs = [(i, i + by) for i in range(peers) if 0 <= i + by < peers]
    return lax.ppermute(x, axis, pairs)


def swapped(x, axis, mask):
    return lax.ppermute(x, axis, [(i, i ^ mask) for i in range(lax.axis_size(axis))])


def exchange(blocks):
    return lax.all_to_all(blocks, "tensor", split_axis=0, concat_axis=0, tiled=True)


def gathered(cur):
    return exchange(jnp.broadcast_to(cur[None], (lax.axis_size("tensor"),) + cur.shape))


def step_end_grad(rows, w_class, tgt, tokens_total):
    width = rows.shape[1]
    zeta = dot(rows, w_class)
    rf = rows.astype(F32)
    rstd = lax.rsqrt(jnp.sum(rf * rf, axis=1) / width + EPS)
    logits = zeta * rstd[:, None]
    expo = jnp.exp(logits)
    prob = expo / jnp.sum(expo, axis=1, keepdims=True)
    onehot = (tgt[:, None] == jnp.arange(logits.shape[1], dtype=jnp.int32)[None, :]).astype(F32)
    dlog = LOSS_SCALE / tokens_total * (prob - onehot)
    dzeta = dlog * rstd[:, None]
    dmean = jnp.sum(dlog * zeta, axis=1) * -0.5 * rstd * rstd * rstd
    drows = jnp.dot(dzeta, w_class.astype(F32).T, precision=lax.Precision.HIGHEST)
    drows = drows + dmean[:, None] * 2.0 * rf / width
    return drows.astype(BF16)


def among_replicas(x):
    return [x] + [swapped(x, "dp", k) for k in (1, 2, 3)]


def quarters_among_replicas(x, mine_rep):
    ndp = lax.axis_size("dp")
    size = x.shape[0] // ndp
    take = lambda who: lax.dynamic_slice_in_dim(x, who * size, size, axis=0)
    return [take(mine_rep)] + [swapped(take(mine_rep ^ k), "dp", k) for k in (1, 2, 3)]


def by_section(section_at, choices):
    out = choices[-1]
    for s in reversed(range(len(choices) - 1)):
        out = jnp.where(section_at == s, choices[s], out)
    return out


def after(x, *marks):
    return lax.optimization_barrier((x,) + marks)[0]


def on_device(embeds, source, lengths, bounds, targets, w_query, w_key, w_value, w_out, w_class):
    nst = lax.axis_size("section")
    peers = lax.axis_size("tensor")
    rep = lax.axis_index("dp")
    section_at = lax.axis_index("section")
    tensor_at = lax.axis_index("tensor")
    ntr, width, dsh = embeds.shape
    weights = (w_query[0], w_key[0], w_value[0], w_out[0])
    w_class = lax.all_gather(w_class, "tensor", axis=0, tiled=True)

    hi, core = rep // 2, rep % 2
    slots = source.reshape(2, 2, ntr) - rep * ntr

    def mine_for(col):
        owner = lax.dynamic_slice_in_dim(slots, col, 1, axis=1)[:, 0]
        out = jnp.zeros((2, ntr, width, dsh), BF16)
        for n in range(ntr):
            out = jnp.where((owner == n)[:, :, None, None], embeds[n][None, None], out)
        return out

    both = mine_for(core) + swapped(mine_for(1 - core), "dp", 1)
    own = lax.dynamic_slice_in_dim(both, hi, 1, axis=0)[0]
    away = lax.dynamic_slice_in_dim(both, 1 - hi, 1, axis=0)[0]
    first = [own[j] + swapped(away[j], "dp", 2) for j in range(ntr)]

    wanted = lax.dynamic_slice_in_dim(source, rep * ntr, ntr)
    lens = lengths[wanted]
    bnd = bounds[wanted]
    tgt = targets[wanted]
    tokens_total = jnp.sum(lens).astype(F32)
    picks = [
        (bnd[j][:, None] == jnp.arange(width, dtype=jnp.int32)[None, :]).astype(BF16)
        for j in range(ntr)
    ]
    nstep = bnd.shape[1]

    def ends_of(which, blocks):
        return jnp.einsum("sr,brd->bsd", picks[which], blocks, preferred_element_type=F32)

    def with_ends(blocks, ends):
        flat = ends.astype(BF16).reshape(1, peers * nstep, dsh)
        return jnp.concatenate(
            [blocks, jnp.broadcast_to(flat, (peers, peers * nstep, dsh))], axis=1
        )

    def sum_of(got):
        return jnp.sum(got[:, :width].astype(F32), axis=0)

    def end_cotangent(which, got, x):
        parts = jnp.sum(got[:, width:].astype(F32), axis=0).reshape(peers, nstep, dsh)
        rows = (ends_of(which, x) + parts).astype(BF16)
        rows = rows.transpose(1, 0, 2).reshape(nstep, peers * dsh)
        grad = step_end_grad(rows, w_class, tgt[which], tokens_total)
        grad = grad.reshape(nstep, peers, dsh)
        back = jnp.einsum("sr,sbd->brd", picks[which], grad, preferred_element_type=F32)
        return back.astype(BF16)

    kept = []
    arriving = None
    for turn in range(nst):
        cur = first[turn] if turn < ntr else jnp.zeros((width, dsh), BF16)
        if arriving is not None:
            cur = jnp.where(section_at == 0, cur, arriving)
        length = jnp.where(section_at == turn, lens[0], lens[1])
        x = gathered(cur)
        now = forward(length, x, *weights)
        kept.append(now)
        blocks = now["part"]
        if turn == nst - 1:
            blocks = with_ends(blocks, ends_of(0, blocks))
        got = exchange(blocks)
        arriving = passed_along((cur.astype(F32) + sum_of(got)).astype(BF16), "section", 1)

    taken = {}
    top = jnp.int32(0)
    g_top = end_cotangent(0, got, x)
    grad = lax.dynamic_slice_in_dim(g_top, tensor_at, 1, axis=0)[0]
    d, dx = backward(top, after(g_top, arriving), kept[-1], kept[-1], weights, True)
    taken[nst] = (d, g_top)
    x = gathered(arriving)
    now = forward(lens[1], x, *weights)
    kept.append(now)
    got = exchange(with_ends(dx, ends_of(1, now["part"])))
    g_top = end_cotangent(1, got, x)

    h_rows, o_rows, g_rows, d_rows = [], [], [], []
    for turn in range(nst + 1, 2 * nst + 1):
        grad = (grad.astype(F32) + sum_of(got)).astype(BF16)
        which = turn - nst - 1
        if which < ntr:
            h = by_section(section_at, [kept[s + which]["h"] for s in range(nst)])
            o = by_section(section_at, [kept[s + which]["o"] for s in range(nst)])
            h_rows += quarters_among_replicas(after(h, grad), rep)
            o_rows += among_replicas(after(o, grad))
        elif turn == 2 * nst:
            back = [taken[2 * nst - 1 - s] for s in range(nst)]
            d_rows += among_replicas(after(by_section(section_at, [b[0] for b in back]), grad))
            g_rows += quarters_among_replicas(
                after(by_section(section_at, [b[1] for b in back]), grad), rep
            )
        grad = passed_along(grad, "section", -1)
        g = gathered(grad)
        if turn == nst + 1:
            g = jnp.where(section_at == nst - 1, g_top, g)
            own_top = lax.dynamic_slice_in_dim(g_top, tensor_at, 1, axis=0)[0]
            grad = jnp.where(section_at == nst - 1, own_top, grad)
        late = 2 * nst + 1 - turn
        early = max(late - 2, 0)
        flag = section_at == late - 1
        if turn < 2 * nst:
            d, dx = backward(flag, g, kept[early], kept[late], weights, True)
            taken[turn] = (d, g)
            got = exchange(dx)
        else:
            (d,) = backward(flag, g, kept[early], kept[late], weights, False)
            taken[turn] = (d, g)

    back = [taken[2 * nst - s] for s in range(nst)]
    g_rows += quarters_among_replicas(by_section(section_at, [b[1] for b in back]), rep)
    d_rows += among_replicas(by_section(section_at, [b[0] for b in back]))
    grad_q, grad_k, grad_v = qkv_grad(h_rows, d_rows)
    grad_o = out_grad(o_rows, g_rows)
    return (grad_q[None], grad_k[None], grad_v[None], grad_o[None])


def solution(mesh):
    placed = (
        P("dp", None, "tensor"),
        P(),
        P(),
        P(),
        P(),
        P("section", None, "tensor"),
        P("section", None, "tensor"),
        P("section", None, "tensor"),
        P("section", "tensor", None),
        P("tensor", None),
    )
    return jax.shard_map(
        on_device,
        mesh=mesh,
        in_specs=placed,
        out_specs=(
            P("section", "dp", "tensor"),
            P("section", "dp", "tensor"),
            P("section", "dp", "tensor"),
            P("section", "tensor", "dp"),
        ),
        check_vma=False,
    )
```

time: 677 us -> 600 us (0.89)
  matrix products: 121 us -> 15.4 us
  Pallas kernels: 0 us -> 86.3 us
  local copies, waits for them, and re-layouts: 102 us -> 46.3 us
  blocking collectives: 58.7 us -> 83.6 us
  other arithmetic: 50.7 us -> 26.2 us
  waiting for transfers between devices: 188 us -> 171 us
  starting transfers between devices: 128 us -> 140 us
    pallas_call x0 -> x12, Pallas kernels: none -> 86.3 us  [the longest x5 44.6 us: backward(): pl.pallas_call(functools.partial(backward_kernel, with_input), out_shape=...]
    dot_general x43 -> x6, matrix products: 64.5 us -> 7.21 us  [the longest x4 5.09 us: ends_of(): jnp.einsum('sr,brd->bsd', picks[which], blocks, preferred_element_type=F32)]
    dot_general x35 -> x2, matrix products: 51.8 us -> 3.76 us  [dot(): return jnp.dot(a, b, preferred_element_type=F32)]
    reshape x48 -> x2, local copies, waits for them, and re-layouts: 38.6 us -> 1.49 us  [end_cotangent(): jnp.sum(got[:, width:].astype(F32), axis=0).reshape(peers, nstep, dsh)]
    all_to_all x3 -> x5, blocking collectives: 58.7 us -> 83.6 us  [exchange(): lax.all_to_all(blocks, 'tensor', split_axis=0, concat_axis=0, tiled=True)]
    ppermute x27, starting transfers between devices: 36.4 us -> 60.8 us  [swapped(): lax.ppermute(x, axis, [(i, i ^ mask) for i in range(lax.axis_size(axis))])]
    all_to_all x14 -> x12, waiting for transfers between devices: 117 us -> 97 us  [exchange(): lax.all_to_all(blocks, 'tensor', split_axis=0, concat_axis=0, tiled=True)]
    ppermute x27, waiting for transfers between devices: 54.1 us -> 39.2 us  [swapped(): lax.ppermute(x, axis, [(i, i ^ mask) for i in range(lax.axis_size(axis))])]
  transfers between devices with their start and end apart: 50 -> 48, of which waited for: 27 -> 30; matrix products, arithmetic and copies ran while one was open for 19% -> 6% of each run, Pallas kernels for 0% -> 3%
where the time goes in v2:
time: 600 us; the launch traced here: 590 us
  waiting for transfers between devices  171 us (28%)
  starting transfers between devices  140 us (23%)
  Pallas kernels  86.3 us (14%)
  blocking collectives  83.6 us (14%)
  local copies, waits for them, and re-layouts  46.3 us (8%)
  other arithmetic  26.2 us (4%)
  between operations  21.5 us (4%)
  matrix products  15.4 us (3%)
    all_to_all x12, waiting for transfers between devices, exchange(): lax.all_to_all(blocks, 'tensor', split_axis=0, concat_axis=0, tiled=True)  97 us
    all_to_all x5, blocking collectives, exchange(): lax.all_to_all(blocks, 'tensor', split_axis=0, concat_axis=0, tiled=True)  83.6 us
    ppermute x27, starting transfers between devices, swapped(): lax.ppermute(x, axis, [(i, i ^ mask) for i in range(lax.axis_size(axis))])  60.8 us
    all_to_all x12, starting transfers between devices, exchange(): lax.all_to_all(blocks, 'tensor', split_axis=0, concat_axis=0, tiled=True)  57.8 us
    pallas_call x5, Pallas kernels, backward(): pl.pallas_call(functools.partial(backward_kernel, with_input), out_shape=...  44.6 us
    ppermute x27, waiting for transfers between devices, swapped(): lax.ppermute(x, axis, [(i, i ^ mask) for i in range(lax.axis_size(axis))])  39.2 us
    pallas_call x5, Pallas kernels, forward(): pl.pallas_call(forward_kernel, out_shape=(jax.ShapeDtypeStruct(x.shape, B...  33.4 us
    unnamed x164, local copies, waits for them, and re-layouts  23.7 us
  transfers between devices with their start and end apart: 48, of which 30 were waited for; matrix products, arithmetic and copies ran while one was open for 6% of the time, Pallas kernels for 3%

profile of v2, /device:TPU:1, one launch (start us, length us, event | category | flops | bytes accessed | tf_op | source)
XLA Modules:
  0.0 590.0 jit_solution(11386944754115593760)
XLA Ops:
  19.7 5.2 all-to-all-start
  27.6 11.4 %all-to-all-done.x_ref = bf16[8,128,512]{2,1,0:T(8,128)(2,1)S(1)} async-done(((bf16[8,128,512]{2,1,0:T(8,128)(2,1)}), bf16[8,128,512]{2,1,0:T(8,128)(2,1)S(1)}, u32[]{:S(2)}, u32[]{:S(2)}) %all-to-all-start) | async-done | bytes 1048608 | tf_op jit(solution)/shard_map/all_to_all | solution.py:294
  39.0 6.5 %forward_layer.5 = (bf16[8,128,512]{2,1,0:T(8,128)(2,1)S(1)}, bf16[8,128,512]{2,1,0:T(8,128)(2,1)S(1)}, f32[128,128]{1,0:T(8,128)S(1)}, bf16[1280,128]{1,0:T(8,128)(2,1)S(1)}, bf16[128,512]{1,0:T(8,128)(2,1)S(1)}) custom-call(s32[1]{0:T(128)} %bitcast.2.len_ref, bf16[8,128,512]{2,1,0:T(8,128)(2,1)S(1)} %all-to-all-done.x_ref, bf16[4096,512]{1,0:T(8,128)(2,1)} %bitcast.141, ...), custom_call_target="tpu_custom_call" | custom-call | flops 1342177280 | bytes 10485760 | tf_op jit(solution)/shard_map/forward_layer/pallas_call | solution.py:91
  49.5 4.6 all-to-all-start.1
  56.5 12.5 %all-to-all-done.1 = bf16[8,128,512]{2,1,0:T(8,128)(2,1)S(1)} async-done(((bf16[8,128,512]{2,1,0:T(8,128)(2,1)}), bf16[8,128,512]{2,1,0:T(8,128)(2,1)S(1)}, u32[]{:S(2)}, u32[]{:S(2)}) %all-to-all-start.1) | async-done | bytes 1048608 | tf_op jit(solution)/shard_map/all_to_all | solution.py:294
  81.6 10.2 %all-to-all-done.2.x_ref = bf16[8,128,512]{2,1,0:T(8,128)(2,1)S(1)} async-done(((bf16[8,128,512]{2,1,0:T(8,128)(2,1)}), bf16[8,128,512]{2,1,0:T(8,128)(2,1)S(1)}, u32[]{:S(2)}, u32[]{:S(2)}) %all-to-all-start.2) | async-done | bytes 1048608 | tf_op jit(solution)/shard_map/all_to_all | solution.py:294
  91.8 6.5 %forward_layer.6 = (bf16[8,128,512]{2,1,0:T(8,128)(2,1)S(1)}, bf16[8,128,512]{2,1,0:T(8,128)(2,1)S(1)}, f32[128,128]{1,0:T(8,128)S(1)}, bf16[1280,128]{1,0:T(8,128)(2,1)S(1)}, bf16[128,512]{1,0:T(8,128)(2,1)S(1)}) custom-call(s32[1]{0:T(128)} %bitcast.11.len_ref, bf16[8,128,512]{2,1,0:T(8,128)(2,1)S(1)} %all-to-all-done.2.x_ref, ...), custom_call_target="tpu_custom_call" | custom-call | flops 1342177280 | bytes 10485760 | tf_op jit(solution)/shard_map/forward_layer/pallas_call | solution.py:91
  98.3 21.2 %all_to_all.85 = bf16[8,128,512]{2,1,0:T(8,128)(2,1)S(1)} all-to-all(bf16[8,128,512]{2,1,0:T(8,128)(2,1)S(1)} %get-tuple-element.50), channel_id=1, replica_groups=mesh['dp'=4,'section'=4,'tensor'=8] {'tensor'}, dimensions={0} | all-to-all | bytes 2097152 | tf_op jit(solution)/shard_map/all_to_all | solution.py:294
  119.7 3.9 collective-permute-start.4
  131.5 9.1 %all-to-all-done.4.x_ref = bf16[8,128,512]{2,1,0:T(8,128)(2,1)S(1)} async-done(((bf16[8,128,512]{2,1,0:T(8,128)(2,1)}), bf16[8,128,512]{2,1,0:T(8,128)(2,1)S(1)}, u32[]{:S(2)}, u32[]{:S(2)}) %all-to-all-start.4) | async-done | bytes 1048608 | tf_op jit(solution)/shard_map/all_to_all | solution.py:294
  140.6 6.5 %forward_layer.7 = (bf16[8,128,512]{2,1,0:T(8,128)(2,1)S(1)}, bf16[8,128,512]{2,1,0:T(8,128)(2,1)S(1)}, f32[128,128]{1,0:T(8,128)S(1)}, bf16[1280,128]{1,0:T(8,128)(2,1)S(1)}, bf16[128,512]{1,0:T(8,128)(2,1)S(1)}) custom-call(s32[1]{0:T(128)} %bitcast.14.len_ref, bf16[8,128,512]{2,1,0:T(8,128)(2,1)S(1)} %all-to-all-done.4.x_ref, ...), custom_call_target="tpu_custom_call" | custom-call | flops 1342177280 | bytes 10485760 | tf_op jit(solution)/shard_map/forward_layer/pallas_call | solution.py:91
  147.1 20.7 %all_to_all.86 = bf16[8,128,512]{2,1,0:T(8,128)(2,1)S(1)} all-to-all(bf16[8,128,512]{2,1,0:T(8,128)(2,1)S(1)} %get-tuple-element.52), channel_id=1, replica_groups=mesh['dp'=4,'section'=4,'tensor'=8] {'tensor'}, dimensions={0} | all-to-all | bytes 2097152 | tf_op jit(solution)/shard_map/all_to_all | solution.py:294
  175.6 3.8 all-to-all-start.6
  181.3 8.0 %all-to-all-done.6.x_ref = bf16[8,128,512]{2,1,0:T(8,128)(2,1)S(1)} async-done(((bf16[8,128,512]{2,1,0:T(8,128)(2,1)}), bf16[8,128,512]{2,1,0:T(8,128)(2,1)S(1)}, u32[]{:S(2)}, u32[]{:S(2)}) %all-to-all-start.6) | async-done | bytes 1048608 | tf_op jit(solution)/shard_map/all_to_all | solution.py:294
  191.5 6.5 %forward_layer.8 = (bf16[8,128,512]{2,1,0:T(8,128)(2,1)S(1)}, bf16[8,128,512]{2,1,0:T(8,128)(2,1)S(1)}, f32[128,128]{1,0:T(8,128)S(1)}, bf16[1280,128]{1,0:T(8,128)(2,1)S(1)}, bf16[128,512]{1,0:T(8,128)(2,1)S(1)}) custom-call(s32[1]{0:T(128)} %bitcast.15.len_ref, bf16[8,128,512]{2,1,0:T(8,128)(2,1)S(1)} %copy-done.17, bf16[4096,512]{1,0:T(8,128)(2,1)} %bitcast.144, ...), custom_call_target="tpu_custom_call" | custom-call | flops 1342177280 | bytes 10485760 | tf_op jit(solution)/shard_map/forward_layer/pallas_call | solution.py:91
  205.1 7.8 %all-to-all-start.7 = ((bf16[8,160,512]{2,1,0:T(8,128)(2,1)}), bf16[8,160,512]{2,1,0:T(8,128)(2,1)}, u32[]{:S(2)}, u32[]{:S(2)}) async-start(bf16[8,160,512]{2,1,0:T(8,128)(2,1)} %pad_maximum_fusion), calls=%async_computation.7 | async-start | bytes 2621440 | tf_op jit(solution)/shard_map/all_to_all | solution.py:294
  218.3 11.2 %all-to-all-done.7 = bf16[8,160,512]{2,1,0:T(8,128)(2,1)} async-done(((bf16[8,160,512]{2,1,0:T(8,128)(2,1)}), bf16[8,160,512]{2,1,0:T(8,128)(2,1)}, u32[]{:S(2)}, u32[]{:S(2)}) %all-to-all-start.7) | async-done | bytes 1310752 | tf_op jit(solution)/shard_map/all_to_all | solution.py:294
  234.7 5.0 collective-permute-start.6
  242.5 11.1 %all-gather.2.cloned.1.call-done = bf16[4096,128]{1,0:T(8,128)(2,1)} async-done(((bf16[512,128]{1,0:T(8,128)(2,1)}), bf16[4096,128]{1,0:T(8,128)(2,1)}) %all-gather.2.cloned.1.call-update) | async-done | bytes 1048592 | tf_op jit(solution)/shard_map/all_gather | solution.py:348
  257.7 4.2 all-to-all-start.8
  266.3 8.8 %backward_layer.4 = (bf16[128,768]{1,0:T(8,128)(2,1)S(1)}, bf16[8,128,512]{2,1,0:T(8,128)(2,1)S(1)}) custom-call(s32[1]{0:T(128)} %constant.69.clone.1.flag_ref, bf16[8,128,512]{2,1,0:T(8,128)(2,1)S(1)} %bitcast.140, bf16[1280,128]{1,0:T(8,128)(2,1)S(1)} %get-tuple-element.56.pack0_ref.pack1_ref, ...), custom_call_target="tpu_custom_call" | custom-call | flops 1342177280 | bytes 10485760 | tf_op jit(solution)/shard_map/backward_layer/pallas_call | solution.py:194
  277.8 7.4 %forward_layer.9 = (bf16[8,128,512]{2,1,0:T(8,128)(2,1)S(1)}, bf16[8,128,512]{2,1,0:T(8,128)(2,1)S(1)}, f32[128,128]{1,0:T(8,128)S(1)}, bf16[1280,128]{1,0:T(8,128)(2,1)S(1)}, bf16[128,512]{1,0:T(8,128)(2,1)S(1)}) custom-call(s32[1]{0:T(128)} %get-tuple-element.126.len_ref, bf16[8,128,512]{2,1,0:T(8,128)(2,1)} %all-to-all-done.8.x_ref, ...), custom_call_target="tpu_custom_call" | custom-call | flops 1342177280 | bytes 10485760 | tf_op jit(solution)/shard_map/forward_layer/pallas_call | solution.py:91
  290.6 5.2 all-to-all-start.9
  295.8 11.9 %all-to-all-done.9 = bf16[8,160,512]{2,1,0:T(8,128)(2,1)} async-done(((bf16[8,160,512]{2,1,0:T(8,128)(2,1)}), bf16[8,160,512]{2,1,0:T(8,128)(2,1)}, u32[]{:S(2)}, u32[]{:S(2)}) %all-to-all-start.9) | async-done | bytes 1310752 | tf_op jit(solution)/shard_map/all_to_all | solution.py:294
  317.0 6.8 %all-to-all-start.10 = ((bf16[8,128,512]{2,1,0:T(8,128)(2,1)}), bf16[8,128,512]{2,1,0:T(8,128)(2,1)}, u32[]{:S(2)}, u32[]{:S(2)}) async-start(bf16[8,128,512]{2,1,0:T(8,128)(2,1)} %broadcast_in_dim.165), calls=%async_computation.10 | async-start | bytes 2097152 | tf_op jit(solution)/shard_map/all_to_all | solution.py:294
  329.4 4.0 all-to-all-done.10
  335.4 9.6 %backward_layer.5 = (bf16[128,768]{1,0:T(8,128)(2,1)S(1)}, bf16[8,128,512]{2,1,0:T(8,128)(2,1)S(1)}) custom-call(s32[1]{0:T(128)} %bitcast.39.flag_ref, bf16[8,128,512]{2,1,0:T(8,128)(2,1)S(1)} %bitcast_select_fusion.g_ref, bf16[1280,128]{1,0:T(8,128)(2,1)S(1)} %copy-done.28, bf16[1280,128]{1,0:T(8,128)(2,1)S(1)} %copy-done.36, ...), custom_call_target="tpu_custom_call" | custom-call | flops 1342177280 | bytes 10485760 | tf_op jit(solution)/shard_map/backward_layer/pallas_call | solution.py:194
  345.0 14.7 %all_to_all.87 = bf16[8,128,512]{2,1,0:T(8,128)(2,1)S(1)} all-to-all(bf16[8,128,512]{2,1,0:T(8,128)(2,1)S(1)} %get-tuple-element.66), channel_id=1, replica_groups=mesh['dp'=4,'section'=4,'tensor'=8] {'tensor'}, dimensions={0} | all-to-all | bytes 2097152 | tf_op jit(solution)/shard_map/all_to_all | solution.py:294
  362.2 4.4 collective-permute-done.14
  368.3 4.2 all-to-all-start.12
  372.6 9.4 %all-to-all-done.12.g_ref = bf16[8,128,512]{2,1,0:T(8,128)(2,1)} async-done(((bf16[8,128,512]{2,1,0:T(8,128)(2,1)}), bf16[8,128,512]{2,1,0:T(8,128)(2,1)}, u32[]{:S(2)}, u32[]{:S(2)}) %all-to-all-start.12) | async-done | bytes 1048608 | tf_op jit(solution)/shard_map/all_to_all | solution.py:294
  383.8 9.7 %backward_layer.6 = (bf16[128,768]{1,0:T(8,128)(2,1)S(1)}, bf16[8,128,512]{2,1,0:T(8,128)(2,1)S(1)}) custom-call(s32[1]{0:T(128)} %bitcast.42.flag_ref, bf16[8,128,512]{2,1,0:T(8,128)(2,1)} %all-to-all-done.12.g_ref, bf16[1280,128]{1,0:T(8,128)(2,1)S(1)} %copy-done.25, bf16[1280,128]{1,0:T(8,128)(2,1)S(1)} %get-tuple-element.56.pack0_ref.pack1_ref, ...), custom_call_target="tpu_custom_call" | custom-call | flops 1342177280 | bytes 10485760 | tf_op jit(solution)/shard_map/backward_layer/pallas_call | solution.py:194
  393.5 13.5 %all_to_all.88 = bf16[8,128,512]{2,1,0:T(8,128)(2,1)S(1)} all-to-all(bf16[8,128,512]{2,1,0:T(8,128)(2,1)S(1)} %get-tuple-element.70), channel_id=1, replica_groups=mesh['dp'=4,'section'=4,'tensor'=8] {'tensor'}, dimensions={0} | all-to-all | bytes 2097152 | tf_op jit(solution)/shard_map/all_to_all | solution.py:294
  408.7 4.7 collective-permute-done.15
  415.1 4.2 all-to-all-start.14
  419.4 9.4 %all-to-all-done.14.g_ref = bf16[8,128,512]{2,1,0:T(8,128)(2,1)} async-done(((bf16[8,128,512]{2,1,0:T(8,128)(2,1)}), bf16[8,128,512]{2,1,0:T(8,128)(2,1)}, u32[]{:S(2)}, u32[]{:S(2)}) %all-to-all-start.14) | async-done | bytes 1048608 | tf_op jit(solution)/shard_map/all_to_all | solution.py:294
  431.9 9.7 %backward_layer.7 = (bf16[128,768]{1,0:T(8,128)(2,1)S(1)}, bf16[8,128,512]{2,1,0:T(8,128)(2,1)S(1)}) custom-call(s32[1]{0:T(128)} %bitcast.41.flag_ref, bf16[8,128,512]{2,1,0:T(8,128)(2,1)} %all-to-all-done.14.g_ref, bf16[1280,128]{1,0:T(8,128)(2,1)S(1)} %copy-done.23, bf16[1280,128]{1,0:T(8,128)(2,1)S(1)} %copy-done.29, bf16[8,128,512]{2,1,0:T(8,128)(2,1)S(1)} %copy-done.8, ...), custom_call_target="tpu_custom_call" | custom-call | flops 1342177280 | bytes 10485760 | tf_op jit(solution)/shard_map/backward_layer/pallas_call | solution.py:194
  441.6 13.5 %all_to_all.89 = bf16[8,128,512]{2,1,0:T(8,128)(2,1)S(1)} all-to-all(bf16[8,128,512]{2,1,0:T(8,128)(2,1)S(1)} %get-tuple-element.77), channel_id=1, replica_groups=mesh['dp'=4,'section'=4,'tensor'=8] {'tensor'}, dimensions={0} | all-to-all | bytes 2097152 | tf_op jit(solution)/shard_map/all_to_all | solution.py:294
  457.3 4.9 collective-permute-done.19
  464.1 4.5 all-to-all-start.16
  472.9 15.1 %collective-permute-start.23 = (bf16[128,512]{1,0:T(8,128)(2,1)}, bf16[128,512]{1,0:T(8,128)(2,1)S(1)}, u32[]{:S(2)}, u32[]{:S(2)}) collective-permute-start(bf16[128,512]{1,0:T(8,128)(2,1)} %get-tuple-element.86.refs_0_), channel_id=1, source_target_pairs={{0,32},{32,0},{64,96},{96,64},{1,33},{33,1},{65,97},{97,65},{2,34}... | collective-permute-start | bytes 393224 | tf_op jit(solution)/shard_map/ppermute | solution.py:290
  488.0 11.7 %collective-permute-start.24 = (bf16[128,512]{1,0:T(8,128)(2,1)}, bf16[128,512]{1,0:T(8,128)(2,1)S(1)}, u32[]{:S(2)}, u32[]{:S(2)}) collective-permute-start(bf16[128,512]{1,0:T(8,128)(2,1)} %get-tuple-element.86.refs_0_), channel_id=1, source_target_pairs={{0,64},{32,96},{64,0},{96,32},{1,65},{33,97},{65,1},{97,33},{2,66}... | collective-permute-start | bytes 393224 | tf_op jit(solution)/shard_map/ppermute | solution.py:290
  511.8 6.8 %backward_heads.1 = bf16[128,768]{1,0:T(8,128)(2,1)S(1)} custom-call(s32[1]{0:T(128)} %bitcast.43.flag_ref, bf16[8,128,512]{2,1,0:T(8,128)(2,1)} %all-to-all-done.16.g_ref, bf16[1280,128]{1,0:T(8,128)(2,1)S(1)} %copy-done.23, bf16[1280,128]{1,0:T(8,128)(2,1)S(1)} %copy-done.26, bf16[8,128,512]{2,1,0:T(8,128)(2,1)S(1)} %copy-done.9, ...), custom_call_target="tpu_custom_call" | custom-call | flops 1342177280 | bytes 10485760 | tf_op jit(solution)/shard_map/backward_heads/pallas_call | solution.py:194
  530.0 4.0 collective-permute-done.12.refs_6_
  536.0 4.1 collective-permute-done.13.refs_7_
  560.0 4.6 qkv_grad.1
  568.2 5.1 collective-permute-done.30.refs_10_
  573.3 5.7 collective-permute-done.31.refs_11_
  (310 shorter events, 175.1 us)
Async XLA Ops:
  9.1 3.0 collective-permute-start
  12.3 6.3 %collective-permute-start.1 = (bf16[128,512]{1,0:T(8,128)(2,1)S(1)}, bf16[128,512]{1,0:T(8,128)(2,1)S(1)}, u32[]{:S(2)}, u32[]{:S(2)}) collective-permute-start(bf16[128,512]{1,0:T(8,128)(2,1)S(1)} %get-tuple-element.113), channel_id=1, source_target_pairs={{0,64},{32,96},{64,0},{96,32},{1,65},{33,97},{65,1},{97,33},{2,66}... | collective-permute-start | bytes 393224 | tf_op jit(solution)/shard_map/ppermute | solution.py:290
  19.7 19.3 %all-to-all-start = ((bf16[8,128,512]{2,1,0:T(8,128)(2,1)}), bf16[8,128,512]{2,1,0:T(8,128)(2,1)S(1)}, u32[]{:S(2)}, u32[]{:S(2)}) async-start(bf16[8,128,512]{2,1,0:T(8,128)(2,1)} %broadcast_in_dim.156), calls=%async_computation | async-start | bytes 2097152 | tf_op jit(solution)/shard_map/all_to_all | solution.py:294
  49.5 19.5 %all-to-all-start.1 = ((bf16[8,128,512]{2,1,0:T(8,128)(2,1)}), bf16[8,128,512]{2,1,0:T(8,128)(2,1)S(1)}, u32[]{:S(2)}, u32[]{:S(2)}) async-start(bf16[8,128,512]{2,1,0:T(8,128)(2,1)} %copy-done.34), calls=%async_computation.1 | async-start | bytes 2097152 | tf_op jit(solution)/shard_map/all_to_all | solution.py:294
  54.0 18.7 %collective-permute-start.2 = (bf16[128,512]{1,0:T(8,128)(2,1)S(1)}, bf16[128,512]{1,0:T(8,128)(2,1)S(1)}, u32[]{:S(2)}, u32[]{:S(2)}) collective-permute-start(bf16[128,512]{1,0:T(8,128)(2,1)S(1)} %get-tuple-element.112), channel_id=1, source_target_pairs={{0,64},{32,96},{64,0},{96,32},{1,65},{33,97},{65,1},{97,33},{2,66}... | collective-permute-start | bytes 393224 | tf_op jit(solution)/shard_map/ppermute | solution.py:290
  69.2 5.5 collective-permute-start.3
  76.6 15.1 %all-to-all-start.2 = ((bf16[8,128,512]{2,1,0:T(8,128)(2,1)}), bf16[8,128,512]{2,1,0:T(8,128)(2,1)S(1)}, u32[]{:S(2)}, u32[]{:S(2)}) async-start(bf16[8,128,512]{2,1,0:T(8,128)(2,1)} %broadcast_in_dim.157), calls=%async_computation.2 | async-start | bytes 2097152 | tf_op jit(solution)/shard_map/all_to_all | solution.py:294
  119.7 5.8 collective-permute-start.4
  126.6 14.0 %all-to-all-start.4 = ((bf16[8,128,512]{2,1,0:T(8,128)(2,1)}), bf16[8,128,512]{2,1,0:T(8,128)(2,1)S(1)}, u32[]{:S(2)}, u32[]{:S(2)}) async-start(bf16[8,128,512]{2,1,0:T(8,128)(2,1)} %broadcast_in_dim.158), calls=%async_computation.4 | async-start | bytes 2097152 | tf_op jit(solution)/shard_map/all_to_all | solution.py:294
  168.1 5.7 collective-permute-start.5
  175.6 13.8 %all-to-all-start.6 = ((bf16[8,128,512]{2,1,0:T(8,128)(2,1)}), bf16[8,128,512]{2,1,0:T(8,128)(2,1)S(1)}, u32[]{:S(2)}, u32[]{:S(2)}) async-start(bf16[8,128,512]{2,1,0:T(8,128)(2,1)} %broadcast_in_dim.159), calls=%async_computation.6 | async-start | bytes 2097152 | tf_op jit(solution)/shard_map/all_to_all | solution.py:294
  205.1 24.4 %all-to-all-start.7 = ((bf16[8,160,512]{2,1,0:T(8,128)(2,1)}), bf16[8,160,512]{2,1,0:T(8,128)(2,1)}, u32[]{:S(2)}, u32[]{:S(2)}) async-start(bf16[8,160,512]{2,1,0:T(8,128)(2,1)} %pad_maximum_fusion), calls=%async_computation.7 | async-start | bytes 2621440 | tf_op jit(solution)/shard_map/all_to_all | solution.py:294
  213.0 40.6 %all-gather.2.cloned.1.call-start = ((), (), s32[]{:S(2)}) async-start(), calls=%async_computation.17 | async-start | bytes 1179648 | tf_op jit(solution)/shard_map/all_gather | solution.py:348
  234.7 21.0 %collective-permute-start.6 = (bf16[128,512]{1,0:T(8,128)(2,1)}, bf16[128,512]{1,0:T(8,128)(2,1)}, u32[]{:S(2)}, u32[]{:S(2)}) collective-permute-start(bf16[128,512]{1,0:T(8,128)(2,1)} %add_convert_fusion.3), channel_id=1, source_target_pairs={{0,8},{8,16},{16,24},{1,9},{9,17},{17,25},{2,10},{10,18},{18,26},{... | collective-permute-start | bytes 393224 | tf_op jit(solution)/shard_map/ppermute | solution.py:286
  257.7 20.1 %all-to-all-start.8 = ((bf16[8,128,512]{2,1,0:T(8,128)(2,1)}), bf16[8,128,512]{2,1,0:T(8,128)(2,1)}, u32[]{:S(2)}, u32[]{:S(2)}) async-start(bf16[8,128,512]{2,1,0:T(8,128)(2,1)} %broadcast_in_dim.162), calls=%async_computation.8 | async-start | bytes 2097152 | tf_op jit(solution)/shard_map/all_to_all | solution.py:294
  290.6 17.1 %all-to-all-start.9 = ((bf16[8,160,512]{2,1,0:T(8,128)(2,1)}), bf16[8,160,512]{2,1,0:T(8,128)(2,1)}, u32[]{:S(2)}, u32[]{:S(2)}) async-start(bf16[8,160,512]{2,1,0:T(8,128)(2,1)} %pad_maximum_fusion.1), calls=%async_computation.9 | async-start | bytes 2621440 | tf_op jit(solution)/shard_map/all_to_all | solution.py:294
  310.2 5.8 collective-permute-start.10
  317.0 16.3 %all-to-all-start.10 = ((bf16[8,128,512]{2,1,0:T(8,128)(2,1)}), bf16[8,128,512]{2,1,0:T(8,128)(2,1)}, u32[]{:S(2)}, u32[]{:S(2)}) async-start(bf16[8,128,512]{2,1,0:T(8,128)(2,1)} %broadcast_in_dim.165), calls=%async_computation.10 | async-start | bytes 2097152 | tf_op jit(solution)/shard_map/all_to_all | solution.py:294
  360.9 5.7 collective-permute-start.14
  368.3 13.7 %all-to-all-start.12 = ((bf16[8,128,512]{2,1,0:T(8,128)(2,1)}), bf16[8,128,512]{2,1,0:T(8,128)(2,1)}, u32[]{:S(2)}, u32[]{:S(2)}) async-start(bf16[8,128,512]{2,1,0:T(8,128)(2,1)} %broadcast_in_dim.166), calls=%async_computation.12 | async-start | bytes 2097152 | tf_op jit(solution)/shard_map/all_to_all | solution.py:294
  407.3 6.1 %collective-permute-start.15 = (bf16[128,512]{1,0:T(8,128)(2,1)S(1)}, bf16[128,512]{1,0:T(8,128)(2,1)S(1)}, u32[]{:S(2)}, u32[]{:S(2)}) collective-permute-start(bf16[128,512]{1,0:T(8,128)(2,1)S(1)} %add_convert_fusion.1), channel_id=1, source_target_pairs={{8,0},{16,8},{24,16},{9,1},{17,9},{25,17},{10,2},{18,10},{26,18},{... | collective-permute-start | bytes 393224 | tf_op jit(solution)/shard_map/ppermute | solution.py:286
  415.1 13.7 %all-to-all-start.14 = ((bf16[8,128,512]{2,1,0:T(8,128)(2,1)}), bf16[8,128,512]{2,1,0:T(8,128)(2,1)}, u32[]{:S(2)}, u32[]{:S(2)}) async-start(bf16[8,128,512]{2,1,0:T(8,128)(2,1)} %broadcast_in_dim.167), calls=%async_computation.14 | async-start | bytes 2097152 | tf_op jit(solution)/shard_map/all_to_all | solution.py:294
  456.0 6.2 %collective-permute-start.19 = (bf16[128,512]{1,0:T(8,128)(2,1)}, bf16[128,512]{1,0:T(8,128)(2,1)}, u32[]{:S(2)}, u32[]{:S(2)}) collective-permute-start(bf16[128,512]{1,0:T(8,128)(2,1)} %add_convert_fusion), channel_id=1, source_target_pairs={{8,0},{16,8},{24,16},{9,1},{17,9},{25,17},{10,2},{18,10},{26,18},{... | collective-permute-start | bytes 393224 | tf_op jit(solution)/shard_map/ppermute | solution.py:286
  464.1 44.8 %all-to-all-start.16 = ((bf16[8,128,512]{2,1,0:T(8,128)(2,1)}), bf16[8,128,512]{2,1,0:T(8,128)(2,1)}, u32[]{:S(2)}, u32[]{:S(2)}) async-start(bf16[8,128,512]{2,1,0:T(8,128)(2,1)} %broadcast_in_dim.168), calls=%async_computation.16 | async-start | bytes 2097152 | tf_op jit(solution)/shard_map/all_to_all | solution.py:294
  472.9 32.1 %collective-permute-start.23 = (bf16[128,512]{1,0:T(8,128)(2,1)}, bf16[128,512]{1,0:T(8,128)(2,1)S(1)}, u32[]{:S(2)}, u32[]{:S(2)}) collective-permute-start(bf16[128,512]{1,0:T(8,128)(2,1)} %get-tuple-element.86.refs_0_), channel_id=1, source_target_pairs={{0,32},{32,0},{64,96},{96,64},{1,33},{33,1},{65,97},{97,65},{2,34}... | collective-permute-start | bytes 393224 | tf_op jit(solution)/shard_map/ppermute | solution.py:290
  488.0 18.0 %collective-permute-start.24 = (bf16[128,512]{1,0:T(8,128)(2,1)}, bf16[128,512]{1,0:T(8,128)(2,1)S(1)}, u32[]{:S(2)}, u32[]{:S(2)}) collective-permute-start(bf16[128,512]{1,0:T(8,128)(2,1)} %get-tuple-element.86.refs_0_), channel_id=1, source_target_pairs={{0,64},{32,96},{64,0},{96,32},{1,65},{33,97},{65,1},{97,33},{2,66}... | collective-permute-start | bytes 393224 | tf_op jit(solution)/shard_map/ppermute | solution.py:290
  499.7 19.0 %collective-permute-start.25 = (bf16[128,512]{1,0:T(8,128)(2,1)}, bf16[128,512]{1,0:T(8,128)(2,1)}, u32[]{:S(2)}, u32[]{:S(2)}) collective-permute-start(bf16[128,512]{1,0:T(8,128)(2,1)} %get-tuple-element.86.refs_0_), channel_id=1, source_target_pairs={{0,96},{32,64},{64,32},{96,0},{1,97},{33,65},{65,33},{97,1},{2,98}... | collective-permute-start | bytes 393224 | tf_op jit(solution)/shard_map/ppermute | solution.py:290
  500.7 18.8 %collective-permute-start.7 = (bf16[2,128,512]{2,1,0:T(8,128)(2,1)}, bf16[2,128,512]{2,1,0:T(8,128)(2,1)}, u32[]{:S(2)}, u32[]{:S(2)}) collective-permute-start(bf16[2,128,512]{2,1,0:T(8,128)(2,1)} %get-tuple-element.108), channel_id=1, source_target_pairs={{0,32},{32,0},{64,96},{96,64},{1,33},{33,1},{65,97},{97,65},{2,34}... | collective-permute-start | bytes 786440 | tf_op jit(solution)/shard_map/ppermute | solution.py:290
  501.1 20.8 %collective-permute-start.8 = (bf16[2,128,512]{2,1,0:T(8,128)(2,1)}, bf16[2,128,512]{2,1,0:T(8,128)(2,1)}, u32[]{:S(2)}, u32[]{:S(2)}) collective-permute-start(bf16[2,128,512]{2,1,0:T(8,128)(2,1)} %get-tuple-element.107), channel_id=1, source_target_pairs={{0,64},{32,96},{64,0},{96,32},{1,65},{33,97},{65,1},{97,33},{2,66}... | collective-permute-start | bytes 786440 | tf_op jit(solution)/shard_map/ppermute | solution.py:290
  505.7 16.4 %collective-permute-start.9 = (bf16[2,128,512]{2,1,0:T(8,128)(2,1)}, bf16[2,128,512]{2,1,0:T(8,128)(2,1)}, u32[]{:S(2)}, u32[]{:S(2)}) collective-permute-start(bf16[2,128,512]{2,1,0:T(8,128)(2,1)} %get-tuple-element.106), channel_id=1, source_target_pairs={{0,96},{32,64},{64,32},{96,0},{1,97},{33,65},{65,33},{97,1},{2,98}... | collective-permute-start | bytes 786440 | tf_op jit(solution)/shard_map/ppermute | solution.py:290
  506.7 16.6 %collective-permute-start.26 = (bf16[128,512]{1,0:T(8,128)(2,1)}, bf16[128,512]{1,0:T(8,128)(2,1)}, u32[]{:S(2)}, u32[]{:S(2)}) collective-permute-start(bf16[128,512]{1,0:T(8,128)(2,1)} %get-tuple-element.88.refs_4_), channel_id=1, source_target_pairs={{0,32},{32,0},{64,96},{96,64},{1,33},{33,1},{65,97},{97,65},{2,34}... | collective-permute-start | bytes 393224 | tf_op jit(solution)/shard_map/ppermute | solution.py:290
  518.6 7.0 %collective-permute-start.27 = (bf16[128,512]{1,0:T(8,128)(2,1)}, bf16[128,512]{1,0:T(8,128)(2,1)S(1)}, u32[]{:S(2)}, u32[]{:S(2)}) collective-permute-start(bf16[128,512]{1,0:T(8,128)(2,1)} %get-tuple-element.88.refs_4_), channel_id=1, source_target_pairs={{0,64},{32,96},{64,0},{96,32},{1,65},{33,97},{65,1},{97,33},{2,66}... | collective-permute-start | bytes 393224 | tf_op jit(solution)/shard_map/ppermute | solution.py:290
  519.6 9.3 %collective-permute-start.28 = (bf16[128,512]{1,0:T(8,128)(2,1)}, bf16[128,512]{1,0:T(8,128)(2,1)S(1)}, u32[]{:S(2)}, u32[]{:S(2)}) collective-permute-start(bf16[128,512]{1,0:T(8,128)(2,1)} %get-tuple-element.88.refs_4_), channel_id=1, source_target_pairs={{0,96},{32,64},{64,32},{96,0},{1,97},{33,65},{65,33},{97,1},{2,98}... | collective-permute-start | bytes 393224 | tf_op jit(solution)/shard_map/ppermute | solution.py:290
  521.9 8.0 %collective-permute-start.11 = (bf16[2,128,512]{2,1,0:T(8,128)(2,1)S(1)}, bf16[2,128,512]{2,1,0:T(8,128)(2,1)S(1)}, u32[]{:S(2)}, u32[]{:S(2)}) collective-permute-start(bf16[2,128,512]{2,1,0:T(8,128)(2,1)S(1)} %copy-done.74), channel_id=1, source_target_pairs={{0,32},{32,0},{64,96},{96,64},{1,33},{33,1},{65,97},{97,65},{2,34}... | collective-permute-start | bytes 786440 | tf_op jit(solution)/shard_map/ppermute | solution.py:290
  522.1 11.9 %collective-permute-start.12 = (bf16[2,128,512]{2,1,0:T(8,128)(2,1)S(1)}, bf16[2,128,512]{2,1,0:T(8,128)(2,1)S(1)}, u32[]{:S(2)}, u32[]{:S(2)}) collective-permute-start(bf16[2,128,512]{2,1,0:T(8,128)(2,1)S(1)} %copy-done.73), channel_id=1, source_target_pairs={{0,64},{32,96},{64,0},{96,32},{1,65},{33,97},{65,1},{97,33},{2,66}... | collective-permute-start | bytes 786440 | tf_op jit(solution)/shard_map/ppermute | solution.py:290
  523.3 16.8 %collective-permute-start.13 = (bf16[2,128,512]{2,1,0:T(8,128)(2,1)S(1)}, bf16[2,128,512]{2,1,0:T(8,128)(2,1)S(1)}, u32[]{:S(2)}, u32[]{:S(2)}) collective-permute-start(bf16[2,128,512]{2,1,0:T(8,128)(2,1)S(1)} %copy-done.72), channel_id=1, source_target_pairs={{0,96},{32,64},{64,32},{96,0},{1,97},{33,65},{65,33},{97,1},{2,98}... | collective-permute-start | bytes 786440 | tf_op jit(solution)/shard_map/ppermute | solution.py:290
  525.6 14.5 %collective-permute-start.16 = (bf16[128,768]{1,0:T(8,128)(2,1)S(1)}, bf16[128,768]{1,0:T(8,128)(2,1)S(1)}, u32[]{:S(2)}, u32[]{:S(2)}) collective-permute-start(bf16[128,768]{1,0:T(8,128)(2,1)S(1)} %get-tuple-element.78.refs_8_), channel_id=1, source_target_pairs={{0,32},{32,0},{64,96},{96,64},{1,33},{33,1},{65,97},{97,65},{2,34}... | collective-permute-start | bytes 589832 | tf_op jit(solution)/shard_map/ppermute | solution.py:290
  528.9 14.9 %collective-permute-start.17 = (bf16[128,768]{1,0:T(8,128)(2,1)S(1)}, bf16[128,768]{1,0:T(8,128)(2,1)S(1)}, u32[]{:S(2)}, u32[]{:S(2)}) collective-permute-start(bf16[128,768]{1,0:T(8,128)(2,1)S(1)} %get-tuple-element.78.refs_8_), channel_id=1, source_target_pairs={{0,64},{32,96},{64,0},{96,32},{1,65},{33,97},{65,1},{97,33},{2,66}... | collective-permute-start | bytes 589832 | tf_op jit(solution)/shard_map/ppermute | solution.py:290
  529.9 28.0 %collective-permute-start.32 = (bf16[2,128,512]{2,1,0:T(8,128)(2,1)S(1)}, bf16[2,128,512]{2,1,0:T(8,128)(2,1)S(1)}, u32[]{:S(2)}, u32[]{:S(2)}) collective-permute-start(bf16[2,128,512]{2,1,0:T(8,128)(2,1)S(1)} %get-tuple-element.96), channel_id=1, source_target_pairs={{0,32},{32,0},{64,96},{96,64},{1,33},{33,1},{65,97},{97,65},{2,34}... | collective-permute-start | bytes 786440 | tf_op jit(solution)/shard_map/ppermute | solution.py:290
  534.0 14.5 %collective-permute-start.18 = (bf16[128,768]{1,0:T(8,128)(2,1)S(1)}, bf16[128,768]{1,0:T(8,128)(2,1)S(1)}, u32[]{:S(2)}, u32[]{:S(2)}) collective-permute-start(bf16[128,768]{1,0:T(8,128)(2,1)S(1)} %get-tuple-element.78.refs_8_), channel_id=1, source_target_pairs={{0,96},{32,64},{64,32},{96,0},{1,97},{33,65},{65,33},{97,1},{2,98}... | collective-permute-start | bytes 589832 | tf_op jit(solution)/shard_map/ppermute | solution.py:290
  540.1 9.3 %collective-permute-start.20 = (bf16[128,768]{1,0:T(8,128)(2,1)S(1)}, bf16[128,768]{1,0:T(8,128)(2,1)S(1)}, u32[]{:S(2)}, u32[]{:S(2)}) collective-permute-start(bf16[128,768]{1,0:T(8,128)(2,1)S(1)} %get-tuple-element.110.refs_12_), channel_id=1, source_target_pairs={{0,32},{32,0},{64,96},{96,64},{1,33},{33,1},{65,97},{97,65},{2,34}... | collective-permute-start | bytes 589832 | tf_op jit(solution)/shard_map/ppermute | solution.py:290
  540.1 12.1 %collective-permute-start.21 = (bf16[128,768]{1,0:T(8,128)(2,1)S(1)}, bf16[128,768]{1,0:T(8,128)(2,1)S(1)}, u32[]{:S(2)}, u32[]{:S(2)}) collective-permute-start(bf16[128,768]{1,0:T(8,128)(2,1)S(1)} %get-tuple-element.110.refs_12_), channel_id=1, source_target_pairs={{0,64},{32,96},{64,0},{96,32},{1,65},{33,97},{65,1},{97,33},{2,66}... | collective-permute-start | bytes 589832 | tf_op jit(solution)/shard_map/ppermute | solution.py:290
  543.8 13.1 %collective-permute-start.22 = (bf16[128,768]{1,0:T(8,128)(2,1)S(1)}, bf16[128,768]{1,0:T(8,128)(2,1)S(1)}, u32[]{:S(2)}, u32[]{:S(2)}) collective-permute-start(bf16[128,768]{1,0:T(8,128)(2,1)S(1)} %get-tuple-element.110.refs_12_), channel_id=1, source_target_pairs={{0,96},{32,64},{64,32},{96,0},{1,97},{33,65},{65,33},{97,1},{2,98}... | collective-permute-start | bytes 589832 | tf_op jit(solution)/shard_map/ppermute | solution.py:290
  548.5 16.1 %collective-permute-start.33 = (bf16[2,128,512]{2,1,0:T(8,128)(2,1)S(1)}, bf16[2,128,512]{2,1,0:T(8,128)(2,1)S(1)}, u32[]{:S(2)}, u32[]{:S(2)}) collective-permute-start(bf16[2,128,512]{2,1,0:T(8,128)(2,1)S(1)} %get-tuple-element.95), channel_id=1, source_target_pairs={{0,64},{32,96},{64,0},{96,32},{1,65},{33,97},{65,1},{97,33},{2,66}... | collective-permute-start | bytes 786440 | tf_op jit(solution)/shard_map/ppermute | solution.py:290
  549.4 18.7 %collective-permute-start.34 = (bf16[2,128,512]{2,1,0:T(8,128)(2,1)S(1)}, bf16[2,128,512]{2,1,0:T(8,128)(2,1)S(1)}, u32[]{:S(2)}, u32[]{:S(2)}) collective-permute-start(bf16[2,128,512]{2,1,0:T(8,128)(2,1)S(1)} %get-tuple-element.94), channel_id=1, source_target_pairs={{0,96},{32,64},{64,32},{96,0},{1,97},{33,65},{65,33},{97,1},{2,98}... | collective-permute-start | bytes 786440 | tf_op jit(solution)/shard_map/ppermute | solution.py:290
  552.2 16.0 %collective-permute-start.29 = (bf16[2,128,512]{2,1,0:T(8,128)(2,1)S(1)}, bf16[2,128,512]{2,1,0:T(8,128)(2,1)S(1)}, u32[]{:S(2)}, u32[]{:S(2)}) collective-permute-start(bf16[2,128,512]{2,1,0:T(8,128)(2,1)S(1)} %get-tuple-element.100), channel_id=1, source_target_pairs={{0,32},{32,0},{64,96},{96,64},{1,33},{33,1},{65,97},{97,65},{2,34}... | collective-permute-start | bytes 786440 | tf_op jit(solution)/shard_map/ppermute | solution.py:290
  557.0 16.4 %collective-permute-start.30 = (bf16[2,128,512]{2,1,0:T(8,128)(2,1)S(1)}, bf16[2,128,512]{2,1,0:T(8,128)(2,1)S(1)}, u32[]{:S(2)}, u32[]{:S(2)}) collective-permute-start(bf16[2,128,512]{2,1,0:T(8,128)(2,1)S(1)} %get-tuple-element.99), channel_id=1, source_target_pairs={{0,64},{32,96},{64,0},{96,32},{1,65},{33,97},{65,1},{97,33},{2,66}... | collective-permute-start | bytes 786440 | tf_op jit(solution)/shard_map/ppermute | solution.py:290
  557.9 21.2 %collective-permute-start.31 = (bf16[2,128,512]{2,1,0:T(8,128)(2,1)S(1)}, bf16[2,128,512]{2,1,0:T(8,128)(2,1)S(1)}, u32[]{:S(2)}, u32[]{:S(2)}) collective-permute-start(bf16[2,128,512]{2,1,0:T(8,128)(2,1)S(1)} %get-tuple-element.98), channel_id=1, source_target_pairs={{0,96},{32,64},{64,32},{96,0},{1,97},{33,65},{65,33},{97,1},{2,98}... | collective-permute-start | bytes 786440 | tf_op jit(solution)/shard_map/ppermute | solution.py:290
  (80 other events, 846.3 us)
Sparse Core Ops, SparseCore 0:
  215.4 38.0 all-gather.1

commit v3 on v2

--- a/solution.py
+++ b/solution.py
@@ -13,7 +13,8 @@
 SCORE_SCALE = 1.0 / HEAD_DIM**0.5
 F32 = jnp.float32
 BF16 = jnp.bfloat16
-VMEM_LIMIT = 48 * 1024 * 1024
+SMALL_VMEM = 16 * 1024 * 1024
+LARGE_VMEM = 48 * 1024 * 1024
 
 
 def dot(a, b):
@@ -36,17 +37,56 @@
     return pl.BlockSpec(memory_space=pltpu.SMEM)
 
 
-def anywhere():
-    return pl.BlockSpec(memory_space=pl.ANY)
-
-
-def kernel_params():
-    return pltpu.CompilerParams(vmem_limit_bytes=VMEM_LIMIT)
-
-
-def forward_kernel(len_ref, x_ref, wq_ref, wk_ref, wv_ref, wo_ref, part_ref, h_ref, scale_ref, pack_ref, o_ref):
+def in_hbm():
+    return pl.BlockSpec(memory_space=pltpu.HBM)
+
+
+def kernel_params(limit):
+    return pltpu.CompilerParams(vmem_limit_bytes=limit)
+
+
+def weight_scratch(wq, wk, wv, wo):
+    return [pltpu.VMEM(w.shape, BF16) for w in (wq, wk, wv, wo)]
+
+
+def weight_copies(hbm, vmem, sems, out_first):
+    wq, wk, wv, wo = zip(hbm, vmem)
+    qkv, out = [], []
+    step = wq[0].shape[0] // 4
+    for n in range(4):
+        rows = pl.ds(n * step, step)
+        qkv.append(
+            [
+                pltpu.make_async_copy(one.at[rows, :], to.at[rows, :], sems.at[0, n, at])
+                for at, (one, to) in enumerate((wq, wk, wv))
+            ]
+        )
+        out.append(
+            [pltpu.make_async_copy(wo[0].at[:, rows], wo[1].at[:, rows], sems.at[1, n, 0])]
+        )
+    for part in (out + qkv) if out_first else (qkv + out):
+        for copy in part:
+            copy.start()
+    return qkv, out
+
+
+def arrived(copies):
+    for copy in copies:
+        copy.wait()
+
+
+def forward_kernel(resident, len_ref, x_ref, wq_in, wk_in, wv_in, wo_in, *rest):
+    part_ref, h_ref, scale_ref, pack_ref, o_ref = rest[:5]
     nblk, rows, dsh = x_ref.shape
-    qh = wq_ref.shape[1] // HEAD_DIM
+    qh = wq_in.shape[1] // HEAD_DIM
+    if resident:
+        wq_ref, wk_ref, wv_ref, wo_ref = wq_in, wk_in, wv_in, wo_in
+        qkv = out = [()] * 4
+    else:
+        wq_ref, wk_ref, wv_ref, wo_ref, sems = rest[5:]
+        qkv, out = weight_copies(
+            (wq_in, wk_in, wv_in, wo_in), (wq_ref, wk_ref, wv_ref, wo_ref), sems, False
+        )
     sq = jnp.zeros((rows, 1), F32)
     for j in range(nblk):
         xf = x_ref[j].astype(F32)
@@ -59,6 +99,8 @@
     for j in range(nblk):
         h = (x_ref[j].astype(F32) * scale).astype(BF16)
         h_ref[j] = h
+        if j % (nblk // 4) == 0:
+            arrived(qkv[j // (nblk // 4)])
         at = pl.ds(j * dsh, dsh)
         q = q + dot(h, wq_ref[at, :])
         k = k + dot(h, wk_ref[at, :])
@@ -81,25 +123,25 @@
         o_ref[:, pl.ds(n * HEAD_DIM, HEAD_DIM)] = dot(weights, v).astype(BF16)
     o = o_ref[...]
     for j in range(nblk):
+        if j % (nblk // 4) == 0:
+            arrived(out[j // (nblk // 4)])
         part_ref[j] = dot(o, wo_ref[:, pl.ds(j * dsh, dsh)]).astype(BF16)
 
 
-def forward(length, x, wq, wk, wv, wo):
+def forward(length, x, wq, wk, wv, wo, resident):
     nblk, rows, dsh = x.shape
     qcol = wq.shape[1]
     packed = 2 * qcol // HEAD_DIM * rows + 2 * rows
+    outs = [(x.shape, BF16), (x.shape, BF16)]
+    outs += [((rows, HEAD_DIM), F32), ((packed, HEAD_DIM), BF16), ((rows, qcol), BF16)]
+    own = weight_scratch(wq, wk, wv, wo) + [pltpu.SemaphoreType.DMA((2, 4, 3))]
     out = pl.pallas_call(
-        forward_kernel,
-        out_shape=(
-            jax.ShapeDtypeStruct(x.shape, BF16),
-            jax.ShapeDtypeStruct(x.shape, BF16),
-            jax.ShapeDtypeStruct((rows, HEAD_DIM), F32),
-            jax.ShapeDtypeStruct((packed, HEAD_DIM), BF16),
-            jax.ShapeDtypeStruct((rows, qcol), BF16),
-        ),
-        in_specs=[in_smem()] + [in_vmem()] * 5,
+        functools.partial(forward_kernel, resident),
+        out_shape=tuple(jax.ShapeDtypeStruct(*one) for one in outs),
+        in_specs=[in_smem(), in_vmem()] + [in_vmem() if resident else in_hbm()] * 4,
         out_specs=tuple([in_vmem()] * 5),
-        compiler_params=kernel_params(),
+        scratch_shapes=[] if resident else own,
+        compiler_params=kernel_params(SMALL_VMEM if resident else LARGE_VMEM),
         cost_estimate=pl.CostEstimate(
             flops=2 * rows * nblk * dsh * (2 * qcol + 2 * HEAD_DIM),
             bytes_accessed=4 * nblk * dsh * (qcol + HEAD_DIM),
@@ -112,16 +154,29 @@
 
 def backward_kernel(
     with_input, flag_ref, g_ref, pack0_ref, pack1_ref, h0_ref, h1_ref, scale0_ref, scale1_ref,
-    wq_ref, wk_ref, wv_ref, wo_ref, *rest
+    wq_any, wk_any, wv_any, wo_any, *rest
 ):
     if with_input:
-        d_ref, dx_ref, pack_ref, h_ref, scale_ref, dh_ref, sems = rest
+        d_ref, dx_ref, wq_ref, wk_ref, wv_ref, wo_ref, pack_ref, sems, keep_sems = rest[:9]
+        h_ref, scale_ref, dh_ref = rest[9:]
     else:
-        d_ref, pack_ref, sems = rest
+        d_ref, wo_ref, pack_ref, sems, keep_sems = rest
     nblk, rows, dsh = g_ref.shape
-    qcol = wq_ref.shape[1]
+    qcol = wq_any.shape[1]
     qh = qcol // HEAD_DIM
     top = qh * rows
+    if with_input:
+        qkv, out = weight_copies(
+            (wq_any, wk_any, wv_any, wo_any), (wq_ref, wk_ref, wv_ref, wo_ref), sems, True
+        )
+    else:
+        step = nblk * dsh // 4
+        out = []
+        for n in range(4):
+            cols = pl.ds(n * step, step)
+            copy = pltpu.make_async_copy(wo_any.at[:, cols], wo_ref.at[:, cols], sems.at[1, n, 0])
+            copy.start()
+            out.append([copy])
     pairs = [(pack0_ref, pack1_ref, pack_ref)]
     if with_input:
         pairs += [(h0_ref, h1_ref, h_ref), (scale0_ref, scale1_ref, scale_ref)]
@@ -129,17 +184,19 @@
 
         @pl.when(flag_ref[0] == 0)
         def _(one=one, to=to, at=at):
-            pltpu.make_async_copy(one, to, sems.at[at]).start()
+            pltpu.make_async_copy(one, to, keep_sems.at[at]).start()
 
         @pl.when(flag_ref[0] != 0)
         def _(two=two, to=to, at=at):
-            pltpu.make_async_copy(two, to, sems.at[at]).start()
+            pltpu.make_async_copy(two, to, keep_sems.at[at]).start()
 
     do = jnp.zeros((rows, qcol), F32)
     for j in range(nblk):
+        if j % (nblk // 4) == 0:
+            arrived(out[j // (nblk // 4)])
         do = do + dot_nt(g_ref[j], wo_ref[:, pl.ds(j * dsh, dsh)])
     do = do.astype(BF16)
-    pltpu.make_async_copy(pack0_ref, pack_ref, sems.at[0]).wait()
+    pltpu.make_async_copy(pack0_ref, pack_ref, keep_sems.at[0]).wait()
     k = pack_ref[pl.ds(2 * top, rows), :]
     v = pack_ref[pl.ds(2 * top + rows, rows), :]
     dk = jnp.zeros((rows, HEAD_DIM), F32)
@@ -160,13 +217,15 @@
     d_ref[:, qcol + HEAD_DIM :] = dv.astype(BF16)
     if not with_input:
         return
-    pltpu.make_async_copy(h0_ref, h_ref, sems.at[1]).wait()
-    pltpu.make_async_copy(scale0_ref, scale_ref, sems.at[2]).wait()
+    pltpu.make_async_copy(h0_ref, h_ref, keep_sems.at[1]).wait()
+    pltpu.make_async_copy(scale0_ref, scale_ref, keep_sems.at[2]).wait()
     dq = d_ref[:, :qcol]
     dk = dk.astype(BF16)
     dv = dv.astype(BF16)
     inner = jnp.zeros((rows, 1), F32)
     for j in range(nblk):
+        if j % (nblk // 4) == 0:
+            arrived(qkv[j // (nblk // 4)])
         at = pl.ds(j * dsh, dsh)
         dh = dot_nt(dq, wq_ref[at, :]) + dot_nt(dk, wk_ref[at, :]) + dot_nt(dv, wv_ref[at, :])
         dh_ref[j] = dh
@@ -182,7 +241,12 @@
     wq, wk, wv, wo = weights
     qcol = wq.shape[1]
     out_shape = [jax.ShapeDtypeStruct((rows, qcol + 2 * HEAD_DIM), BF16)]
-    scratch = [pltpu.VMEM(one["pack"].shape, BF16)]
+    scratch = weight_scratch(*weights) if with_input else [pltpu.VMEM(wo.shape, BF16)]
+    scratch += [
+        pltpu.VMEM(one["pack"].shape, BF16),
+        pltpu.SemaphoreType.DMA((2, 4, 3)),
+        pltpu.SemaphoreType.DMA((3,)),
+    ]
     if with_input:
         out_shape.append(jax.ShapeDtypeStruct(g.shape, BF16))
         scratch += [
@@ -190,14 +254,13 @@
             pltpu.VMEM(one["scale"].shape, F32),
             pltpu.VMEM(g.shape, F32),
         ]
-    scratch.append(pltpu.SemaphoreType.DMA((3,)))
     return pl.pallas_call(
         functools.partial(backward_kernel, with_input),
         out_shape=tuple(out_shape),
-        in_specs=[in_smem(), in_vmem()] + [anywhere()] * 6 + [in_vmem()] * 4,
+        in_specs=[in_smem(), in_vmem()] + [in_hbm()] * 10,
         out_specs=tuple([in_vmem()] * len(out_shape)),
         scratch_shapes=scratch,
-        compiler_params=kernel_params(),
+        compiler_params=kernel_params(LARGE_VMEM),
         cost_estimate=pl.CostEstimate(
             flops=2 * rows * nblk * dsh * (2 * qcol + 2 * HEAD_DIM),
             bytes_accessed=4 * nblk * dsh * (qcol + HEAD_DIM),
@@ -210,74 +273,56 @@
     )
 
 
-def qkv_grad_kernel(n, *refs):
-    h_refs, d_refs = refs[:n], refs[n : 2 * n]
-    gq_ref, gk_ref, gv_ref, h_all, d_all = refs[2 * n :]
-    rows = d_refs[0].shape[0]
-    nblk, _, dsh = h_refs[0].shape
-    qcol = gq_ref.shape[1]
+def rows_grad_kernel(n, splits, with_total, *refs):
+    a_refs, b_refs, refs = refs[:n], refs[n : 2 * n], refs[2 * n :]
+    totals, refs = (refs[: len(splits)], refs[len(splits) :]) if with_total else ((), refs)
+    outs, (a_all, b_all) = refs[: len(splits)], refs[len(splits) :]
+    rows = a_refs[0].shape[-2]
+
+    def place(to, piece, i):
+        at = pl.ds(i * rows, rows)
+        if len(piece.shape) == 2:
+            to[at, :] = piece[...]
+        else:
+            for b in range(piece.shape[0]):
+                to[at, pl.ds(b * piece.shape[2], piece.shape[2])] = piece[b]
+
     for i in range(n):
-        at = pl.ds(i * rows, rows)
-        d_all[at, :] = d_refs[i][...]
-        for b in range(nblk):
-            h_all[at, pl.ds(b * dsh, dsh)] = h_refs[i][b]
-    for c in range(nblk * dsh // 256):
+        place(a_all, a_refs[i], i)
+        place(b_all, b_refs[i], i)
+    for c in range(a_all.shape[1] // 256):
         cols = pl.ds(c * 256, 256)
-        got = dot_tn(h_all[:, cols], d_all[...])
-        gq_ref[cols, :] = got[:, :qcol]
-        gk_ref[cols, :] = got[:, qcol : qcol + HEAD_DIM]
-        gv_ref[cols, :] = got[:, qcol + HEAD_DIM :]
-
-
-def qkv_grad(h, d):
-    n = len(h)
-    rows, dcol = d[0].shape
-    nblk, _, dsh = h[0].shape
-    width = nblk * dsh
+        got = dot_tn(a_all[:, cols], b_all[...])
+        for i, (start, stop) in enumerate(splits):
+            part = got[:, start:stop]
+            outs[i][cols, :] = totals[i][cols, :] + part if with_total else part
+
+
+def rows_grad(a, b, widths, totals=()):
+    n = len(a)
+    wide = lambda x: x.shape[-1] * (x.shape[0] if x.ndim == 3 else 1)
+    rows = a[0].shape[-2]
+    splits, at = [], 0
+    for w in widths:
+        splits.append((at, at + w))
+        at += w
     return pl.pallas_call(
-        functools.partial(qkv_grad_kernel, n),
-        out_shape=(
-            jax.ShapeDtypeStruct((width, dcol - 2 * HEAD_DIM), F32),
-            jax.ShapeDtypeStruct((width, HEAD_DIM), F32),
-            jax.ShapeDtypeStruct((width, HEAD_DIM), F32),
+        functools.partial(rows_grad_kernel, n, splits, bool(totals)),
+        out_shape=tuple(jax.ShapeDtypeStruct((wide(a[0]), w), F32) for w in widths),
+        in_specs=[in_vmem()] * (2 * n + len(totals)),
+        out_specs=tuple([in_vmem()] * len(widths)),
+        scratch_shapes=[
+            pltpu.VMEM((n * rows, wide(a[0])), BF16),
+            pltpu.VMEM((n * rows, wide(b[0])), BF16),
+        ],
+        compiler_params=kernel_params(LARGE_VMEM),
+        cost_estimate=pl.CostEstimate(
+            flops=2 * n * rows * wide(a[0]) * wide(b[0]),
+            bytes_accessed=4 * wide(a[0]) * wide(b[0]),
+            transcendentals=0,
         ),
-        in_specs=[in_vmem()] * (2 * n),
-        out_specs=tuple([in_vmem()] * 3),
-        scratch_shapes=[pltpu.VMEM((n * rows, width), BF16), pltpu.VMEM((n * rows, dcol), BF16)],
-        compiler_params=kernel_params(),
-        name="qkv_grad",
-    )(*h, *d)
-
-
-def out_grad_kernel(n, *refs):
-    o_refs, g_refs = refs[:n], refs[n : 2 * n]
-    go_ref, o_all, g_all = refs[2 * n :]
-    rows, qcol = o_refs[0].shape
-    nblk, _, dsh = g_refs[0].shape
-    for i in range(n):
-        at = pl.ds(i * rows, rows)
-        o_all[at, :] = o_refs[i][...]
-        for b in range(nblk):
-            g_all[at, pl.ds(b * dsh, dsh)] = g_refs[i][b]
-    for c in range(qcol // 256):
-        cols = pl.ds(c * 256, 256)
-        go_ref[cols, :] = dot_tn(o_all[:, cols], g_all[...])
-
-
-def out_grad(o, g):
-    n = len(o)
-    rows, qcol = o[0].shape
-    nblk, _, dsh = g[0].shape
-    width = nblk * dsh
-    return pl.pallas_call(
-        functools.partial(out_grad_kernel, n),
-        out_shape=jax.ShapeDtypeStruct((qcol, width), F32),
-        in_specs=[in_vmem()] * (2 * n),
-        out_specs=in_vmem(),
-        scratch_shapes=[pltpu.VMEM((n * rows, qcol), BF16), pltpu.VMEM((n * rows, width), BF16)],
-        compiler_params=kernel_params(),
-        name="out_grad",
-    )(*o, *g)
+        name="weight_grad",
+    )(*a, *b, *totals)
 
 
 def passed_along(x, axis, by):
@@ -288,6 +333,13 @@
 
 def swapped(x, axis, mask):
     return lax.ppermute(x, axis, [(i, i ^ mask) for i in range(lax.axis_size(axis))])
+
+
+def mirrored(x, mask):
+    ndp, peers = lax.axis_size("dp"), lax.axis_size("tensor")
+    to = lambda p, r: (p ^ mask) * peers + (r + peers // 2) % peers
+    pairs = [(p * peers + r, to(p, r)) for p in range(ndp) for r in range(peers)]
+    return lax.ppermute(x, ("dp", "tensor"), pairs)
 
 
 def exchange(blocks):
@@ -315,17 +367,6 @@
     return drows.astype(BF16)
 
 
-def among_replicas(x):
-    return [x] + [swapped(x, "dp", k) for k in (1, 2, 3)]
-
-
-def quarters_among_replicas(x, mine_rep):
-    ndp = lax.axis_size("dp")
-    size = x.shape[0] // ndp
-    take = lambda who: lax.dynamic_slice_in_dim(x, who * size, size, axis=0)
-    return [take(mine_rep)] + [swapped(take(mine_rep ^ k), "dp", k) for k in (1, 2, 3)]
-
-
 def by_section(section_at, choices):
     out = choices[-1]
     for s in reversed(range(len(choices) - 1)):
@@ -335,6 +376,10 @@
 
 def after(x, *marks):
     return lax.optimization_barrier((x,) + marks)[0]
+
+
+def together(*xs):
+    return lax.optimization_barrier(xs)
 
 
 def on_device(embeds, source, lengths, bounds, targets, w_query, w_key, w_value, w_out, w_class):
@@ -360,7 +405,11 @@
     both = mine_for(core) + swapped(mine_for(1 - core), "dp", 1)
     own = lax.dynamic_slice_in_dim(both, hi, 1, axis=0)[0]
     away = lax.dynamic_slice_in_dim(both, 1 - hi, 1, axis=0)[0]
-    first = [own[j] + swapped(away[j], "dp", 2) for j in range(ntr)]
+    away = [away[j] for j in range(ntr)]
+
+    def first(j):
+        return own[j] + swapped(away[j], "dp", 2)
+
 
     wanted = lax.dynamic_slice_in_dim(source, rep * ntr, ntr)
     lens = lengths[wanted]
@@ -396,19 +445,26 @@
 
     kept = []
     arriving = None
+    spans = [jnp.where(section_at == turn, lens[0], lens[1]) for turn in range(nst + 1)]
     for turn in range(nst):
-        cur = first[turn] if turn < ntr else jnp.zeros((width, dsh), BF16)
+        cur = first(turn) if turn < ntr else jnp.zeros((width, dsh), BF16)
+        if turn == 1:
+            spans, picks, bnd, tgt, tokens_total, w_class, cur, arriving = together(
+                spans, picks, bnd, tgt, tokens_total, w_class, cur, arriving
+            )
         if arriving is not None:
             cur = jnp.where(section_at == 0, cur, arriving)
-        length = jnp.where(section_at == turn, lens[0], lens[1])
         x = gathered(cur)
-        now = forward(length, x, *weights)
+        now = forward(spans[turn], x, *weights, True)
         kept.append(now)
         blocks = now["part"]
         if turn == nst - 1:
             blocks = with_ends(blocks, ends_of(0, blocks))
         got = exchange(blocks)
-        arriving = passed_along((cur.astype(F32) + sum_of(got)).astype(BF16), "section", 1)
+        arriving = (cur.astype(F32) + sum_of(got)).astype(BF16)
+        if turn == 0:
+            away = [away[0], after(away[1], arriving)]
+        arriving = passed_along(arriving, "section", 1)
 
     taken = {}
     top = jnp.int32(0)
@@ -417,28 +473,59 @@
     d, dx = backward(top, after(g_top, arriving), kept[-1], kept[-1], weights, True)
     taken[nst] = (d, g_top)
     x = gathered(arriving)
-    now = forward(lens[1], x, *weights)
+    now = forward(spans[nst], x, *weights, False)
     kept.append(now)
     got = exchange(with_ends(dx, ends_of(1, now["part"])))
     g_top = end_cotangent(1, got, x)
 
-    h_rows, o_rows, g_rows, d_rows = [], [], [], []
+    def chosen(choices, n=None):
+        if n is None:
+            return by_section(section_at, choices)
+        size = peers // lax.axis_size("dp")
+        cut = lambda x: lax.dynamic_slice_in_dim(x, n * size, size, axis=0)
+        return by_section(section_at, [cut(x) for x in choices])
+
+    def not_before(choices, mark):
+        return [after(x, mark) for x in choices]
+
+    seen = lambda name, which: [kept[s + which][name] for s in range(nst)]
+    back = lambda n, which: [taken[2 * nst - 1 - s + which][n] for s in range(nst)]
+
+    pieces = {}
+
+    def send_quarters(name, choices, masks):
+        for k in masks:
+            mine = chosen(choices, rep ^ k)
+            if k:
+                mine = swapped(mine, "dp", k) if k == 1 else mirrored(mine, k)
+            pieces[name, k] = mine
+
+    def send_whole(name, choices):
+        mine = chosen(choices)
+        far = swapped(mine, "dp", 2)
+        pieces[name, 0], pieces[name, 2] = mine, far
+        pieces[name, 1], pieces[name, 3] = swapped(mine, "dp", 1), swapped(far, "dp", 1)
+
+    def until(x):
+        return after(x, *pieces.values())
+
+    qcol = weights[0].shape[1]
+    widths = (qcol, HEAD_DIM, HEAD_DIM)
+    wide_o = (peers // lax.axis_size("dp") * dsh,)
+    of = lambda name: [pieces[name, k] for k in range(4)]
     for turn in range(nst + 1, 2 * nst + 1):
         grad = (grad.astype(F32) + sum_of(got)).astype(BF16)
         which = turn - nst - 1
         if which < ntr:
-            h = by_section(section_at, [kept[s + which]["h"] for s in range(nst)])
-            o = by_section(section_at, [kept[s + which]["o"] for s in range(nst)])
-            h_rows += quarters_among_replicas(after(h, grad), rep)
-            o_rows += among_replicas(after(o, grad))
-        elif turn == 2 * nst:
-            back = [taken[2 * nst - 1 - s] for s in range(nst)]
-            d_rows += among_replicas(after(by_section(section_at, [b[0] for b in back]), grad))
-            g_rows += quarters_among_replicas(
-                after(by_section(section_at, [b[1] for b in back]), grad), rep
-            )
+            send_quarters(("h", which), not_before(seen("h", which), grad), (0, 2))
+        elif turn < 2 * nst:
+            send_whole(("o", 0), not_before(seen("o", 0), grad))
+            send_whole(("o", 1), not_before(seen("o", 1), grad))
+        else:
+            send_quarters(("g", 0), not_before(back(1, 0), grad), (1, 3))
+            send_whole(("d", 0), not_before(back(0, 0), grad))
         grad = passed_along(grad, "section", -1)
-        g = gathered(grad)
+        g = until(gathered(grad))
         if turn == nst + 1:
             g = jnp.where(section_at == nst - 1, g_top, g)
             own_top = lax.dynamic_slice_in_dim(g_top, tensor_at, 1, axis=0)[0]
@@ -449,16 +536,22 @@
         if turn < 2 * nst:
             d, dx = backward(flag, g, kept[early], kept[late], weights, True)
             taken[turn] = (d, g)
-            got = exchange(dx)
+            if which < ntr:
+                send_quarters(("h", which), not_before(seen("h", which), dx), (1, 3))
+            else:
+                send_quarters(("g", 0), not_before(back(1, 0), dx), (0, 2))
+            got = until(exchange(dx))
         else:
+            taken[turn] = (d, g)
+            send_quarters(("g", 1), back(1, 1), range(4))
             (d,) = backward(flag, g, kept[early], kept[late], weights, False)
             taken[turn] = (d, g)
-
-    back = [taken[2 * nst - s] for s in range(nst)]
-    g_rows += quarters_among_replicas(by_section(section_at, [b[1] for b in back]), rep)
-    d_rows += among_replicas(by_section(section_at, [b[0] for b in back]))
-    grad_q, grad_k, grad_v = qkv_grad(h_rows, d_rows)
-    grad_o = out_grad(o_rows, g_rows)
+            send_whole(("d", 1), back(0, 1))
+
+    total_qkv = rows_grad(of(("h", 0)), of(("d", 0)), widths)
+    total_o = rows_grad(of(("o", 0)), of(("g", 0)), wide_o)
+    (grad_o,) = rows_grad(of(("o", 1)), of(("g", 1)), wide_o, total_o)
+    grad_q, grad_k, grad_v = rows_grad(of(("h", 1)), of(("d", 1)), widths, total_qkv)
     return (grad_q[None], grad_k[None], grad_v[None], grad_o[None])
 
 

time: 600 us -> 552 us (0.920)
  waiting for transfers between devices: 171 us -> 130 us
  Pallas kernels: 86.3 us -> 65.9 us
  other arithmetic: 26.2 us -> 41.8 us
  blocking collectives: 83.6 us -> 69.2 us
  local copies, waits for them, and re-layouts: 46.3 us -> 55.9 us
    all_to_all x12, waiting for transfers between devices: 97 us -> 52.5 us  [exchange(): lax.all_to_all(blocks, 'tensor', split_axis=0, concat_axis=0, tiled=True)]
    ppermute x27 -> x19, starting transfers between devices: 60.8 us -> 25 us  [swapped(): lax.ppermute(x, axis, [(i, i ^ mask) for i in range(lax.axis_size(axis))])]
    ppermute x0 -> x8, starting transfers between devices: none -> 35.2 us  [mirrored(): return lax.ppermute(x, ('dp', 'tensor'), pairs)]
    ppermute x0 -> x8, waiting for transfers between devices: none -> 30.9 us  [mirrored(): return lax.ppermute(x, ('dp', 'tensor'), pairs)]
    ppermute x27 -> x19, waiting for transfers between devices: 39.2 us -> 21.9 us  [swapped(): lax.ppermute(x, axis, [(i, i ^ mask) for i in range(lax.axis_size(axis))])]
    unnamed x164 -> x192, local copies, waits for them, and re-layouts: 23.7 us -> 39.2 us
    all_to_all x5, blocking collectives: 83.6 us -> 69.2 us  [exchange(): lax.all_to_all(blocks, 'tensor', split_axis=0, concat_axis=0, tiled=True)]
    pallas_call x7 -> x9, Pallas kernels: 41.7 us -> 29.9 us  [the longest x5 18.7 us: forward(): pl.pallas_call(functools.partial(forward_kernel, resident), out_shape=tup...]
  transfers between devices with their start and end apart: 48 -> 48, of which waited for: 30 -> 28; matrix products, arithmetic and copies ran while one was open for 6% -> 7% of each run, Pallas kernels for 3% -> 3%
where the time goes in v3:
time: 552 us; the launch traced here: 541 us
  starting transfers between devices  141 us (26%)
  waiting for transfers between devices  130 us (24%)
  blocking collectives  69.2 us (13%)
  Pallas kernels  65.9 us (12%)
  local copies, waits for them, and re-layouts  55.9 us (10%)
  other arithmetic  41.8 us (8%)
  between operations  22.8 us (4%)
  matrix products  13.8 us (2%)
    all_to_all x5, blocking collectives, exchange(): lax.all_to_all(blocks, 'tensor', split_axis=0, concat_axis=0, tiled=True)  69.2 us
    all_to_all x12, starting transfers between devices, exchange(): lax.all_to_all(blocks, 'tensor', split_axis=0, concat_axis=0, tiled=True)  57.3 us
    all_to_all x12, waiting for transfers between devices, exchange(): lax.all_to_all(blocks, 'tensor', split_axis=0, concat_axis=0, tiled=True)  52.5 us
    unnamed x192, local copies, waits for them, and re-layouts  39.2 us
    pallas_call x5, Pallas kernels, backward(): pl.pallas_call(functools.partial(backward_kernel, with_input), out_shape=...  36 us
    ppermute x8, starting transfers between devices, mirrored(): return lax.ppermute(x, ('dp', 'tensor'), pairs)  35.2 us
    ppermute x8, waiting for transfers between devices, mirrored(): return lax.ppermute(x, ('dp', 'tensor'), pairs)  30.9 us
    ppermute x19, starting transfers between devices, swapped(): lax.ppermute(x, axis, [(i, i ^ mask) for i in range(lax.axis_size(axis))])  25 us
  transfers between devices with their start and end apart: 48, of which 28 were waited for; matrix products, arithmetic and copies ran while one was open for 7% of the time, Pallas kernels for 3%

profile of v3, /device:TPU:1, one launch (start us, length us, event | category | flops | bytes accessed | tf_op | source)
XLA Modules:
  0.0 541.2 jit_solution(16456393537458448550)
XLA Ops:
  15.3 3.4 collective-permute-done.1
  19.7 5.2 all-to-all-start
  28.3 10.7 %all-to-all-done.x_ref = bf16[8,128,512]{2,1,0:T(8,128)(2,1)S(1)} async-done(((bf16[8,128,512]{2,1,0:T(8,128)(2,1)}), bf16[8,128,512]{2,1,0:T(8,128)(2,1)S(1)}, u32[]{:S(2)}, u32[]{:S(2)}) %all-to-all-start) | async-done | bytes 1048608 | tf_op jit(solution)/shard_map/all_to_all | solution.py:346
  50.3 4.8 all-to-all-start.1
  63.0 9.6 %all-to-all-done.1 = bf16[8,128,512]{2,1,0:T(8,128)(2,1)S(1)} async-done(((bf16[8,128,512]{2,1,0:T(8,128)(2,1)}), bf16[8,128,512]{2,1,0:T(8,128)(2,1)S(1)}, u32[]{:S(2)}, u32[]{:S(2)}) %all-to-all-start.1) | async-done | bytes 1048608 | tf_op jit(solution)/shard_map/all_to_all | solution.py:346
  75.2 3.6 collective-permute-start.3
  80.8 15.9 %all_to_all.85.x_ref = bf16[8,128,512]{2,1,0:T(8,128)(2,1)S(1)} all-to-all(bf16[8,128,512]{2,1,0:T(8,128)(2,1)S(1)} %broadcast_in_dim.157), channel_id=1, replica_groups=mesh['dp'=4,'section'=4,'tensor'=8] {'tensor'}, dimensions={0} | all-to-all | bytes 2097152 | tf_op jit(solution)/shard_map/all_to_all | solution.py:346
  104.2 14.3 %all_to_all.86 = bf16[8,128,512]{2,1,0:T(8,128)(2,1)S(1)} all-to-all(bf16[8,128,512]{2,1,0:T(8,128)(2,1)S(1)} %get-tuple-element.103), channel_id=1, replica_groups=mesh['dp'=4,'section'=4,'tensor'=8] {'tensor'}, dimensions={0} | all-to-all | bytes 2097152 | tf_op jit(solution)/shard_map/all_to_all | solution.py:346
  118.7 3.6 collective-permute-start.4
  124.3 13.1 %all_to_all.87.x_ref = bf16[8,128,512]{2,1,0:T(8,128)(2,1)S(1)} all-to-all(bf16[8,128,512]{2,1,0:T(8,128)(2,1)S(1)} %broadcast_in_dim.158), channel_id=1, replica_groups=mesh['dp'=4,'section'=4,'tensor'=8] {'tensor'}, dimensions={0} | all-to-all | bytes 2097152 | tf_op jit(solution)/shard_map/all_to_all | solution.py:346
  140.5 12.7 %all_to_all.88 = bf16[8,128,512]{2,1,0:T(8,128)(2,1)S(1)} all-to-all(bf16[8,128,512]{2,1,0:T(8,128)(2,1)S(1)} %get-tuple-element.105), channel_id=1, replica_groups=mesh['dp'=4,'section'=4,'tensor'=8] {'tensor'}, dimensions={0} | all-to-all | bytes 2097152 | tf_op jit(solution)/shard_map/all_to_all | solution.py:346
  153.4 7.4 %collective-permute-start.5 = (bf16[128,512]{1,0:T(8,128)(2,1)S(1)}, bf16[128,512]{1,0:T(8,128)(2,1)S(1)}, u32[]{:S(2)}, u32[]{:S(2)}) collective-permute-start(bf16[128,512]{1,0:T(8,128)(2,1)S(1)} %add_convert_fusion.4), channel_id=1, source_target_pairs={{0,8},{8,16},{16,24},{1,9},{9,17},{17,25},{2,10},{10,18},{18,26},{... | collective-permute-start | bytes 393224 | tf_op jit(solution)/shard_map/ppermute | solution.py:331
  163.5 13.2 %all_to_all.89.x_ref = bf16[8,128,512]{2,1,0:T(8,128)(2,1)S(1)} all-to-all(bf16[8,128,512]{2,1,0:T(8,128)(2,1)S(1)} %broadcast_in_dim.159), channel_id=1, replica_groups=mesh['dp'=4,'section'=4,'tensor'=8] {'tensor'}, dimensions={0} | all-to-all | bytes 2097152 | tf_op jit(solution)/shard_map/all_to_all | solution.py:346
  186.7 4.3 all-to-all-start.7
  191.6 10.2 %all-to-all-done.7 = bf16[8,160,512]{2,1,0:T(8,128)(2,1)} async-done(((bf16[8,160,512]{2,1,0:T(8,128)(2,1)}), bf16[8,160,512]{2,1,0:T(8,128)(2,1)}, u32[]{:S(2)}, u32[]{:S(2)}) %all-to-all-start.7) | async-done | bytes 1310752 | tf_op jit(solution)/shard_map/all_to_all | solution.py:346
  208.1 4.1 collective-permute-start.6
  215.2 4.2 all-to-all-start.8
  223.7 7.3 %backward_layer.4 = (bf16[128,768]{1,0:T(8,128)(2,1)S(1)}, bf16[8,128,512]{2,1,0:T(8,128)(2,1)S(1)}) custom-call(s32[1]{0:T(128)} %constant.66.clone.1.flag_ref, bf16[8,128,512]{2,1,0:T(8,128)(2,1)S(1)} %bitcast.162, bf16[1280,128]{1,0:T(8,128)(2,1)S(1)} %get-tuple-element.113.pack0_ref.pack1_ref, ...), custom_call_target="tpu_custom_call" | custom-call | flops 1342177280 | bytes 10485760 | tf_op jit(solution)/shard_map/backward_layer/pallas_call | solution.py:257
  233.7 6.6 %forward_layer.9 = (bf16[8,128,512]{2,1,0:T(8,128)(2,1)S(1)}, bf16[8,128,512]{2,1,0:T(8,128)(2,1)S(1)}, f32[128,128]{1,0:T(8,128)S(1)}, bf16[1280,128]{1,0:T(8,128)(2,1)S(1)}, bf16[128,512]{1,0:T(8,128)(2,1)S(1)}) custom-call(s32[1]{0:T(128)} %bitcast.29.len_ref, bf16[8,128,512]{2,1,0:T(8,128)(2,1)} %all-to-all-done.8.x_ref, bf16[4096,512]{1,0:T(8,128)(2,1)} %bitcast.123, ...), custom_call_target="tpu_custom_call" | custom-call | flops 1342177280 | bytes 10485760 | tf_op jit(solution)/shard_map/forward_layer/pallas_call | solution.py:138
  245.7 5.4 all-to-all-start.9
  251.1 10.9 %all-to-all-done.9 = bf16[8,160,512]{2,1,0:T(8,128)(2,1)} async-done(((bf16[8,160,512]{2,1,0:T(8,128)(2,1)}), bf16[8,160,512]{2,1,0:T(8,128)(2,1)}, u32[]{:S(2)}, u32[]{:S(2)}) %all-to-all-start.9) | async-done | bytes 1310752 | tf_op jit(solution)/shard_map/all_to_all | solution.py:346
  277.5 4.2 all-to-all-start.10
  293.3 7.5 %backward_layer.5 = (bf16[128,768]{1,0:T(8,128)(2,1)S(1)}, bf16[8,128,512]{2,1,0:T(8,128)(2,1)S(1)}) custom-call(s32[1]{0:T(128)} %bitcast.40.flag_ref, bf16[8,128,512]{2,1,0:T(8,128)(2,1)S(1)} %bitcast_select_fusion.g_ref, bf16[1280,128]{1,0:T(8,128)(2,1)S(1)} %copy-done.33, bf16[1280,128]{1,0:T(8,128)(2,1)S(1)} %copy-done.50, ...), custom_call_target="tpu_custom_call" | custom-call | flops 1342177280 | bytes 10485760 | tf_op jit(solution)/shard_map/backward_layer/pallas_call | solution.py:257
  302.4 4.2 all-to-all-start.11
  307.8 15.5 %collective-permute-start.10 = (bf16[2,128,512]{2,1,0:T(8,128)(2,1)S(1)}, bf16[2,128,512]{2,1,0:T(8,128)(2,1)S(1)}, u32[]{:S(2)}, u32[]{:S(2)}) collective-permute-start(bf16[2,128,512]{2,1,0:T(8,128)(2,1)S(1)} %get-tuple-element.200), channel_id=1, source_target_pairs={{0,100},{1,101},{2,102},{3,103},{4,96},{5,97},{6,98},{7,99},{32,68... | collective-permute-start | bytes 786440 | tf_op jit(solution)/shard_map/ppermute | solution.py:342
  323.3 6.3 %collective-permute-done.10.refs_3_ = bf16[2,128,512]{2,1,0:T(8,128)(2,1)S(1)} collective-permute-done((bf16[2,128,512]{2,1,0:T(8,128)(2,1)S(1)}, bf16[2,128,512]{2,1,0:T(8,128)(2,1)S(1)}, u32[]{:S(2)}, u32[]{:S(2)}) %collective-permute-start.10) | collective-permute-done | bytes 262176 | tf_op jit(solution)/shard_map/ppermute | solution.py:342
  334.8 5.8 %collective-permute-done.11 = bf16[128,512]{1,0:T(8,128)(2,1)S(1)} collective-permute-done((bf16[128,512]{1,0:T(8,128)(2,1)S(1)}, bf16[128,512]{1,0:T(8,128)(2,1)S(1)}, u32[]{:S(2)}, u32[]{:S(2)}) %collective-permute-start.11) | collective-permute-done | bytes 131104 | tf_op jit(solution)/shard_map/ppermute | solution.py:331
  342.3 4.2 all-to-all-start.12
  351.8 4.9 collective-permute-done.12.refs_2_
  360.0 8.5 %backward_layer.6 = (bf16[128,768]{1,0:T(8,128)(2,1)S(1)}, bf16[8,128,512]{2,1,0:T(8,128)(2,1)S(1)}) custom-call(s32[1]{0:T(128)} %bitcast.42.flag_ref, bf16[8,128,512]{2,1,0:T(8,128)(2,1)} %all-to-all-done.12.g_ref, bf16[1280,128]{1,0:T(8,128)(2,1)S(1)} %copy-done.30, bf16[1280,128]{1,0:T(8,128)(2,1)S(1)} %get-tuple-element.113.pack0_ref.pack1_ref, ...), custom_call_target="tpu_custom_call" | custom-call | flops 1342177280 | bytes 10485760 | tf_op jit(solution)/shard_map/backward_layer/pallas_call | solution.py:257
  370.1 7.0 %all-to-all-start.13 = ((bf16[8,128,512]{2,1,0:T(8,128)(2,1)}), bf16[8,128,512]{2,1,0:T(8,128)(2,1)}, u32[]{:S(2)}, u32[]{:S(2)}) async-start(bf16[8,128,512]{2,1,0:T(8,128)(2,1)} %copy-done.39), calls=%async_computation.13 | async-start | bytes 2097152 | tf_op jit(solution)/shard_map/all_to_all | solution.py:346
  378.3 4.9 collective-permute-start.14
  383.5 5.9 %collective-permute-done.14.refs_3_ = bf16[2,128,512]{2,1,0:T(8,128)(2,1)S(1)} collective-permute-done((bf16[2,128,512]{2,1,0:T(8,128)(2,1)S(1)}, bf16[2,128,512]{2,1,0:T(8,128)(2,1)S(1)}, u32[]{:S(2)}, u32[]{:S(2)}) %collective-permute-start.14) | collective-permute-done | bytes 262176 | tf_op jit(solution)/shard_map/ppermute | solution.py:342
  394.6 7.0 %collective-permute-done.15 = bf16[128,512]{1,0:T(8,128)(2,1)S(1)} collective-permute-done((bf16[128,512]{1,0:T(8,128)(2,1)S(1)}, bf16[128,512]{1,0:T(8,128)(2,1)S(1)}, u32[]{:S(2)}, u32[]{:S(2)}) %collective-permute-start.15) | collective-permute-done | bytes 131104 | tf_op jit(solution)/shard_map/ppermute | solution.py:331
  402.7 4.7 all-to-all-start.14
  414.2 8.6 %collective-permute-done.19.refs_2_ = bf16[128,512]{1,0:T(8,128)(2,1)} collective-permute-done((bf16[128,512]{1,0:T(8,128)(2,1)}, bf16[128,512]{1,0:T(8,128)(2,1)}, u32[]{:S(2)}, u32[]{:S(2)}) %collective-permute-start.19) | collective-permute-done | bytes 131104 | tf_op jit(solution)/shard_map/ppermute | solution.py:335
  422.7 3.5 collective-permute-start.21
  434.2 7.3 %backward_layer.7 = (bf16[128,768]{1,0:T(8,128)(2,1)S(1)}, bf16[8,128,512]{2,1,0:T(8,128)(2,1)S(1)}) custom-call(s32[1]{0:T(128)} %bitcast.44.flag_ref, bf16[8,128,512]{2,1,0:T(8,128)(2,1)S(1)} %copy-done.16, bf16[1280,128]{1,0:T(8,128)(2,1)S(1)} %copy-done.28, bf16[1280,128]{1,0:T(8,128)(2,1)S(1)} %copy-done.34, bf16[8,128,512]{2,1,0:T(8,128)(2,1)S(1)} %copy-done.21, ...), custom_call_target="tpu_custom_call" | custom-call | flops 1342177280 | bytes 10485760 | tf_op jit(solution)/shard_map/backward_layer/pallas_call | solution.py:257
  443.2 4.7 all-to-all-start.15
  453.1 5.9 %collective-permute-done.22.refs_6_ = bf16[2,128,512]{2,1,0:T(8,128)(2,1)S(1)} collective-permute-done((bf16[2,128,512]{2,1,0:T(8,128)(2,1)S(1)}, bf16[2,128,512]{2,1,0:T(8,128)(2,1)S(1)}, u32[]{:S(2)}, u32[]{:S(2)}) %collective-permute-start.22) | collective-permute-done | bytes 262176 | tf_op jit(solution)/shard_map/ppermute | solution.py:342
  458.9 4.0 all-to-all-done.15
  466.6 5.8 %collective-permute-done.23 = bf16[128,512]{1,0:T(8,128)(2,1)S(1)} collective-permute-done((bf16[128,512]{1,0:T(8,128)(2,1)S(1)}, bf16[128,512]{1,0:T(8,128)(2,1)S(1)}, u32[]{:S(2)}, u32[]{:S(2)}) %collective-permute-start.23) | collective-permute-done | bytes 131104 | tf_op jit(solution)/shard_map/ppermute | solution.py:331
  473.4 4.3 all-to-all-start.16
  483.7 3.7 collective-permute-start.25
  487.9 6.6 %collective-permute-done.26.refs_6_ = bf16[128,768]{1,0:T(8,128)(2,1)} collective-permute-done((bf16[128,768]{1,0:T(8,128)(2,1)}, bf16[128,768]{1,0:T(8,128)(2,1)}, u32[]{:S(2)}, u32[]{:S(2)}) %collective-permute-start.26) | collective-permute-done | bytes 196640 | tf_op jit(solution)/shard_map/ppermute | solution.py:335
  501.7 5.5 %backward_heads.1 = bf16[128,768]{1,0:T(8,128)(2,1)S(1)} custom-call(s32[1]{0:T(128)} %bitcast.43.flag_ref, bf16[8,128,512]{2,1,0:T(8,128)(2,1)} %all-to-all-done.16.g_ref, bf16[1280,128]{1,0:T(8,128)(2,1)S(1)} %copy-done.28, bf16[1280,128]{1,0:T(8,128)(2,1)S(1)} %copy-done.31, bf16[8,128,512]{2,1,0:T(8,128)(2,1)S(1)} %copy-done.22, ...), custom_call_target="tpu_custom_call" | custom-call | flops 1342177280 | bytes 10485760 | tf_op jit(solution)/shard_map/backward_heads/pallas_call | solution.py:257
  521.4 5.6 %collective-permute-done.33.refs_6_ = bf16[2,128,512]{2,1,0:T(8,128)(2,1)S(1)} collective-permute-done((bf16[2,128,512]{2,1,0:T(8,128)(2,1)S(1)}, bf16[2,128,512]{2,1,0:T(8,128)(2,1)S(1)}, u32[]{:S(2)}, u32[]{:S(2)}) %collective-permute-start.33) | collective-permute-done | bytes 262176 | tf_op jit(solution)/shard_map/ppermute | solution.py:342
  530.3 3.6 weight_grad.5
  (344 shorter events, 188.2 us)
Async XLA Ops:
  9.1 3.0 collective-permute-start
  12.3 6.3 %collective-permute-start.1 = (bf16[128,512]{1,0:T(8,128)(2,1)S(1)}, bf16[128,512]{1,0:T(8,128)(2,1)S(1)}, u32[]{:S(2)}, u32[]{:S(2)}) collective-permute-start(bf16[128,512]{1,0:T(8,128)(2,1)S(1)} %get-tuple-element.204), channel_id=1, source_target_pairs={{0,64},{32,96},{64,0},{96,32},{1,65},{33,97},{65,1},{97,33},{2,66}... | collective-permute-start | bytes 393224 | tf_op jit(solution)/shard_map/ppermute | solution.py:335
  19.7 19.3 %all-to-all-start = ((bf16[8,128,512]{2,1,0:T(8,128)(2,1)}), bf16[8,128,512]{2,1,0:T(8,128)(2,1)S(1)}, u32[]{:S(2)}, u32[]{:S(2)}) async-start(bf16[8,128,512]{2,1,0:T(8,128)(2,1)} %broadcast_in_dim.156), calls=%async_computation | async-start | bytes 2097152 | tf_op jit(solution)/shard_map/all_to_all | solution.py:346
  24.9 54.8 %all-gather.2.cloned.1.call-start = ((), (), s32[]{:S(2)}) async-start(), calls=%async_computation.17 | async-start | bytes 1179648 | tf_op jit(solution)/shard_map/all_gather | solution.py:393
  50.3 22.3 %all-to-all-start.1 = ((bf16[8,128,512]{2,1,0:T(8,128)(2,1)}), bf16[8,128,512]{2,1,0:T(8,128)(2,1)S(1)}, u32[]{:S(2)}, u32[]{:S(2)}) async-start(bf16[8,128,512]{2,1,0:T(8,128)(2,1)} %copy-done.38), calls=%async_computation.1 | async-start | bytes 2097152 | tf_op jit(solution)/shard_map/all_to_all | solution.py:346
  72.8 6.0 %collective-permute-start.2 = (bf16[128,512]{1,0:T(8,128)(2,1)S(1)}, bf16[128,512]{1,0:T(8,128)(2,1)S(1)}, u32[]{:S(2)}, u32[]{:S(2)}) collective-permute-start(bf16[128,512]{1,0:T(8,128)(2,1)S(1)} %get-tuple-element.97), channel_id=1, source_target_pairs={{0,64},{32,96},{64,0},{96,32},{1,65},{33,97},{65,1},{97,33},{2,66}... | collective-permute-start | bytes 393224 | tf_op jit(solution)/shard_map/ppermute | solution.py:335
  75.2 5.5 %collective-permute-start.3 = (bf16[128,512]{1,0:T(8,128)(2,1)S(1)}, bf16[128,512]{1,0:T(8,128)(2,1)S(1)}, u32[]{:S(2)}, u32[]{:S(2)}) collective-permute-start(bf16[128,512]{1,0:T(8,128)(2,1)S(1)} %add_convert_fusion.6), channel_id=1, source_target_pairs={{0,8},{8,16},{16,24},{1,9},{9,17},{17,25},{2,10},{10,18},{18,26},{... | collective-permute-start | bytes 393224 | tf_op jit(solution)/shard_map/ppermute | solution.py:331
  118.7 5.5 %collective-permute-start.4 = (bf16[128,512]{1,0:T(8,128)(2,1)S(1)}, bf16[128,512]{1,0:T(8,128)(2,1)S(1)}, u32[]{:S(2)}, u32[]{:S(2)}) collective-permute-start(bf16[128,512]{1,0:T(8,128)(2,1)S(1)} %add_convert_fusion.5), channel_id=1, source_target_pairs={{0,8},{8,16},{16,24},{1,9},{9,17},{17,25},{2,10},{10,18},{18,26},{... | collective-permute-start | bytes 393224 | tf_op jit(solution)/shard_map/ppermute | solution.py:331
  153.4 9.3 %collective-permute-start.5 = (bf16[128,512]{1,0:T(8,128)(2,1)S(1)}, bf16[128,512]{1,0:T(8,128)(2,1)S(1)}, u32[]{:S(2)}, u32[]{:S(2)}) collective-permute-start(bf16[128,512]{1,0:T(8,128)(2,1)S(1)} %add_convert_fusion.4), channel_id=1, source_target_pairs={{0,8},{8,16},{16,24},{1,9},{9,17},{17,25},{2,10},{10,18},{18,26},{... | collective-permute-start | bytes 393224 | tf_op jit(solution)/shard_map/ppermute | solution.py:331
  186.7 15.1 %all-to-all-start.7 = ((bf16[8,160,512]{2,1,0:T(8,128)(2,1)}), bf16[8,160,512]{2,1,0:T(8,128)(2,1)}, u32[]{:S(2)}, u32[]{:S(2)}) async-start(bf16[8,160,512]{2,1,0:T(8,128)(2,1)} %pad_maximum_fusion), calls=%async_computation.7 | async-start | bytes 2621440 | tf_op jit(solution)/shard_map/all_to_all | solution.py:346
  208.1 6.0 %collective-permute-start.6 = (bf16[128,512]{1,0:T(8,128)(2,1)S(1)}, bf16[128,512]{1,0:T(8,128)(2,1)S(1)}, u32[]{:S(2)}, u32[]{:S(2)}) collective-permute-start(bf16[128,512]{1,0:T(8,128)(2,1)S(1)} %add_convert_fusion.3), channel_id=1, source_target_pairs={{0,8},{8,16},{16,24},{1,9},{9,17},{17,25},{2,10},{10,18},{18,26},{... | collective-permute-start | bytes 393224 | tf_op jit(solution)/shard_map/ppermute | solution.py:331
  215.2 18.4 %all-to-all-start.8 = ((bf16[8,128,512]{2,1,0:T(8,128)(2,1)}), bf16[8,128,512]{2,1,0:T(8,128)(2,1)}, u32[]{:S(2)}, u32[]{:S(2)}) async-start(bf16[8,128,512]{2,1,0:T(8,128)(2,1)} %broadcast_in_dim.162), calls=%async_computation.8 | async-start | bytes 2097152 | tf_op jit(solution)/shard_map/all_to_all | solution.py:346
  245.7 16.3 %all-to-all-start.9 = ((bf16[8,160,512]{2,1,0:T(8,128)(2,1)}), bf16[8,160,512]{2,1,0:T(8,128)(2,1)}, u32[]{:S(2)}, u32[]{:S(2)}) async-start(bf16[8,160,512]{2,1,0:T(8,128)(2,1)} %pad_maximum_fusion.1), calls=%async_computation.9 | async-start | bytes 2621440 | tf_op jit(solution)/shard_map/all_to_all | solution.py:346
  265.0 10.6 %collective-permute-start.7 = (bf16[128,512]{1,0:T(8,128)(2,1)}, bf16[128,512]{1,0:T(8,128)(2,1)}, u32[]{:S(2)}, u32[]{:S(2)}) collective-permute-start(bf16[128,512]{1,0:T(8,128)(2,1)} %fusion.8), channel_id=1, source_target_pairs={{8,0},{16,8},{24,16},{9,1},{17,9},{25,17},{10,2},{18,10},{26,18},{... | collective-permute-start | bytes 393224 | tf_op jit(solution)/shard_map/ppermute | solution.py:331
  271.4 16.5 %collective-permute-start.8 = (bf16[2,128,512]{2,1,0:T(8,128)(2,1)}, bf16[2,128,512]{2,1,0:T(8,128)(2,1)}, u32[]{:S(2)}, u32[]{:S(2)}) collective-permute-start(bf16[2,128,512]{2,1,0:T(8,128)(2,1)} %get-tuple-element.202), channel_id=1, source_target_pairs={{0,68},{1,69},{2,70},{3,71},{4,64},{5,65},{6,66},{7,67},{32,100},{... | collective-permute-start | bytes 786440 | tf_op jit(solution)/shard_map/ppermute | solution.py:342
  277.5 13.7 %all-to-all-start.10 = ((bf16[8,128,512]{2,1,0:T(8,128)(2,1)}), bf16[8,128,512]{2,1,0:T(8,128)(2,1)}, u32[]{:S(2)}, u32[]{:S(2)}) async-start(bf16[8,128,512]{2,1,0:T(8,128)(2,1)} %broadcast_in_dim.165), calls=%async_computation.10 | async-start | bytes 2097152 | tf_op jit(solution)/shard_map/all_to_all | solution.py:346
  302.4 28.7 %all-to-all-start.11 = ((bf16[8,128,512]{2,1,0:T(8,128)(2,1)}), bf16[8,128,512]{2,1,0:T(8,128)(2,1)}, u32[]{:S(2)}, u32[]{:S(2)}) async-start(bf16[8,128,512]{2,1,0:T(8,128)(2,1)} %copy-done.37), calls=%async_computation.11 | async-start | bytes 2097152 | tf_op jit(solution)/shard_map/all_to_all | solution.py:346
  307.8 21.8 %collective-permute-start.10 = (bf16[2,128,512]{2,1,0:T(8,128)(2,1)S(1)}, bf16[2,128,512]{2,1,0:T(8,128)(2,1)S(1)}, u32[]{:S(2)}, u32[]{:S(2)}) collective-permute-start(bf16[2,128,512]{2,1,0:T(8,128)(2,1)S(1)} %get-tuple-element.200), channel_id=1, source_target_pairs={{0,100},{1,101},{2,102},{3,103},{4,96},{5,97},{6,98},{7,99},{32,68... | collective-permute-start | bytes 786440 | tf_op jit(solution)/shard_map/ppermute | solution.py:342
  323.3 7.1 %collective-permute-start.9 = (bf16[2,128,512]{2,1,0:T(8,128)(2,1)S(1)}, bf16[2,128,512]{2,1,0:T(8,128)(2,1)S(1)}, u32[]{:S(2)}, u32[]{:S(2)}) collective-permute-start(bf16[2,128,512]{2,1,0:T(8,128)(2,1)S(1)} %get-tuple-element.201), channel_id=1, source_target_pairs={{0,32},{32,0},{64,96},{96,64},{1,33},{33,1},{65,97},{97,65},{2,34}... | collective-permute-start | bytes 786440 | tf_op jit(solution)/shard_map/ppermute | solution.py:335
  333.5 7.1 %collective-permute-start.11 = (bf16[128,512]{1,0:T(8,128)(2,1)S(1)}, bf16[128,512]{1,0:T(8,128)(2,1)S(1)}, u32[]{:S(2)}, u32[]{:S(2)}) collective-permute-start(bf16[128,512]{1,0:T(8,128)(2,1)S(1)} %add_convert_fusion.2), channel_id=1, source_target_pairs={{8,0},{16,8},{24,16},{9,1},{17,9},{25,17},{10,2},{18,10},{26,18},{... | collective-permute-start | bytes 393224 | tf_op jit(solution)/shard_map/ppermute | solution.py:331
  342.3 15.9 %all-to-all-start.12 = ((bf16[8,128,512]{2,1,0:T(8,128)(2,1)}), bf16[8,128,512]{2,1,0:T(8,128)(2,1)}, u32[]{:S(2)}, u32[]{:S(2)}) async-start(bf16[8,128,512]{2,1,0:T(8,128)(2,1)} %broadcast_in_dim.166), calls=%async_computation.12 | async-start | bytes 2097152 | tf_op jit(solution)/shard_map/all_to_all | solution.py:346
  348.6 8.2 %collective-permute-start.12 = (bf16[2,128,512]{2,1,0:T(8,128)(2,1)}, bf16[2,128,512]{2,1,0:T(8,128)(2,1)}, u32[]{:S(2)}, u32[]{:S(2)}) collective-permute-start(bf16[2,128,512]{2,1,0:T(8,128)(2,1)} %get-tuple-element.198), channel_id=1, source_target_pairs={{0,68},{1,69},{2,70},{3,71},{4,64},{5,65},{6,66},{7,67},{32,100},{... | collective-permute-start | bytes 786440 | tf_op jit(solution)/shard_map/ppermute | solution.py:342
  370.1 21.5 %all-to-all-start.13 = ((bf16[8,128,512]{2,1,0:T(8,128)(2,1)}), bf16[8,128,512]{2,1,0:T(8,128)(2,1)}, u32[]{:S(2)}, u32[]{:S(2)}) async-start(bf16[8,128,512]{2,1,0:T(8,128)(2,1)} %copy-done.39), calls=%async_computation.13 | async-start | bytes 2097152 | tf_op jit(solution)/shard_map/all_to_all | solution.py:346
  378.3 11.0 %collective-permute-start.14 = (bf16[2,128,512]{2,1,0:T(8,128)(2,1)S(1)}, bf16[2,128,512]{2,1,0:T(8,128)(2,1)S(1)}, u32[]{:S(2)}, u32[]{:S(2)}) collective-permute-start(bf16[2,128,512]{2,1,0:T(8,128)(2,1)S(1)} %get-tuple-element.196), channel_id=1, source_target_pairs={{0,100},{1,101},{2,102},{3,103},{4,96},{5,97},{6,98},{7,99},{32,68... | collective-permute-start | bytes 786440 | tf_op jit(solution)/shard_map/ppermute | solution.py:342
  383.3 6.1 %collective-permute-start.13 = (bf16[2,128,512]{2,1,0:T(8,128)(2,1)S(1)}, bf16[2,128,512]{2,1,0:T(8,128)(2,1)S(1)}, u32[]{:S(2)}, u32[]{:S(2)}) collective-permute-start(bf16[2,128,512]{2,1,0:T(8,128)(2,1)S(1)} %get-tuple-element.197), channel_id=1, source_target_pairs={{0,32},{32,0},{64,96},{96,64},{1,33},{33,1},{65,97},{97,65},{2,34}... | collective-permute-start | bytes 786440 | tf_op jit(solution)/shard_map/ppermute | solution.py:335
  393.1 8.5 %collective-permute-start.15 = (bf16[128,512]{1,0:T(8,128)(2,1)S(1)}, bf16[128,512]{1,0:T(8,128)(2,1)S(1)}, u32[]{:S(2)}, u32[]{:S(2)}) collective-permute-start(bf16[128,512]{1,0:T(8,128)(2,1)S(1)} %add_convert_fusion.1), channel_id=1, source_target_pairs={{8,0},{16,8},{24,16},{9,1},{17,9},{25,17},{10,2},{18,10},{26,18},{... | collective-permute-start | bytes 393224 | tf_op jit(solution)/shard_map/ppermute | solution.py:331
  402.7 26.3 %all-to-all-start.14 = ((bf16[8,128,512]{2,1,0:T(8,128)(2,1)}), bf16[8,128,512]{2,1,0:T(8,128)(2,1)S(1)}, u32[]{:S(2)}, u32[]{:S(2)}) async-start(bf16[8,128,512]{2,1,0:T(8,128)(2,1)} %broadcast_in_dim.167), calls=%async_computation.14 | async-start | bytes 2097152 | tf_op jit(solution)/shard_map/all_to_all | solution.py:346
  409.3 13.4 %collective-permute-start.19 = (bf16[128,512]{1,0:T(8,128)(2,1)}, bf16[128,512]{1,0:T(8,128)(2,1)}, u32[]{:S(2)}, u32[]{:S(2)}) collective-permute-start(bf16[128,512]{1,0:T(8,128)(2,1)} %get-tuple-element.206.refs_0_), channel_id=1, source_target_pairs={{0,64},{32,96},{64,0},{96,32},{1,65},{33,97},{65,1},{97,33},{2,66}... | collective-permute-start | bytes 393224 | tf_op jit(solution)/shard_map/ppermute | solution.py:335
  410.7 15.5 %collective-permute-start.16 = (bf16[128,512]{1,0:T(8,128)(2,1)}, bf16[128,512]{1,0:T(8,128)(2,1)}, u32[]{:S(2)}, u32[]{:S(2)}) collective-permute-start(bf16[128,512]{1,0:T(8,128)(2,1)} %get-tuple-element.207.refs_0_), channel_id=1, source_target_pairs={{0,64},{32,96},{64,0},{96,32},{1,65},{33,97},{65,1},{97,33},{2,66}... | collective-permute-start | bytes 393224 | tf_op jit(solution)/shard_map/ppermute | solution.py:335
  412.3 15.3 %collective-permute-start.20 = (bf16[128,512]{1,0:T(8,128)(2,1)}, bf16[128,512]{1,0:T(8,128)(2,1)}, u32[]{:S(2)}, u32[]{:S(2)}) collective-permute-start(bf16[128,512]{1,0:T(8,128)(2,1)} %get-tuple-element.206.refs_0_), channel_id=1, source_target_pairs={{0,32},{32,0},{64,96},{96,64},{1,33},{33,1},{65,97},{97,65},{2,34}... | collective-permute-start | bytes 393224 | tf_op jit(solution)/shard_map/ppermute | solution.py:335
  414.1 13.5 %collective-permute-start.17 = (bf16[128,512]{1,0:T(8,128)(2,1)}, bf16[128,512]{1,0:T(8,128)(2,1)}, u32[]{:S(2)}, u32[]{:S(2)}) collective-permute-start(bf16[128,512]{1,0:T(8,128)(2,1)} %get-tuple-element.207.refs_0_), channel_id=1, source_target_pairs={{0,32},{32,0},{64,96},{96,64},{1,33},{33,1},{65,97},{97,65},{2,34}... | collective-permute-start | bytes 393224 | tf_op jit(solution)/shard_map/ppermute | solution.py:335
  422.7 4.9 collective-permute-start.21
  426.2 2.7 collective-permute-start.18
  443.2 19.8 %all-to-all-start.15 = ((bf16[8,128,512]{2,1,0:T(8,128)(2,1)}), bf16[8,128,512]{2,1,0:T(8,128)(2,1)}, u32[]{:S(2)}, u32[]{:S(2)}) async-start(bf16[8,128,512]{2,1,0:T(8,128)(2,1)} %copy-done.42), calls=%async_computation.15 | async-start | bytes 2097152 | tf_op jit(solution)/shard_map/all_to_all | solution.py:346
  450.0 8.9 %collective-permute-start.22 = (bf16[2,128,512]{2,1,0:T(8,128)(2,1)S(1)}, bf16[2,128,512]{2,1,0:T(8,128)(2,1)S(1)}, u32[]{:S(2)}, u32[]{:S(2)}) collective-permute-start(bf16[2,128,512]{2,1,0:T(8,128)(2,1)S(1)} %get-tuple-element.194), channel_id=1, source_target_pairs={{0,68},{1,69},{2,70},{3,71},{4,64},{5,65},{6,66},{7,67},{32,100},{... | collective-permute-start | bytes 786440 | tf_op jit(solution)/shard_map/ppermute | solution.py:342
  465.3 7.1 %collective-permute-start.23 = (bf16[128,512]{1,0:T(8,128)(2,1)S(1)}, bf16[128,512]{1,0:T(8,128)(2,1)S(1)}, u32[]{:S(2)}, u32[]{:S(2)}) collective-permute-start(bf16[128,512]{1,0:T(8,128)(2,1)S(1)} %add_convert_fusion), channel_id=1, source_target_pairs={{8,0},{16,8},{24,16},{9,1},{17,9},{25,17},{10,2},{18,10},{26,18},{... | collective-permute-start | bytes 393224 | tf_op jit(solution)/shard_map/ppermute | solution.py:331
  473.4 25.2 %all-to-all-start.16 = ((bf16[8,128,512]{2,1,0:T(8,128)(2,1)}), bf16[8,128,512]{2,1,0:T(8,128)(2,1)}, u32[]{:S(2)}, u32[]{:S(2)}) async-start(bf16[8,128,512]{2,1,0:T(8,128)(2,1)} %broadcast_in_dim.168), calls=%async_computation.16 | async-start | bytes 2097152 | tf_op jit(solution)/shard_map/all_to_all | solution.py:346
  479.5 15.0 %collective-permute-start.26 = (bf16[128,768]{1,0:T(8,128)(2,1)}, bf16[128,768]{1,0:T(8,128)(2,1)}, u32[]{:S(2)}, u32[]{:S(2)}) collective-permute-start(bf16[128,768]{1,0:T(8,128)(2,1)} %select_select_fusion.18.refs_4_), channel_id=1, source_target_pairs={{0,64},{32,96},{64,0},{96,32},{1,65},{33,97},{65,1},{97,33},{2,66}... | collective-permute-start | bytes 589832 | tf_op jit(solution)/shard_map/ppermute | solution.py:335
  483.7 14.9 %collective-permute-start.25 = (bf16[2,128,512]{2,1,0:T(8,128)(2,1)}, bf16[2,128,512]{2,1,0:T(8,128)(2,1)}, u32[]{:S(2)}, u32[]{:S(2)}) collective-permute-start(bf16[2,128,512]{2,1,0:T(8,128)(2,1)} %get-tuple-element.192), channel_id=1, source_target_pairs={{0,100},{1,101},{2,102},{3,103},{4,96},{5,97},{6,98},{7,99},{32,68... | collective-permute-start | bytes 786440 | tf_op jit(solution)/shard_map/ppermute | solution.py:342
  487.4 11.2 %collective-permute-start.24 = (bf16[2,128,512]{2,1,0:T(8,128)(2,1)}, bf16[2,128,512]{2,1,0:T(8,128)(2,1)}, u32[]{:S(2)}, u32[]{:S(2)}) collective-permute-start(bf16[2,128,512]{2,1,0:T(8,128)(2,1)} %get-tuple-element.193), channel_id=1, source_target_pairs={{0,32},{32,0},{64,96},{96,64},{1,33},{33,1},{65,97},{97,65},{2,34}... | collective-permute-start | bytes 786440 | tf_op jit(solution)/shard_map/ppermute | solution.py:335
  487.4 9.6 %collective-permute-start.27 = (bf16[128,768]{1,0:T(8,128)(2,1)}, bf16[128,768]{1,0:T(8,128)(2,1)}, u32[]{:S(2)}, u32[]{:S(2)}) collective-permute-start(bf16[128,768]{1,0:T(8,128)(2,1)} %select_select_fusion.18.refs_4_), channel_id=1, source_target_pairs={{0,32},{32,0},{64,96},{96,64},{1,33},{33,1},{65,97},{97,65},{2,34}... | collective-permute-start | bytes 589832 | tf_op jit(solution)/shard_map/ppermute | solution.py:335
  494.5 4.1 collective-permute-start.28
  507.3 7.2 %collective-permute-start.30 = (bf16[128,768]{1,0:T(8,128)(2,1)S(1)}, bf16[128,768]{1,0:T(8,128)(2,1)S(1)}, u32[]{:S(2)}, u32[]{:S(2)}) collective-permute-start(bf16[128,768]{1,0:T(8,128)(2,1)S(1)} %select_select_fusion.17.refs_4_), channel_id=1, source_target_pairs={{0,64},{32,96},{64,0},{96,32},{1,65},{33,97},{65,1},{97,33},{2,66}... | collective-permute-start | bytes 589832 | tf_op jit(solution)/shard_map/ppermute | solution.py:335
  510.1 11.3 %collective-permute-start.34 = (bf16[2,128,512]{2,1,0:T(8,128)(2,1)S(1)}, bf16[2,128,512]{2,1,0:T(8,128)(2,1)S(1)}, u32[]{:S(2)}, u32[]{:S(2)}) collective-permute-start(bf16[2,128,512]{2,1,0:T(8,128)(2,1)S(1)} %get-tuple-element.188), channel_id=1, source_target_pairs={{0,100},{1,101},{2,102},{3,103},{4,96},{5,97},{6,98},{7,99},{32,68... | collective-permute-start | bytes 786440 | tf_op jit(solution)/shard_map/ppermute | solution.py:342
  512.8 14.1 %collective-permute-start.33 = (bf16[2,128,512]{2,1,0:T(8,128)(2,1)S(1)}, bf16[2,128,512]{2,1,0:T(8,128)(2,1)S(1)}, u32[]{:S(2)}, u32[]{:S(2)}) collective-permute-start(bf16[2,128,512]{2,1,0:T(8,128)(2,1)S(1)} %get-tuple-element.189), channel_id=1, source_target_pairs={{0,68},{1,69},{2,70},{3,71},{4,64},{5,65},{6,66},{7,67},{32,100},{... | collective-permute-start | bytes 786440 | tf_op jit(solution)/shard_map/ppermute | solution.py:342
  513.4 13.6 %collective-permute-start.32 = (bf16[2,128,512]{2,1,0:T(8,128)(2,1)S(1)}, bf16[2,128,512]{2,1,0:T(8,128)(2,1)S(1)}, u32[]{:S(2)}, u32[]{:S(2)}) collective-permute-start(bf16[2,128,512]{2,1,0:T(8,128)(2,1)S(1)} %get-tuple-element.190), channel_id=1, source_target_pairs={{0,32},{32,0},{64,96},{96,64},{1,33},{33,1},{65,97},{97,65},{2,34}... | collective-permute-start | bytes 786440 | tf_op jit(solution)/shard_map/ppermute | solution.py:335
  513.5 16.7 %collective-permute-start.29 = (bf16[128,768]{1,0:T(8,128)(2,1)S(1)}, bf16[128,768]{1,0:T(8,128)(2,1)S(1)}, u32[]{:S(2)}, u32[]{:S(2)}) collective-permute-start(bf16[128,768]{1,0:T(8,128)(2,1)S(1)} %select_select_fusion.17.refs_4_), channel_id=1, source_target_pairs={{0,32},{32,0},{64,96},{96,64},{1,33},{33,1},{65,97},{97,65},{2,34}... | collective-permute-start | bytes 589832 | tf_op jit(solution)/shard_map/ppermute | solution.py:335
  514.4 15.8 %collective-permute-start.31 = (bf16[128,768]{1,0:T(8,128)(2,1)S(1)}, bf16[128,768]{1,0:T(8,128)(2,1)S(1)}, u32[]{:S(2)}, u32[]{:S(2)}) collective-permute-start(bf16[128,768]{1,0:T(8,128)(2,1)S(1)} %collective-permute-done.30.refs_6_), channel_id=1, source_target_pairs={{0,32},{32,0},{64,96},{96,64},{1,33},{33,1},{65,97},{97,65},{2,34}... | collective-permute-start | bytes 589832 | tf_op jit(solution)/shard_map/ppermute | solution.py:335
  (94 other events, 681.2 us)
Sparse Core Ops, SparseCore 0:
  27.4 41.3 all-gather.1

commit v4 on v3

v4 whole, which is shorter than its diff:
```python
import functools

import jax
import jax.numpy as jnp
from jax import lax
from jax.experimental import pallas as pl
from jax.experimental.pallas import tpu as pltpu
from jax.sharding import PartitionSpec as P

HEAD_DIM = 128
EPS = 1e-06
LOSS_SCALE = 16384.0
SCORE_SCALE = 1.0 / HEAD_DIM**0.5
F32 = jnp.float32
BF16 = jnp.bfloat16
VMEM_LIMIT = 16 * 1024 * 1024


def dot(a, b):
    return jnp.dot(a, b, preferred_element_type=F32)


def dot_nt(a, b):
    return lax.dot_general(a, b, (((1,), (1,)), ((), ())), preferred_element_type=F32)


def dot_tn(a, b):
    return lax.dot_general(a, b, (((0,), (0,)), ((), ())), preferred_element_type=F32)


def in_vmem():
    return pl.BlockSpec(memory_space=pltpu.VMEM)


def in_smem():
    return pl.BlockSpec(memory_space=pltpu.SMEM)


def anywhere():
    return pl.BlockSpec(memory_space=pl.ANY)


def kernel_params(limit):
    return pltpu.CompilerParams(vmem_limit_bytes=limit)


def place_ends(ends_ref, block, rows, nstep):
    ends_ref[pl.ds(block * nstep, nstep), :] = rows[:nstep]


def forward_kernel(mode, nstep, len_ref, x_ref, wq_ref, wk_ref, wv_ref, wo_ref, *rest):
    if mode == "all":
        part_ref, h_ref, scale_ref, pack_ref, o_ref = rest
    else:
        pick_ref, part_ref, h_ref, scale_ref, pack_ref, o_ref, ends_ref = rest
    nblk, rows, dsh = x_ref.shape
    qh = wq_ref.shape[1] // HEAD_DIM
    sq = jnp.zeros((rows, 1), F32)
    for j in range(nblk):
        xf = x_ref[j].astype(F32)
        sq = sq + jnp.sum(xf * xf, axis=1, keepdims=True)
    scale = lax.rsqrt(sq / (nblk * dsh) + EPS)
    scale_ref[...] = jnp.broadcast_to(scale, scale_ref.shape)
    q = jnp.zeros((rows, wq_ref.shape[1]), F32)
    k = jnp.zeros((rows, HEAD_DIM), F32)
    v = jnp.zeros((rows, HEAD_DIM), F32)
    for j in range(nblk):
        h = (x_ref[j].astype(F32) * scale).astype(BF16)
        h_ref[j] = h
        at = pl.ds(j * dsh, dsh)
        q = q + dot(h, wq_ref[at, :])
        k = k + dot(h, wk_ref[at, :])
        v = v + dot(h, wv_ref[at, :])
    q = q.astype(BF16)
    k = k.astype(BF16)
    v = v.astype(BF16)
    top = qh * rows
    pack_ref[pl.ds(2 * top, rows), :] = k
    pack_ref[pl.ds(2 * top + rows, rows), :] = v
    posq = lax.broadcasted_iota(jnp.int32, (rows, rows), 0)
    posk = lax.broadcasted_iota(jnp.int32, (rows, rows), 1)
    keep = ((posk <= posq) & (posk < len_ref[0])).astype(F32)
    for n in range(qh):
        qn = q[:, n * HEAD_DIM : (n + 1) * HEAD_DIM]
        pack_ref[pl.ds(n * rows, rows), :] = qn
        expo = jnp.exp(dot_nt(qn, k) * SCORE_SCALE) * keep
        weights = (expo / jnp.sum(expo, axis=1, keepdims=True)).astype(BF16)
        pack_ref[pl.ds(top + n * rows, rows), :] = weights
        o_ref[:, pl.ds(n * HEAD_DIM, HEAD_DIM)] = dot(weights, v).astype(BF16)
    o = o_ref[...]
    if mode == "ends":
        o = dot(pick_ref[...], o).astype(BF16)
    for j in range(nblk):
        part = dot(o, wo_ref[:, pl.ds(j * dsh, dsh)])
        if mode == "ends":
            place_ends(ends_ref, j, part, nstep)
            continue
        part_ref[j, :rows] = part.astype(BF16)
        if mode == "both":
            place_ends(ends_ref, j, dot(pick_ref[...], part.astype(BF16)), nstep)
    if mode == "ends":
        part_ref[...] = ends_ref[...].astype(BF16)
    elif mode == "both":
        for j in range(nblk):
            part_ref[j, rows:] = ends_ref[...].astype(BF16)


def forward(length, x, weights, mode="all", pick=None, nstep=0):
    nblk, rows, dsh = x.shape
    qcol = weights[0].shape[1]
    packed = 2 * qcol // HEAD_DIM * rows + 2 * rows
    nend = nblk * nstep
    part = {"all": x.shape, "both": (nblk, rows + nend, dsh), "ends": (nend, dsh)}[mode]
    outs = [(part, BF16), (x.shape, BF16)]
    outs += [((rows, HEAD_DIM), F32), ((packed, HEAD_DIM), BF16), ((rows, qcol), BF16)]
    more = [] if mode == "all" else [pick]
    out = pl.pallas_call(
        functools.partial(forward_kernel, mode, nstep),
        out_shape=tuple(jax.ShapeDtypeStruct(*one) for one in outs),
        in_specs=[in_smem()] + [in_vmem()] * (5 + len(more)),
        out_specs=tuple([in_vmem()] * 5),
        scratch_shapes=[pltpu.VMEM((nend, dsh), F32)] if more else [],
        compiler_params=kernel_params(VMEM_LIMIT),
        cost_estimate=pl.CostEstimate(
            flops=2 * rows * nblk * dsh * (2 * qcol + 2 * HEAD_DIM),
            bytes_accessed=4 * nblk * dsh * (qcol + HEAD_DIM),
            transcendentals=rows * rows * qcol // HEAD_DIM,
        ),
        name="forward_layer",
    )(length, x, *weights, *more)
    return dict(zip(("part", "h", "scale", "pack", "o"), out))


def step_end_kernel(nstep, factor_ref, got_ref, x_ref, pick_ref, class_ref, hot_ref, out_ref, sum_ref, row_ref):
    nblk, rows, dsh = x_ref.shape
    width = nblk * dsh
    nend = nblk * nstep
    parts = jnp.zeros((nend, dsh), F32)
    for j in range(nblk):
        parts = parts + got_ref[j, rows:].astype(F32)
    sum_ref[...] = parts
    npad = pick_ref.shape[0]
    row_ref[...] = jnp.zeros(row_ref.shape, F32)
    zeta = jnp.zeros((npad, class_ref.shape[1]), F32)
    sumsq = jnp.zeros((npad, 1), F32)
    for j in range(nblk):
        row_ref[j, :nstep] = sum_ref[pl.ds(j * nstep, nstep), :]
        full = (dot(pick_ref[...], x_ref[j]) + row_ref[j]).astype(BF16)
        ff = full.astype(F32)
        row_ref[j] = ff
        zeta = zeta + dot(full, class_ref[pl.ds(j * dsh, dsh), :])
        sumsq = sumsq + jnp.sum(ff * ff, axis=1, keepdims=True)
    rstd = lax.rsqrt(sumsq / width + EPS)
    expo = jnp.exp(zeta * rstd)
    prob = expo / jnp.sum(expo, axis=1, keepdims=True)
    dlog = factor_ref[0] * (prob - hot_ref[...])
    dzeta = dlog * rstd
    dmean = jnp.sum(dlog * zeta, axis=1, keepdims=True) * -0.5 * rstd * rstd * rstd
    high = dzeta.astype(BF16)
    mid = (dzeta - high.astype(F32)).astype(BF16)
    low = (dzeta - high.astype(F32) - mid.astype(F32)).astype(BF16)
    for j in range(nblk):
        head = class_ref[pl.ds(j * dsh, dsh), :]
        back = dot_nt(high, head) + (dot_nt(mid, head) + dot_nt(low, head))
        back = (back + dmean * 2.0 * row_ref[j] / width).astype(BF16)
        out_ref[j] = dot_tn(pick_ref[...], back).astype(BF16)


def step_end_grad(factor, got, x, pick, w_class, hot, nstep):
    nblk, rows, dsh = x.shape
    return pl.pallas_call(
        functools.partial(step_end_kernel, nstep),
        out_shape=jax.ShapeDtypeStruct(x.shape, BF16),
        in_specs=[in_smem()] + [in_vmem()] * 5,
        out_specs=in_vmem(),
        scratch_shapes=[
            pltpu.VMEM((nblk * nstep, dsh), F32),
            pltpu.VMEM((nblk, pick.shape[0], dsh), F32),
        ],
        compiler_params=kernel_params(VMEM_LIMIT),
        cost_estimate=pl.CostEstimate(
            flops=16 * rows * nblk * dsh * pick.shape[0], bytes_accessed=4 * rows * nblk * dsh,
            transcendentals=0,
        ),
        name="step_end_grad",
    )(factor, got, x, pick, w_class, hot)


def backward_kernel(
    with_input, with_ends, flag_ref, g_ref, pack0_ref, pack1_ref, h0_ref, h1_ref, scale0_ref, scale1_ref,
    wq_ref, wk_ref, wv_ref, wo_ref, *rest
):
    if with_ends:
        ends_ref, rest = rest[0], rest[1:]
    if with_input:
        d_ref, dx_ref, pack_ref, keep_sems, h_ref, scale_ref, dh_ref = rest
    else:
        d_ref, pack_ref, keep_sems = rest
    nblk, rows, dsh = g_ref.shape
    qcol = wq_ref.shape[1]
    qh = qcol // HEAD_DIM
    top = qh * rows
    pairs = [(pack0_ref, pack1_ref, pack_ref)]
    if with_input:
        pairs += [(h0_ref, h1_ref, h_ref), (scale0_ref, scale1_ref, scale_ref)]
    for at, (one, two, to) in enumerate(pairs):

        @pl.when(flag_ref[0] == 0)
        def _(one=one, to=to, at=at):
            pltpu.make_async_copy(one, to, keep_sems.at[at]).start()

        @pl.when(flag_ref[0] != 0)
        def _(two=two, to=to, at=at):
            pltpu.make_async_copy(two, to, keep_sems.at[at]).start()

    do = jnp.zeros((rows, qcol), F32)
    for j in range(nblk):
        do = do + dot_nt(g_ref[j], wo_ref[:, pl.ds(j * dsh, dsh)])
    do = do.astype(BF16)
    pltpu.make_async_copy(pack0_ref, pack_ref, keep_sems.at[0]).wait()
    k = pack_ref[pl.ds(2 * top, rows), :]
    v = pack_ref[pl.ds(2 * top + rows, rows), :]
    dk = jnp.zeros((rows, HEAD_DIM), F32)
    dv = jnp.zeros((rows, HEAD_DIM), F32)
    for n in range(qh):
        cols = slice(n * HEAD_DIM, (n + 1) * HEAD_DIM)
        qn = pack_ref[pl.ds(n * rows, rows), :]
        weights = pack_ref[pl.ds(top + n * rows, rows), :]
        don = do[:, cols]
        wf = weights.astype(F32)
        dw = dot_nt(don, v)
        ds = wf * (dw - jnp.sum(dw * wf, axis=1, keepdims=True)) * SCORE_SCALE
        ds = ds.astype(BF16)
        d_ref[:, cols] = dot(ds, k).astype(BF16)
        dk = dk + dot_tn(ds, qn)
        dv = dv + dot_tn(weights, don)
    d_ref[:, qcol : qcol + HEAD_DIM] = dk.astype(BF16)
    d_ref[:, qcol + HEAD_DIM :] = dv.astype(BF16)
    if not with_input:
        return
    pltpu.make_async_copy(h0_ref, h_ref, keep_sems.at[1]).wait()
    pltpu.make_async_copy(scale0_ref, scale_ref, keep_sems.at[2]).wait()
    dq = d_ref[:, :qcol]
    dk = dk.astype(BF16)
    dv = dv.astype(BF16)
    inner = jnp.zeros((rows, 1), F32)
    for j in range(nblk):
        at = pl.ds(j * dsh, dsh)
        dh = dot_nt(dq, wq_ref[at, :]) + dot_nt(dk, wk_ref[at, :]) + dot_nt(dv, wv_ref[at, :])
        dh_ref[j] = dh
        inner = inner + jnp.sum(dh * h_ref[j].astype(F32), axis=1, keepdims=True)
    inner = inner / (nblk * dsh)
    scale = scale_ref[:, :1]
    for j in range(nblk):
        dx_ref[j, :rows] = (scale * (dh_ref[j] - h_ref[j].astype(F32) * inner)).astype(BF16)
        if with_ends:
            dx_ref[j, rows:] = ends_ref[...]


def backward(flag, g, one, two, weights, with_input, ends=()):
    nblk, rows, dsh = g.shape
    wq, wk, wv, wo = weights
    qcol = wq.shape[1]
    out_shape = [jax.ShapeDtypeStruct((rows, qcol + 2 * HEAD_DIM), BF16)]
    scratch = [pltpu.VMEM(one["pack"].shape, BF16), pltpu.SemaphoreType.DMA((3,))]
    if with_input:
        below = sum(x.shape[0] for x in ends)
        out_shape.append(jax.ShapeDtypeStruct((nblk, rows + below, dsh), BF16))
        scratch += [
            pltpu.VMEM(g.shape, BF16),
            pltpu.VMEM(one["scale"].shape, F32),
            pltpu.VMEM(g.shape, F32),
        ]
    return pl.pallas_call(
        functools.partial(backward_kernel, with_input, bool(ends)),
        out_shape=tuple(out_shape),
        in_specs=[in_smem(), in_vmem()] + [anywhere()] * 6 + [in_vmem()] * (4 + len(ends)),
        out_specs=tuple([in_vmem()] * len(out_shape)),
        scratch_shapes=scratch,
        compiler_params=kernel_params(VMEM_LIMIT),
        cost_estimate=pl.CostEstimate(
            flops=2 * rows * nblk * dsh * (2 * qcol + 2 * HEAD_DIM),
            bytes_accessed=4 * nblk * dsh * (qcol + HEAD_DIM),
            transcendentals=0,
        ),
        name="backward_layer" if with_input else "backward_heads",
    )(
        flag, g, one["pack"], two["pack"], one["h"], two["h"],
        one["scale"], two["scale"], wq, wk, wv, wo, *ends,
    )


def rows_grad_kernel(n, splits, with_total, *refs):
    a_refs, b_refs, refs = refs[:n], refs[n : 2 * n], refs[2 * n :]
    totals, refs = (refs[: len(splits)], refs[len(splits) :]) if with_total else ((), refs)
    outs, (a_all, b_all) = refs[: len(splits)], refs[len(splits) :]
    rows = a_refs[0].shape[-2]

    def place(to, piece, i):
        at = pl.ds(i * rows, rows)
        if len(piece.shape) == 2:
            to[at, :] = piece[...]
        else:
            for b in range(piece.shape[0]):
                to[at, pl.ds(b * piece.shape[2], piece.shape[2])] = piece[b]

    for i in range(n):
        place(a_all, a_refs[i], i)
        place(b_all, b_refs[i], i)
    for c in range(a_all.shape[1] // 256):
        cols = pl.ds(c * 256, 256)
        got = dot_tn(a_all[:, cols], b_all[...])
        for i, (start, stop) in enumerate(splits):
            part = got[:, start:stop]
            outs[i][cols, :] = totals[i][cols, :] + part if with_total else part


def rows_grad(a, b, widths, totals=()):
    n = len(a)
    wide = lambda x: x.shape[-1] * (x.shape[0] if x.ndim == 3 else 1)
    rows = a[0].shape[-2]
    splits, at = [], 0
    for w in widths:
        splits.append((at, at + w))
        at += w
    return pl.pallas_call(
        functools.partial(rows_grad_kernel, n, splits, bool(totals)),
        out_shape=tuple(jax.ShapeDtypeStruct((wide(a[0]), w), F32) for w in widths),
        in_specs=[in_vmem()] * (2 * n + len(totals)),
        out_specs=tuple([in_vmem()] * len(widths)),
        scratch_shapes=[
            pltpu.VMEM((n * rows, wide(a[0])), BF16),
            pltpu.VMEM((n * rows, wide(b[0])), BF16),
        ],
        compiler_params=kernel_params(VMEM_LIMIT),
        cost_estimate=pl.CostEstimate(
            flops=2 * n * rows * wide(a[0]) * wide(b[0]),
            bytes_accessed=4 * wide(a[0]) * wide(b[0]),
            transcendentals=0,
        ),
        name="weight_grad",
    )(*a, *b, *totals)


def passed_along(x, axis, by):
    peers = lax.axis_size(axis)
    pairs = [(i, i + by) for i in range(peers) if 0 <= i + by < peers]
    return lax.ppermute(x, axis, pairs)


def swapped(x, axis, mask):
    return lax.ppermute(x, axis, [(i, i ^ mask) for i in range(lax.axis_size(axis))])


def mirrored(x, mask):
    ndp, peers = lax.axis_size("dp"), lax.axis_size("tensor")
    to = lambda p, r: (p ^ mask) * peers + (r + peers // 2) % peers
    pairs = [(p * peers + r, to(p, r)) for p in range(ndp) for r in range(peers)]
    return lax.ppermute(x, ("dp", "tensor"), pairs)


def exchange(blocks):
    return lax.all_to_all(blocks, "tensor", split_axis=0, concat_axis=0, tiled=True)


def gathered(cur):
    return exchange(jnp.broadcast_to(cur[None], (lax.axis_size("tensor"),) + cur.shape))


def by_section(masks, choices):
    out = choices[-1]
    for mask, choice in zip(masks, choices[:-1]):
        out = jnp.where(mask, choice, out)
    return out


def after(x, *marks):
    return lax.optimization_barrier((x,) + marks)[0]


def together(*xs):
    return lax.optimization_barrier(xs)


def on_device(embeds, source, lengths, bounds, targets, w_query, w_key, w_value, w_out, w_class):
    nst = lax.axis_size("section")
    peers = lax.axis_size("tensor")
    rep = lax.axis_index("dp")
    section_at = lax.axis_index("section")
    tensor_at = lax.axis_index("tensor")
    ntr, width, dsh = embeds.shape
    weights = (w_query[0], w_key[0], w_value[0], w_out[0])
    w_class = lax.all_gather(w_class, "tensor", axis=0, tiled=True)

    hi, core = rep // 2, rep % 2
    slots = source.reshape(2, 2, ntr) - rep * ntr

    def mine_for(col):
        owner = lax.dynamic_slice_in_dim(slots, col, 1, axis=1)[:, 0]
        out = jnp.zeros((2, ntr, width, dsh), BF16)
        for n in range(ntr):
            out = jnp.where((owner == n)[:, :, None, None], embeds[n][None, None], out)
        return out

    both = mine_for(core) + swapped(mine_for(1 - core), "dp", 1)
    own = lax.dynamic_slice_in_dim(both, hi, 1, axis=0)[0]
    away = lax.dynamic_slice_in_dim(both, 1 - hi, 1, axis=0)[0]
    away = [away[j] for j in range(ntr)]

    def first(j):
        return own[j] + swapped(away[j], "dp", 2)


    wanted = lax.dynamic_slice_in_dim(source, rep * ntr, ntr)
    lens = lengths[wanted]
    bnd = bounds[wanted]
    tgt = targets[wanted]
    nstep = bnd.shape[1]
    factor = (LOSS_SCALE / jnp.sum(lens).astype(F32)).reshape(1)

    def one_hot(ids, size):
        hot = ids[:, None] == jnp.arange(size, dtype=jnp.int32)[None, :]
        return jnp.concatenate([hot, jnp.zeros((16 - nstep, size), bool)], axis=0)

    picks = [one_hot(bnd[j], width).astype(BF16) for j in range(ntr)]
    hots = [one_hot(tgt[j], w_class.shape[1]).astype(F32) for j in range(ntr)]
    spans = [jnp.where(section_at == n, lens[0], lens[1]).reshape(1) for n in range(nst + 1)]
    flags = [(section_at == s).astype(jnp.int32).reshape(1) for s in range(nst)]
    masks = [section_at == s for s in range(nst)]
    quarter = peers // lax.axis_size("dp")
    starts = [((rep ^ k) * quarter).astype(jnp.uint32) for k in range(4)]
    block_at = tensor_at.astype(jnp.uint32)

    def sum_of(got):
        return jnp.sum(got[:, :width].astype(F32), axis=0)

    kept = []
    arriving = None
    for turn in range(nst):
        cur = first(turn) if turn < ntr else jnp.zeros((width, dsh), BF16)
        if turn == 0:
            cur, factor, picks, hots, spans, flags, masks, starts, block_at = together(
                cur, factor, picks, hots, spans, flags, masks, starts, block_at
            )
        if arriving is not None:
            cur, arriving = together(cur, arriving)
            cur = jnp.where(masks[0], cur, arriving)
        x = gathered(cur)
        if turn == nst - 1:
            now = forward(spans[turn], x, weights, "both", picks[0], nstep)
        else:
            now = forward(spans[turn], x, weights)
        kept.append(now)
        blocks = now["part"]
        if turn == 0:
            blocks, w_class = together(blocks, w_class)
        got = exchange(blocks)
        arriving = (cur.astype(F32) + sum_of(got)).astype(BF16)
        if turn == 0:
            away = [away[0], after(away[1], arriving)]
        arriving = passed_along(arriving, "section", 1)

    def end_cotangent(which, got, x):
        return step_end_grad(factor, got, x, picks[which], w_class, hots[which], nstep)

    def own_block(blocks):
        return lax.dynamic_slice_in_dim(blocks, block_at, 1, axis=0)[0]

    taken = {}
    g_top = end_cotangent(0, got, x)
    grad = own_block(g_top)
    arriving, g_top, grad = together(arriving, g_top, grad)
    x = gathered(arriving)
    now = forward(spans[nst], x, weights, "ends", picks[1], nstep)
    d, dx = backward(
        jnp.zeros((1,), jnp.int32), g_top, kept[-1], kept[-1], weights, True, (now["part"],)
    )
    taken[nst] = (d, g_top)
    kept.append(now)
    got = exchange(dx)

    def chosen(choices, k=None):
        if k is None:
            return by_section(masks, choices)
        cut = lambda x: lax.dynamic_slice_in_dim(x, starts[k], quarter, axis=0)
        return by_section(masks, [cut(x) for x in choices])

    def not_before(choices, mark):
        return [after(x, mark) for x in choices]

    seen = lambda name, which: [kept[s + which][name] for s in range(nst)]
    back = lambda n, which: [taken[2 * nst - 1 - s + which][n] for s in range(nst)]

    pieces = {}

    def send_quarter(name, choices, k):
        mine = chosen(choices, k)
        if k:
            mine = swapped(mine, "dp", k) if k == 1 else mirrored(mine, k)
        pieces[name, k] = mine

    def send_whole(name, choices):
        mine = chosen(choices)
        far = swapped(mine, "dp", 2)
        pieces[name, 0], pieces[name, 2] = mine, far
        pieces[name, 1], pieces[name, 3] = swapped(mine, "dp", 1), swapped(far, "dp", 1)

    widths = (weights[0].shape[1], HEAD_DIM, HEAD_DIM)
    wide_o = (quarter * dsh,)
    of = lambda name: [pieces[name, k] for k in range(4)]
    for turn in range(nst + 1, 2 * nst + 1):
        grad = (grad.astype(F32) + sum_of(got)).astype(BF16)
        hs = [not_before(seen("h", w), grad) for w in range(ntr)]
        if turn == nst + 1:
            g_top = end_cotangent(1, got, x)
            send_quarter("h0", hs[0], 2)
        elif turn == nst + 2:
            for name, which, k in (("h0", 0, 3), ("h0", 0, 1), ("h0", 0, 0), ("h1", 1, 2)):
                send_quarter(name, hs[which], k)
        elif turn == nst + 3:
            for k in (3, 1, 0):
                send_quarter("h1", hs[1], k)
            for w in range(ntr):
                send_whole(f"o{w}", not_before(seen("o", w), grad))
        else:
            for k in range(4):
                send_quarter("g0", not_before(back(1, 0), grad), k)
            send_whole("d0", not_before(back(0, 0), grad))
        grad = after(passed_along(grad, "section", -1), *pieces.values())
        if turn == nst + 1:
            grad = jnp.where(masks[nst - 1], own_block(g_top), grad)
        g = gathered(grad)
        late = 2 * nst + 1 - turn
        early = max(late - 2, 0)
        flag = flags[late - 1]
        if turn < 2 * nst:
            d, dx = backward(flag, g, kept[early], kept[late], weights, True)
            taken[turn] = (d, g)
            got = exchange(dx)
        else:
            taken[turn] = (d, g)
            for k in (2, 3, 1, 0):
                send_quarter("g1", back(1, 1), k)
            (d,) = backward(flag, g, kept[early], kept[late], weights, False)
            taken[turn] = (d, g)
            send_whole("d1", back(0, 1))

    total_qkv = rows_grad(of("h0"), of("d0"), widths)
    total_o = rows_grad(of("o0"), of("g0"), wide_o)
    (grad_o,) = rows_grad(of("o1"), of("g1"), wide_o, total_o)
    grad_q, grad_k, grad_v = rows_grad(of("h1"), of("d1"), widths, total_qkv)
    return (grad_q[None], grad_k[None], grad_v[None], grad_o[None])


def solution(mesh):
    placed = (
        P("dp", None, "tensor"),
        P(),
        P(),
        P(),
        P(),
        P("section", None, "tensor"),
        P("section", None, "tensor"),
        P("section", None, "tensor"),
        P("section", "tensor", None),
        P("tensor", None),
    )
    return jax.shard_map(
        on_device,
        mesh=mesh,
        in_specs=placed,
        out_specs=(
            P("section", "dp", "tensor"),
            P("section", "dp", "tensor"),
            P("section", "dp", "tensor"),
            P("section", "tensor", "dp"),
        ),
        check_vma=False,
    )
```

time: 552 us -> 493 us (0.89)
  blocking collectives: 69.2 us -> 262 us
  waiting for transfers between devices: 130 us -> 44.8 us
  starting transfers between devices: 141 us -> 80.2 us
  local copies, waits for them, and re-layouts: 55.9 us -> 14 us
  other arithmetic: 41.8 us -> 6.48 us
  matrix products: 13.8 us -> 0 us
  Pallas kernels: 65.9 us -> 53.7 us
    all_to_all x5 -> x17, blocking collectives: 69.2 us -> 262 us  [exchange(): lax.all_to_all(blocks, 'tensor', split_axis=0, concat_axis=0, tiled=True)]
    all_to_all x12 -> x0, starting transfers between devices: 57.3 us -> none  [exchange(): lax.all_to_all(blocks, 'tensor', split_axis=0, concat_axis=0, tiled=True)]
    all_to_all x12 -> x0, waiting for transfers between devices: 52.5 us -> none  [exchange(): lax.all_to_all(blocks, 'tensor', split_axis=0, concat_axis=0, tiled=True)]
    unnamed x192 -> x42, local copies, waits for them, and re-layouts: 39.2 us -> 9.1 us
    ppermute x19, waiting for transfers between devices: 21.9 us -> 2.57 us  [swapped(): lax.ppermute(x, axis, [(i, i ^ mask) for i in range(lax.axis_size(axis))])]
    ppermute x19, starting transfers between devices: 25 us -> 44.1 us  [swapped(): lax.ppermute(x, axis, [(i, i ^ mask) for i in range(lax.axis_size(axis))])]
    ppermute x8, starting transfers between devices: 35.2 us -> 16.9 us  [mirrored(): return lax.ppermute(x, ('dp', 'tensor'), pairs)]
    select_n x14 -> x12, other arithmetic: 18.3 us -> 1.03 us  [the longest x8 0.96 us: by_section(): out = jnp.where(mask, choice, out)]
  transfers between devices with their start and end apart: 48 -> 36, of which waited for: 28 -> 16; matrix products, arithmetic and copies ran while one was open for 7% -> 2% of each run, Pallas kernels for 3% -> 3%
where the time goes in v4:
time: 493 us; the launch traced here: 484 us
  blocking collectives  262 us (53%)
  starting transfers between devices  80.2 us (16%)
  Pallas kernels  53.7 us (11%)
  waiting for transfers between devices  44.8 us (9%)
  between operations  22.4 us (5%)
  local copies, waits for them, and re-layouts  14 us (3%)
  other arithmetic  6.48 us (1%)
    all_to_all x17, blocking collectives, exchange(): lax.all_to_all(blocks, 'tensor', split_axis=0, concat_axis=0, tiled=True)  262 us
    ppermute x19, starting transfers between devices, swapped(): lax.ppermute(x, axis, [(i, i ^ mask) for i in range(lax.axis_size(axis))])  44.1 us
    ppermute x8, waiting for transfers between devices, mirrored(): return lax.ppermute(x, ('dp', 'tensor'), pairs)  28 us
    pallas_call x5, Pallas kernels, backward(): pl.pallas_call(functools.partial(backward_kernel, with_input, bool(ends))...  24.4 us
    ppermute x8, starting transfers between devices, passed_along(): return lax.ppermute(x, axis, pairs)  19.1 us
    ppermute x8, starting transfers between devices, mirrored(): return lax.ppermute(x, ('dp', 'tensor'), pairs)  16.9 us
    pallas_call x5, Pallas kernels, forward(): pl.pallas_call(functools.partial(forward_kernel, mode, nstep), out_shape=...  16.3 us
    ppermute x8, waiting for transfers between devices, passed_along(): return lax.ppermute(x, axis, pairs)  13.5 us
  transfers between devices with their start and end apart: 36, of which 16 were waited for; matrix products, arithmetic and copies ran while one was open for 2% of the time, Pallas kernels for 3%

profile of v4, /device:TPU:1, one launch (start us, length us, event | category | flops | bytes accessed | tf_op | source)
XLA Modules:
  0.0 483.5 jit_solution(15571077692507298008)
XLA Ops:
  16.4 2.8 collective-permute-start.1
  27.8 22.9 %all_to_all.85.x_ref = bf16[8,128,512]{2,1,0:T(8,128)(2,1)S(1)} all-to-all(bf16[8,128,512]{2,1,0:T(8,128)(2,1)S(1)} %broadcast_in_dim.134), channel_id=1, replica_groups=mesh['dp'=4,'section'=4,'tensor'=8] {'tensor'}, dimensions={0} | all-to-all | bytes 2097152 | tf_op jit(solution)/shard_map/all_to_all | solution.py:363
  55.1 3.0 forward_layer.5
  59.7 17.5 %all_to_all.86 = bf16[8,128,512]{2,1,0:T(8,128)(2,1)S(1)} all-to-all(bf16[8,128,512]{2,1,0:T(8,128)(2,1)} %copy-done.10), channel_id=1, replica_groups=mesh['dp'=4,'section'=4,'tensor'=8] {'tensor'}, dimensions={0} | all-to-all | bytes 2097152 | tf_op jit(solution)/shard_map/all_to_all | solution.py:363
  77.5 3.0 collective-permute-start.2
  84.8 14.3 %all_to_all.87.x_ref = bf16[8,128,512]{2,1,0:T(8,128)(2,1)S(1)} all-to-all(bf16[8,128,512]{2,1,0:T(8,128)(2,1)S(1)} %broadcast_in_dim.135), channel_id=1, replica_groups=mesh['dp'=4,'section'=4,'tensor'=8] {'tensor'}, dimensions={0} | all-to-all | bytes 2097152 | tf_op jit(solution)/shard_map/all_to_all | solution.py:363
  101.2 3.0 forward_layer.6
  104.2 13.2 %all_to_all.88 = bf16[8,128,512]{2,1,0:T(8,128)(2,1)S(1)} all-to-all(bf16[8,128,512]{2,1,0:T(8,128)(2,1)S(1)} %get-tuple-element.120), channel_id=1, replica_groups=mesh['dp'=4,'section'=4,'tensor'=8] {'tensor'}, dimensions={0} | all-to-all | bytes 2097152 | tf_op jit(solution)/shard_map/all_to_all | solution.py:363
  117.6 4.1 collective-permute-start.4
  123.8 13.5 %all_to_all.89.x_ref = bf16[8,128,512]{2,1,0:T(8,128)(2,1)S(1)} all-to-all(bf16[8,128,512]{2,1,0:T(8,128)(2,1)S(1)} %broadcast_in_dim.136), channel_id=1, replica_groups=mesh['dp'=4,'section'=4,'tensor'=8] {'tensor'}, dimensions={0} | all-to-all | bytes 2097152 | tf_op jit(solution)/shard_map/all_to_all | solution.py:363
  137.3 3.0 forward_layer.7
  140.3 12.9 %all_to_all.90 = bf16[8,128,512]{2,1,0:T(8,128)(2,1)S(1)} all-to-all(bf16[8,128,512]{2,1,0:T(8,128)(2,1)S(1)} %get-tuple-element.124), channel_id=1, replica_groups=mesh['dp'=4,'section'=4,'tensor'=8] {'tensor'}, dimensions={0} | all-to-all | bytes 2097152 | tf_op jit(solution)/shard_map/all_to_all | solution.py:363
  153.3 3.6 collective-permute-start.5
  159.0 12.9 %all_to_all.91.x_ref = bf16[8,128,512]{2,1,0:T(8,128)(2,1)S(1)} all-to-all(bf16[8,128,512]{2,1,0:T(8,128)(2,1)S(1)} %broadcast_in_dim.137), channel_id=1, replica_groups=mesh['dp'=4,'section'=4,'tensor'=8] {'tensor'}, dimensions={0} | all-to-all | bytes 2097152 | tf_op jit(solution)/shard_map/all_to_all | solution.py:363
  171.9 4.3 forward_layer.8
  176.2 14.3 %all_to_all.92.got_ref = bf16[8,160,512]{2,1,0:T(8,128)(2,1)S(1)} all-to-all(bf16[8,160,512]{2,1,0:T(8,128)(2,1)S(1)} %get-tuple-element.131), channel_id=1, replica_groups=mesh['dp'=4,'section'=4,'tensor'=8] {'tensor'}, dimensions={0} | all-to-all | bytes 2621440 | tf_op jit(solution)/shard_map/all_to_all | solution.py:363
  190.6 4.1 collective-permute-start.6
  194.7 3.2 step_end_grad.2.g_ref
  198.1 12.7 %all_to_all.93.x_ref = bf16[8,128,512]{2,1,0:T(8,128)(2,1)S(1)} all-to-all(bf16[8,128,512]{2,1,0:T(8,128)(2,1)S(1)} %broadcast_in_dim.138), channel_id=1, replica_groups=mesh['dp'=4,'section'=4,'tensor'=8] {'tensor'}, dimensions={0} | all-to-all | bytes 2097152 | tf_op jit(solution)/shard_map/all_to_all | solution.py:363
  210.8 3.1 forward_layer.9
  213.9 5.3 %backward_layer.4 = (bf16[128,768]{1,0:T(8,128)(2,1)S(1)}, bf16[8,160,512]{2,1,0:T(8,128)(2,1)S(1)}) custom-call(s32[1]{0:T(128)} %constant.61.clone.1.flag_ref, bf16[8,128,512]{2,1,0:T(8,128)(2,1)S(1)} %step_end_grad.2.g_ref, bf16[1280,128]{1,0:T(8,128)(2,1)S(1)} %get-tuple-element.136.pack0_ref.pack1_ref, ...), custom_call_target="tpu_custom_call" | custom-call | flops 1342177280 | bytes 10485760 | tf_op jit(solution)/shard_map/backward_layer/pallas_call | solution.py:274
  219.2 14.1 %all_to_all.94.got_ref = bf16[8,160,512]{2,1,0:T(8,128)(2,1)S(1)} all-to-all(bf16[8,160,512]{2,1,0:T(8,128)(2,1)S(1)} %get-tuple-element.142), channel_id=1, replica_groups=mesh['dp'=4,'section'=4,'tensor'=8] {'tensor'}, dimensions={0} | all-to-all | bytes 2621440 | tf_op jit(solution)/shard_map/all_to_all | solution.py:363
  233.6 3.1 collective-permute-start.8
  238.0 3.2 step_end_grad.3
  242.9 12.7 %all_to_all.95.g_ref = bf16[8,128,512]{2,1,0:T(8,128)(2,1)S(1)} all-to-all(bf16[8,128,512]{2,1,0:T(8,128)(2,1)S(1)} %broadcast_in_dim.139), channel_id=1, replica_groups=mesh['dp'=4,'section'=4,'tensor'=8] {'tensor'}, dimensions={0} | all-to-all | bytes 2097152 | tf_op jit(solution)/shard_map/all_to_all | solution.py:363
  255.6 5.5 %backward_layer.5 = (bf16[128,768]{1,0:T(8,128)(2,1)S(1)}, bf16[8,128,512]{2,1,0:T(8,128)(2,1)S(1)}) custom-call(s32[1]{0:T(128)} %bitcast.19.flag_ref, bf16[8,128,512]{2,1,0:T(8,128)(2,1)S(1)} %all_to_all.95.g_ref, bf16[1280,128]{1,0:T(8,128)(2,1)S(1)} %get-tuple-element.156.pack0_ref.pack1_ref, bf16[1280,128]{1,0:T(8,128)(2,1)S(1)} %get-tuple-element.157.pack1_ref, ...), custom_call_target="tpu_custom_call" | custom-call | flops 1342177280 | bytes 10485760 | tf_op jit(solution)/shard_map/backward_layer/pallas_call | solution.py:274
  261.1 16.7 %all_to_all.96 = bf16[8,128,512]{2,1,0:T(8,128)(2,1)S(1)} all-to-all(bf16[8,128,512]{2,1,0:T(8,128)(2,1)S(1)} %get-tuple-element.161), channel_id=1, replica_groups=mesh['dp'=4,'section'=4,'tensor'=8] {'tensor'}, dimensions={0} | all-to-all | bytes 2097152 | tf_op jit(solution)/shard_map/all_to_all | solution.py:363
  278.2 18.8 %collective-permute-start.11 = (bf16[2,128,512]{2,1,0:T(8,128)(2,1)S(1)}, bf16[2,128,512]{2,1,0:T(8,128)(2,1)S(1)}, u32[]{:S(2)}, u32[]{:S(2)}) collective-permute-start(bf16[2,128,512]{2,1,0:T(8,128)(2,1)S(1)} %get-tuple-element.226), channel_id=1, source_target_pairs={{0,32},{32,0},{64,96},{96,64},{1,33},{33,1},{65,97},{97,65},{2,34}... | collective-permute-start | bytes 786440 | tf_op jit(solution)/shard_map/ppermute | solution.py:352
  300.9 5.0 %collective-permute-done.9 = bf16[128,512]{1,0:T(8,128)(2,1)S(1)} collective-permute-done((bf16[128,512]{1,0:T(8,128)(2,1)S(1)}, bf16[128,512]{1,0:T(8,128)(2,1)S(1)}, u32[]{:S(2)}, u32[]{:S(2)}) %collective-permute-start.9) | collective-permute-done | bytes 131104 | tf_op jit(solution)/shard_map/ppermute | solution.py:348
  306.7 4.8 collective-permute-done.12.refs_2_
  311.6 16.7 %all_to_all.97.g_ref = bf16[8,128,512]{2,1,0:T(8,128)(2,1)S(1)} all-to-all(bf16[8,128,512]{2,1,0:T(8,128)(2,1)S(1)} %broadcast_in_dim.140), channel_id=1, replica_groups=mesh['dp'=4,'section'=4,'tensor'=8] {'tensor'}, dimensions={0} | all-to-all | bytes 2097152 | tf_op jit(solution)/shard_map/all_to_all | solution.py:363
  328.3 5.3 %backward_layer.6 = (bf16[128,768]{1,0:T(8,128)(2,1)S(1)}, bf16[8,128,512]{2,1,0:T(8,128)(2,1)S(1)}) custom-call(s32[1]{0:T(128)} %bitcast.18.flag_ref, bf16[8,128,512]{2,1,0:T(8,128)(2,1)S(1)} %all_to_all.97.g_ref, bf16[1280,128]{1,0:T(8,128)(2,1)S(1)} %get-tuple-element.172.pack0_ref.pack1_ref, ...), custom_call_target="tpu_custom_call" | custom-call | flops 1342177280 | bytes 10485760 | tf_op jit(solution)/shard_map/backward_layer/pallas_call | solution.py:274
  333.6 15.8 %all_to_all.98 = bf16[8,128,512]{2,1,0:T(8,128)(2,1)S(1)} all-to-all(bf16[8,128,512]{2,1,0:T(8,128)(2,1)S(1)} %get-tuple-element.174), channel_id=1, replica_groups=mesh['dp'=4,'section'=4,'tensor'=8] {'tensor'}, dimensions={0} | all-to-all | bytes 2097152 | tf_op jit(solution)/shard_map/all_to_all | solution.py:363
  349.7 3.8 collective-permute-start.20
  366.1 2.8 collective-permute-done.14.refs_3_
  369.1 16.8 %all_to_all.99.g_ref = bf16[8,128,512]{2,1,0:T(8,128)(2,1)S(1)} all-to-all(bf16[8,128,512]{2,1,0:T(8,128)(2,1)S(1)} %broadcast_in_dim.141), channel_id=1, replica_groups=mesh['dp'=4,'section'=4,'tensor'=8] {'tensor'}, dimensions={0} | all-to-all | bytes 2097152 | tf_op jit(solution)/shard_map/all_to_all | solution.py:363
  385.8 5.6 %backward_layer.7 = (bf16[128,768]{1,0:T(8,128)(2,1)S(1)}, bf16[8,128,512]{2,1,0:T(8,128)(2,1)S(1)}) custom-call(s32[1]{0:T(128)} %bitcast.17.flag_ref, bf16[8,128,512]{2,1,0:T(8,128)(2,1)S(1)} %all_to_all.99.g_ref, bf16[1280,128]{1,0:T(8,128)(2,1)S(1)} %get-tuple-element.192.pack0_ref, bf16[1280,128]{1,0:T(8,128)(2,1)S(1)} %get-tuple-element.156.pack0_ref.pack1_ref, ...), custom_call_target="tpu_custom_call" | custom-call | flops 1342177280 | bytes 10485760 | tf_op jit(solution)/shard_map/backward_layer/pallas_call | solution.py:274
  391.4 18.2 %all_to_all.100 = bf16[8,128,512]{2,1,0:T(8,128)(2,1)S(1)} all-to-all(bf16[8,128,512]{2,1,0:T(8,128)(2,1)S(1)} %get-tuple-element.196), channel_id=1, replica_groups=mesh['dp'=4,'section'=4,'tensor'=8] {'tensor'}, dimensions={0} | all-to-all | bytes 2097152 | tf_op jit(solution)/shard_map/all_to_all | solution.py:363
  412.6 4.2 collective-permute-start.25
  420.9 5.0 %collective-permute-done.25.refs_7_ = bf16[2,128,512]{2,1,0:T(8,128)(2,1)S(1)} collective-permute-done((bf16[2,128,512]{2,1,0:T(8,128)(2,1)S(1)}, bf16[2,128,512]{2,1,0:T(8,128)(2,1)S(1)}, u32[]{:S(2)}, u32[]{:S(2)}) %collective-permute-start.25) | collective-permute-done | bytes 262176 | tf_op jit(solution)/shard_map/ppermute | solution.py:359
  426.0 5.6 %collective-permute-done.24.refs_6_ = bf16[2,128,512]{2,1,0:T(8,128)(2,1)S(1)} collective-permute-done((bf16[2,128,512]{2,1,0:T(8,128)(2,1)S(1)}, bf16[2,128,512]{2,1,0:T(8,128)(2,1)S(1)}, u32[]{:S(2)}, u32[]{:S(2)}) %collective-permute-start.24) | collective-permute-done | bytes 262176 | tf_op jit(solution)/shard_map/ppermute | solution.py:359
  431.7 16.9 %all_to_all.101.g_ref = bf16[8,128,512]{2,1,0:T(8,128)(2,1)S(1)} all-to-all(bf16[8,128,512]{2,1,0:T(8,128)(2,1)S(1)} %broadcast_in_dim.142), channel_id=1, replica_groups=mesh['dp'=4,'section'=4,'tensor'=8] {'tensor'}, dimensions={0} | all-to-all | bytes 2097152 | tf_op jit(solution)/shard_map/all_to_all | solution.py:363
  448.5 2.7 backward_heads.1
  452.4 4.3 collective-permute-start.34
  458.0 2.7 collective-permute-start.31
  462.4 3.3 collective-permute-done.34.refs_7_
  465.8 5.6 %collective-permute-done.33.refs_6_ = bf16[2,128,512]{2,1,0:T(8,128)(2,1)S(1)} collective-permute-done((bf16[2,128,512]{2,1,0:T(8,128)(2,1)S(1)}, bf16[2,128,512]{2,1,0:T(8,128)(2,1)S(1)}, u32[]{:S(2)}, u32[]{:S(2)}) %collective-permute-start.33) | collective-permute-done | bytes 262176 | tf_op jit(solution)/shard_map/ppermute | solution.py:359
  473.5 2.7 weight_grad.5
  (163 shorter events, 62.5 us)
Async XLA Ops:
  7.2 7.5 %copy-start.18 = (s32[8,4]{0,1:T(4,128)S(1)}, s32[8,4]{0,1:T(4,128)}, u32[]{:S(2)}) copy-start(s32[8,4]{0,1:T(4,128)} %param.14) | copy-start | bytes 388
  7.2 52.6 %all-gather.2.cloned.1.call-start = ((), (), s32[]{:S(2)}) async-start(), calls=%async_computation.17 | async-start | bytes 1179648 | tf_op jit(solution)/shard_map/all_gather | solution.py:393
  9.9 5.6 %collective-permute-start = (bf16[2,2,128,512]{3,2,1,0:T(8,128)(2,1)S(1)}, bf16[2,2,128,512]{3,2,1,0:T(8,128)(2,1)S(1)}, u32[]{:S(2)}, u32[]{:S(2)}) collective-permute-start(bf16[2,2,128,512]{3,2,1,0:T(8,128)(2,1)S(1)} %select_select_fusion), channel_id=1, source_target_pairs={{0,32},{32,0},{64,96},{96,64},{1,33},{33,1},{65,97},{97,65},{2,34}... | collective-permute-start | bytes 1572872 | tf_op jit(solution)/shard_map/ppermute | solution.py:352
  15.6 35.1 %copy-start.14 = (bf16[2,2,128,512]{3,2,1,0:T(8,128)(2,1)}, bf16[2,2,128,512]{3,2,1,0:T(8,128)(2,1)S(1)}, u32[]{:S(2)}) copy-start(bf16[2,2,128,512]{3,2,1,0:T(8,128)(2,1)S(1)} %select_add_fusion) | copy-start | bytes 1572868
  15.6 35.1 %copy-start.7 = (bf16[1,4096,128]{2,1,0:T(8,128)(2,1)S(1)}, bf16[1,4096,128]{2,1,0:T(8,128)(2,1)}, u32[]{:S(2)}) copy-start(bf16[1,4096,128]{2,1,0:T(8,128)(2,1)} %param.16) | copy-start | bytes 3145732
  15.7 35.1 %copy-start.8 = (bf16[1,4096,128]{2,1,0:T(8,128)(2,1)S(1)}, bf16[1,4096,128]{2,1,0:T(8,128)(2,1)}, u32[]{:S(2)}) copy-start(bf16[1,4096,128]{2,1,0:T(8,128)(2,1)} %param.17) | copy-start | bytes 3145732
  16.4 11.3 %collective-permute-start.1 = (bf16[128,512]{1,0:T(8,128)(2,1)S(1)}, bf16[128,512]{1,0:T(8,128)(2,1)S(1)}, u32[]{:S(2)}, u32[]{:S(2)}) collective-permute-start(bf16[128,512]{1,0:T(8,128)(2,1)S(1)} %get-tuple-element.230), channel_id=1, source_target_pairs={{0,64},{32,96},{64,0},{96,32},{1,65},{33,97},{65,1},{97,33},{2,66}... | collective-permute-start | bytes 393224 | tf_op jit(solution)/shard_map/ppermute | solution.py:352
  27.7 23.0 %copy-start.15 = (bf16[128,512]{1,0:T(8,128)(2,1)}, bf16[128,512]{1,0:T(8,128)(2,1)S(1)}, u32[]{:S(2)}) copy-start(bf16[128,512]{1,0:T(8,128)(2,1)S(1)} %fusion.1) | copy-start | bytes 393220
  59.7 17.7 %copy-start.16 = (bf16[128,512]{1,0:T(8,128)(2,1)S(1)}, bf16[128,512]{1,0:T(8,128)(2,1)}, u32[]{:S(2)}) copy-start(bf16[128,512]{1,0:T(8,128)(2,1)} %copy-done.15) | copy-start | bytes 393220
  59.7 17.7 %copy-start.17 = (bf16[128,512]{1,0:T(8,128)(2,1)S(1)}, bf16[128,512]{1,0:T(8,128)(2,1)}, u32[]{:S(2)}) copy-start(bf16[128,512]{1,0:T(8,128)(2,1)} %get-tuple-element.116) | copy-start | bytes 393220
  77.4 21.6 %copy-start.3 = (bf16[1,4096,512]{2,1,0:T(8,128)(2,1)S(1)}, bf16[1,4096,512]{2,1,0:T(8,128)(2,1)}, u32[]{:S(2)}) copy-start(bf16[1,4096,512]{2,1,0:T(8,128)(2,1)} %param.15) | copy-start | bytes 12582916
  77.5 5.4 %collective-permute-start.2 = (bf16[128,512]{1,0:T(8,128)(2,1)S(1)}, bf16[128,512]{1,0:T(8,128)(2,1)S(1)}, u32[]{:S(2)}, u32[]{:S(2)}) collective-permute-start(bf16[128,512]{1,0:T(8,128)(2,1)S(1)} %copy-done.17), channel_id=1, source_target_pairs={{0,64},{32,96},{64,0},{96,32},{1,65},{33,97},{65,1},{97,33},{2,66}... | collective-permute-start | bytes 393224 | tf_op jit(solution)/shard_map/ppermute | solution.py:352
  80.5 4.2 collective-permute-start.3
  117.6 6.0 %collective-permute-start.4 = (bf16[128,512]{1,0:T(8,128)(2,1)S(1)}, bf16[128,512]{1,0:T(8,128)(2,1)S(1)}, u32[]{:S(2)}, u32[]{:S(2)}) collective-permute-start(bf16[128,512]{1,0:T(8,128)(2,1)S(1)} %add_convert_fusion.6), channel_id=1, source_target_pairs={{0,8},{8,16},{16,24},{1,9},{9,17},{17,25},{2,10},{10,18},{18,26},{... | collective-permute-start | bytes 393224 | tf_op jit(solution)/shard_map/ppermute | solution.py:348
  153.3 5.5 %collective-permute-start.5 = (bf16[128,512]{1,0:T(8,128)(2,1)S(1)}, bf16[128,512]{1,0:T(8,128)(2,1)S(1)}, u32[]{:S(2)}, u32[]{:S(2)}) collective-permute-start(bf16[128,512]{1,0:T(8,128)(2,1)S(1)} %add_convert_fusion.5), channel_id=1, source_target_pairs={{0,8},{8,16},{16,24},{1,9},{9,17},{17,25},{2,10},{10,18},{18,26},{... | collective-permute-start | bytes 393224 | tf_op jit(solution)/shard_map/ppermute | solution.py:348
  176.2 18.5 %copy-start.9 = (bf16[4096,128]{1,0:T(8,128)(2,1)S(1)}, bf16[4096,128]{1,0:T(8,128)(2,1)}, u32[]{:S(2)}) copy-start(bf16[4096,128]{1,0:T(8,128)(2,1)} %all-gather.2.cloned.1.call-done.class_ref) | copy-start | bytes 3145732
  176.2 18.5 %copy-start.13 = (f32[16,128]{1,0:T(8,128)S(1)}, f32[16,128]{1,0:T(8,128)}, u32[]{:S(2)}) copy-start(f32[16,128]{1,0:T(8,128)} %pad_convert_fusion.1.hot_ref) | copy-start | bytes 24580
  190.6 7.4 %collective-permute-start.6 = (bf16[128,512]{1,0:T(8,128)(2,1)S(1)}, bf16[128,512]{1,0:T(8,128)(2,1)S(1)}, u32[]{:S(2)}, u32[]{:S(2)}) collective-permute-start(bf16[128,512]{1,0:T(8,128)(2,1)S(1)} %add_convert_fusion.4), channel_id=1, source_target_pairs={{0,8},{8,16},{16,24},{1,9},{9,17},{17,25},{2,10},{10,18},{18,26},{... | collective-permute-start | bytes 393224 | tf_op jit(solution)/shard_map/ppermute | solution.py:348
  194.7 16.1 %copy-start.6 = (bf16[1,512,4096]{2,1,0:T(8,128)(2,1)S(1)}, bf16[1,512,4096]{2,1,0:T(8,128)(2,1)}, u32[]{:S(2)}) copy-start(bf16[1,512,4096]{2,1,0:T(8,128)(2,1)} %param.18) | copy-start | bytes 12582916
  233.6 9.2 %collective-permute-start.8 = (bf16[2,128,512]{2,1,0:T(8,128)(2,1)S(1)}, bf16[2,128,512]{2,1,0:T(8,128)(2,1)S(1)}, u32[]{:S(2)}, u32[]{:S(2)}) collective-permute-start(bf16[2,128,512]{2,1,0:T(8,128)(2,1)S(1)} %select_select_fusion.16), channel_id=1, source_target_pairs={{0,68},{1,69},{2,70},{3,71},{4,64},{5,65},{6,66},{7,67},{32,100},{... | collective-permute-start | bytes 786440 | tf_op jit(solution)/shard_map/ppermute | solution.py:359
  236.7 6.0 %collective-permute-start.7 = (bf16[128,512]{1,0:T(8,128)(2,1)S(1)}, bf16[128,512]{1,0:T(8,128)(2,1)S(1)}, u32[]{:S(2)}, u32[]{:S(2)}) collective-permute-start(bf16[128,512]{1,0:T(8,128)(2,1)S(1)} %add_convert_fusion.3), channel_id=1, source_target_pairs={{8,0},{16,8},{24,16},{9,1},{17,9},{25,17},{10,2},{18,10},{26,18},{... | collective-permute-start | bytes 393224 | tf_op jit(solution)/shard_map/ppermute | solution.py:348
  278.2 27.7 %collective-permute-start.11 = (bf16[2,128,512]{2,1,0:T(8,128)(2,1)S(1)}, bf16[2,128,512]{2,1,0:T(8,128)(2,1)S(1)}, u32[]{:S(2)}, u32[]{:S(2)}) collective-permute-start(bf16[2,128,512]{2,1,0:T(8,128)(2,1)S(1)} %get-tuple-element.226), channel_id=1, source_target_pairs={{0,32},{32,0},{64,96},{96,64},{1,33},{33,1},{65,97},{97,65},{2,34}... | collective-permute-start | bytes 786440 | tf_op jit(solution)/shard_map/ppermute | solution.py:352
  296.9 9.8 %collective-permute-start.10 = (bf16[2,128,512]{2,1,0:T(8,128)(2,1)S(1)}, bf16[2,128,512]{2,1,0:T(8,128)(2,1)S(1)}, u32[]{:S(2)}, u32[]{:S(2)}) collective-permute-start(bf16[2,128,512]{2,1,0:T(8,128)(2,1)S(1)} %get-tuple-element.227), channel_id=1, source_target_pairs={{0,100},{1,101},{2,102},{3,103},{4,96},{5,97},{6,98},{7,99},{32,68... | collective-permute-start | bytes 786440 | tf_op jit(solution)/shard_map/ppermute | solution.py:359
  297.4 14.1 %collective-permute-start.12 = (bf16[2,128,512]{2,1,0:T(8,128)(2,1)S(1)}, bf16[2,128,512]{2,1,0:T(8,128)(2,1)S(1)}, u32[]{:S(2)}, u32[]{:S(2)}) collective-permute-start(bf16[2,128,512]{2,1,0:T(8,128)(2,1)S(1)} %get-tuple-element.228), channel_id=1, source_target_pairs={{0,68},{1,69},{2,70},{3,71},{4,64},{5,65},{6,66},{7,67},{32,100},{... | collective-permute-start | bytes 786440 | tf_op jit(solution)/shard_map/ppermute | solution.py:359
  299.6 6.3 %collective-permute-start.9 = (bf16[128,512]{1,0:T(8,128)(2,1)S(1)}, bf16[128,512]{1,0:T(8,128)(2,1)S(1)}, u32[]{:S(2)}, u32[]{:S(2)}) collective-permute-start(bf16[128,512]{1,0:T(8,128)(2,1)S(1)} %add_convert_fusion.2), channel_id=1, source_target_pairs={{8,0},{16,8},{24,16},{9,1},{17,9},{25,17},{10,2},{18,10},{26,18},{... | collective-permute-start | bytes 393224 | tf_op jit(solution)/shard_map/ppermute | solution.py:348
  333.6 16.0 %copy-start.12 = (bf16[128,512]{1,0:T(8,128)(2,1)S(1)}, bf16[128,512]{1,0:T(8,128)(2,1)}, u32[]{:S(2)}) copy-start(bf16[128,512]{1,0:T(8,128)(2,1)} %copy-done.11) | copy-start | bytes 393220
  349.7 8.0 %collective-permute-start.20 = (bf16[128,512]{1,0:T(8,128)(2,1)S(1)}, bf16[128,512]{1,0:T(8,128)(2,1)S(1)}, u32[]{:S(2)}, u32[]{:S(2)}) collective-permute-start(bf16[128,512]{1,0:T(8,128)(2,1)S(1)} %get-tuple-element.231.refs_0_), channel_id=1, source_target_pairs={{0,32},{32,0},{64,96},{96,64},{1,33},{33,1},{65,97},{97,65},{2,34}... | collective-permute-start | bytes 393224 | tf_op jit(solution)/shard_map/ppermute | solution.py:352
  353.5 6.6 %collective-permute-start.19 = (bf16[128,512]{1,0:T(8,128)(2,1)S(1)}, bf16[128,512]{1,0:T(8,128)(2,1)S(1)}, u32[]{:S(2)}, u32[]{:S(2)}) collective-permute-start(bf16[128,512]{1,0:T(8,128)(2,1)S(1)} %get-tuple-element.231.refs_0_), channel_id=1, source_target_pairs={{0,64},{32,96},{64,0},{96,32},{1,65},{33,97},{65,1},{97,33},{2,66}... | collective-permute-start | bytes 393224 | tf_op jit(solution)/shard_map/ppermute | solution.py:352
  354.7 6.7 %collective-permute-start.17 = (bf16[128,512]{1,0:T(8,128)(2,1)S(1)}, bf16[128,512]{1,0:T(8,128)(2,1)S(1)}, u32[]{:S(2)}, u32[]{:S(2)}) collective-permute-start(bf16[128,512]{1,0:T(8,128)(2,1)S(1)} %get-tuple-element.232.refs_0_), channel_id=1, source_target_pairs={{0,32},{32,0},{64,96},{96,64},{1,33},{33,1},{65,97},{97,65},{2,34}... | collective-permute-start | bytes 393224 | tf_op jit(solution)/shard_map/ppermute | solution.py:352
  355.1 7.8 %collective-permute-start.16 = (bf16[128,512]{1,0:T(8,128)(2,1)S(1)}, bf16[128,512]{1,0:T(8,128)(2,1)S(1)}, u32[]{:S(2)}, u32[]{:S(2)}) collective-permute-start(bf16[128,512]{1,0:T(8,128)(2,1)S(1)} %get-tuple-element.232.refs_0_), channel_id=1, source_target_pairs={{0,64},{32,96},{64,0},{96,32},{1,65},{33,97},{65,1},{97,33},{2,66}... | collective-permute-start | bytes 393224 | tf_op jit(solution)/shard_map/ppermute | solution.py:352
  357.0 11.9 %collective-permute-start.14 = (bf16[2,128,512]{2,1,0:T(8,128)(2,1)S(1)}, bf16[2,128,512]{2,1,0:T(8,128)(2,1)S(1)}, u32[]{:S(2)}, u32[]{:S(2)}) collective-permute-start(bf16[2,128,512]{2,1,0:T(8,128)(2,1)S(1)} %get-tuple-element.222), channel_id=1, source_target_pairs={{0,100},{1,101},{2,102},{3,103},{4,96},{5,97},{6,98},{7,99},{32,68... | collective-permute-start | bytes 786440 | tf_op jit(solution)/shard_map/ppermute | solution.py:359
  357.7 11.2 %collective-permute-start.13 = (bf16[2,128,512]{2,1,0:T(8,128)(2,1)S(1)}, bf16[2,128,512]{2,1,0:T(8,128)(2,1)S(1)}, u32[]{:S(2)}, u32[]{:S(2)}) collective-permute-start(bf16[2,128,512]{2,1,0:T(8,128)(2,1)S(1)} %get-tuple-element.223), channel_id=1, source_target_pairs={{0,32},{32,0},{64,96},{96,64},{1,33},{33,1},{65,97},{97,65},{2,34}... | collective-permute-start | bytes 786440 | tf_op jit(solution)/shard_map/ppermute | solution.py:352
  360.1 6.0 %collective-permute-start.15 = (bf16[128,512]{1,0:T(8,128)(2,1)S(1)}, bf16[128,512]{1,0:T(8,128)(2,1)S(1)}, u32[]{:S(2)}, u32[]{:S(2)}) collective-permute-start(bf16[128,512]{1,0:T(8,128)(2,1)S(1)} %add_convert_fusion.1), channel_id=1, source_target_pairs={{8,0},{16,8},{24,16},{9,1},{17,9},{25,17},{10,2},{18,10},{26,18},{... | collective-permute-start | bytes 393224 | tf_op jit(solution)/shard_map/ppermute | solution.py:348
  361.4 4.7 collective-permute-start.21
  362.9 3.2 collective-permute-start.18
  409.8 8.1 %collective-permute-start.22 = (bf16[128,512]{1,0:T(8,128)(2,1)S(1)}, bf16[128,512]{1,0:T(8,128)(2,1)S(1)}, u32[]{:S(2)}, u32[]{:S(2)}) collective-permute-start(bf16[128,512]{1,0:T(8,128)(2,1)S(1)} %add_convert_fusion), channel_id=1, source_target_pairs={{8,0},{16,8},{24,16},{9,1},{17,9},{25,17},{10,2},{18,10},{26,18},{... | collective-permute-start | bytes 393224 | tf_op jit(solution)/shard_map/ppermute | solution.py:348
  411.1 7.9 %collective-permute-start.26 = (bf16[128,768]{1,0:T(8,128)(2,1)S(1)}, bf16[128,768]{1,0:T(8,128)(2,1)S(1)}, u32[]{:S(2)}, u32[]{:S(2)}) collective-permute-start(bf16[128,768]{1,0:T(8,128)(2,1)S(1)} %select_select_fusion.18.refs_4_), channel_id=1, source_target_pairs={{0,64},{32,96},{64,0},{96,32},{1,65},{33,97},{65,1},{97,33},{2,66}... | collective-permute-start | bytes 589832 | tf_op jit(solution)/shard_map/ppermute | solution.py:352
  412.6 13.4 %collective-permute-start.25 = (bf16[2,128,512]{2,1,0:T(8,128)(2,1)S(1)}, bf16[2,128,512]{2,1,0:T(8,128)(2,1)S(1)}, u32[]{:S(2)}, u32[]{:S(2)}) collective-permute-start(bf16[2,128,512]{2,1,0:T(8,128)(2,1)S(1)} %get-tuple-element.218), channel_id=1, source_target_pairs={{0,100},{1,101},{2,102},{3,103},{4,96},{5,97},{6,98},{7,99},{32,68... | collective-permute-start | bytes 786440 | tf_op jit(solution)/shard_map/ppermute | solution.py:359
  416.8 14.8 %collective-permute-start.24 = (bf16[2,128,512]{2,1,0:T(8,128)(2,1)S(1)}, bf16[2,128,512]{2,1,0:T(8,128)(2,1)S(1)}, u32[]{:S(2)}, u32[]{:S(2)}) collective-permute-start(bf16[2,128,512]{2,1,0:T(8,128)(2,1)S(1)} %get-tuple-element.219), channel_id=1, source_target_pairs={{0,68},{1,69},{2,70},{3,71},{4,64},{5,65},{6,66},{7,67},{32,100},{... | collective-permute-start | bytes 786440 | tf_op jit(solution)/shard_map/ppermute | solution.py:359
  417.9 13.7 %collective-permute-start.23 = (bf16[2,128,512]{2,1,0:T(8,128)(2,1)S(1)}, bf16[2,128,512]{2,1,0:T(8,128)(2,1)S(1)}, u32[]{:S(2)}, u32[]{:S(2)}) collective-permute-start(bf16[2,128,512]{2,1,0:T(8,128)(2,1)S(1)} %get-tuple-element.220), channel_id=1, source_target_pairs={{0,32},{32,0},{64,96},{96,64},{1,33},{33,1},{65,97},{97,65},{2,34}... | collective-permute-start | bytes 786440 | tf_op jit(solution)/shard_map/ppermute | solution.py:352
  417.9 3.0 collective-permute-start.27
  419.1 12.5 %collective-permute-start.28 = (bf16[128,768]{1,0:T(8,128)(2,1)S(1)}, bf16[128,768]{1,0:T(8,128)(2,1)S(1)}, u32[]{:S(2)}, u32[]{:S(2)}) collective-permute-start(bf16[128,768]{1,0:T(8,128)(2,1)S(1)} %collective-permute-done.26.refs_6_), channel_id=1, source_target_pairs={{0,32},{32,0},{64,96},{96,64},{1,33},{33,1},{65,97},{97,65},{2,34}... | collective-permute-start | bytes 589832 | tf_op jit(solution)/shard_map/ppermute | solution.py:352
  451.3 6.8 %collective-permute-start.30 = (bf16[128,768]{1,0:T(8,128)(2,1)S(1)}, bf16[128,768]{1,0:T(8,128)(2,1)S(1)}, u32[]{:S(2)}, u32[]{:S(2)}) collective-permute-start(bf16[128,768]{1,0:T(8,128)(2,1)S(1)} %select_select_fusion.17.refs_4_), channel_id=1, source_target_pairs={{0,64},{32,96},{64,0},{96,32},{1,65},{33,97},{65,1},{97,33},{2,66}... | collective-permute-start | bytes 589832 | tf_op jit(solution)/shard_map/ppermute | solution.py:352
  452.4 13.4 %collective-permute-start.34 = (bf16[2,128,512]{2,1,0:T(8,128)(2,1)S(1)}, bf16[2,128,512]{2,1,0:T(8,128)(2,1)S(1)}, u32[]{:S(2)}, u32[]{:S(2)}) collective-permute-start(bf16[2,128,512]{2,1,0:T(8,128)(2,1)S(1)} %get-tuple-element.214), channel_id=1, source_target_pairs={{0,100},{1,101},{2,102},{3,103},{4,96},{5,97},{6,98},{7,99},{32,68... | collective-permute-start | bytes 786440 | tf_op jit(solution)/shard_map/ppermute | solution.py:359
  456.7 14.7 %collective-permute-start.33 = (bf16[2,128,512]{2,1,0:T(8,128)(2,1)S(1)}, bf16[2,128,512]{2,1,0:T(8,128)(2,1)S(1)}, u32[]{:S(2)}, u32[]{:S(2)}) collective-permute-start(bf16[2,128,512]{2,1,0:T(8,128)(2,1)S(1)} %get-tuple-element.215), channel_id=1, source_target_pairs={{0,68},{1,69},{2,70},{3,71},{4,64},{5,65},{6,66},{7,67},{32,100},{... | collective-permute-start | bytes 786440 | tf_op jit(solution)/shard_map/ppermute | solution.py:359
  457.5 13.9 %collective-permute-start.32 = (bf16[2,128,512]{2,1,0:T(8,128)(2,1)S(1)}, bf16[2,128,512]{2,1,0:T(8,128)(2,1)S(1)}, u32[]{:S(2)}, u32[]{:S(2)}) collective-permute-start(bf16[2,128,512]{2,1,0:T(8,128)(2,1)S(1)} %get-tuple-element.216), channel_id=1, source_target_pairs={{0,32},{32,0},{64,96},{96,64},{1,33},{33,1},{65,97},{97,65},{2,34}... | collective-permute-start | bytes 786440 | tf_op jit(solution)/shard_map/ppermute | solution.py:352
  457.5 15.9 %collective-permute-start.29 = (bf16[128,768]{1,0:T(8,128)(2,1)S(1)}, bf16[128,768]{1,0:T(8,128)(2,1)S(1)}, u32[]{:S(2)}, u32[]{:S(2)}) collective-permute-start(bf16[128,768]{1,0:T(8,128)(2,1)S(1)} %select_select_fusion.17.refs_4_), channel_id=1, source_target_pairs={{0,32},{32,0},{64,96},{96,64},{1,33},{33,1},{65,97},{97,65},{2,34}... | collective-permute-start | bytes 589832 | tf_op jit(solution)/shard_map/ppermute | solution.py:352
  458.0 15.4 %collective-permute-start.31 = (bf16[128,768]{1,0:T(8,128)(2,1)S(1)}, bf16[128,768]{1,0:T(8,128)(2,1)S(1)}, u32[]{:S(2)}, u32[]{:S(2)}) collective-permute-start(bf16[128,768]{1,0:T(8,128)(2,1)S(1)} %collective-permute-done.30.refs_6_), channel_id=1, source_target_pairs={{0,32},{32,0},{64,96},{96,64},{1,33},{33,1},{65,97},{97,65},{2,34}... | collective-permute-start | bytes 589832 | tf_op jit(solution)/shard_map/ppermute | solution.py:352
  (7 other events, 15.9 us)
Sparse Core Ops, SparseCore 0:
  9.7 42.8 all-gather.1

commit v5 on v4

--- a/solution.py
+++ b/solution.py
@@ -290,56 +290,59 @@
     )
 
 
-def rows_grad_kernel(n, splits, with_total, *refs):
-    a_refs, b_refs, refs = refs[:n], refs[n : 2 * n], refs[2 * n :]
-    totals, refs = (refs[: len(splits)], refs[len(splits) :]) if with_total else ((), refs)
-    outs, (a_all, b_all) = refs[: len(splits)], refs[len(splits) :]
-    rows = a_refs[0].shape[-2]
-
-    def place(to, piece, i):
-        at = pl.ds(i * rows, rows)
-        if len(piece.shape) == 2:
-            to[at, :] = piece[...]
-        else:
-            for b in range(piece.shape[0]):
-                to[at, pl.ds(b * piece.shape[2], piece.shape[2])] = piece[b]
-
-    for i in range(n):
-        place(a_all, a_refs[i], i)
-        place(b_all, b_refs[i], i)
-    for c in range(a_all.shape[1] // 256):
-        cols = pl.ds(c * 256, 256)
-        got = dot_tn(a_all[:, cols], b_all[...])
-        for i, (start, stop) in enumerate(splits):
-            part = got[:, start:stop]
-            outs[i][cols, :] = totals[i][cols, :] + part if with_total else part
-
-
-def rows_grad(a, b, widths, totals=()):
-    n = len(a)
-    wide = lambda x: x.shape[-1] * (x.shape[0] if x.ndim == 3 else 1)
-    rows = a[0].shape[-2]
-    splits, at = [], 0
-    for w in widths:
-        splits.append((at, at + w))
-        at += w
+def gather_rows(to, pieces):
+    per = to.shape[2] // pieces[0][0].shape[2]
+    for i, run in enumerate(pieces):
+        at = 0
+        for piece in run:
+            nblk, rows, dsh = piece.shape
+            for b in range(nblk):
+                cols = pl.ds((at + b) % per * dsh, dsh)
+                to[(at + b) // per, pl.ds(i * rows, rows), cols] = piece[b]
+            at += nblk
+
+
+def weight_grad_kernel(wide_first, runs, core_ref, *refs):
+    nwide = sum(runs)
+    wides, narrows, (mine_ref, give_ref, wide_all, narrow_all) = refs[:nwide], refs[nwide:-4], refs[-4:]
+    pieces, at = [], 0
+    for n in runs:
+        pieces.append(wides[at : at + n])
+        at += n
+    gather_rows(wide_all, pieces)
+    rows = narrows[0].shape[0]
+    for i, piece in enumerate(narrows):
+        narrow_all[pl.ds(i * rows, rows), :] = piece[...]
+    core = core_ref[0]
+    for out_ref, quarter in ((give_ref, 1 - core), (mine_ref, core)):
+        for c in range(out_ref.shape[0] // 256):
+            cols = pl.ds(c * 256, 256)
+            if wide_first:
+                got = dot_tn(wide_all[quarter, :, cols], narrow_all[...])
+            else:
+                got = dot_tn(narrow_all[:, cols], wide_all[quarter])
+            out_ref[cols, :] = got.astype(out_ref.dtype)
+
+
+def weight_grad(core, wide, narrow, wide_first):
+    rows, cols = narrow[0].shape
+    dsh = wide[0][0].shape[2]
+    width = sum(x.shape[0] for x in wide[0]) * dsh // 2
+    shape = (width, cols) if wide_first else (cols, width)
+    total = len(narrow) * rows
+    flat = [x for run in wide for x in run]
     return pl.pallas_call(
-        functools.partial(rows_grad_kernel, n, splits, bool(totals)),
-        out_shape=tuple(jax.ShapeDtypeStruct((wide(a[0]), w), F32) for w in widths),
-        in_specs=[in_vmem()] * (2 * n + len(totals)),
-        out_specs=tuple([in_vmem()] * len(widths)),
-        scratch_shapes=[
-            pltpu.VMEM((n * rows, wide(a[0])), BF16),
-            pltpu.VMEM((n * rows, wide(b[0])), BF16),
-        ],
+        functools.partial(weight_grad_kernel, wide_first, tuple(len(run) for run in wide)),
+        out_shape=(jax.ShapeDtypeStruct(shape, F32), jax.ShapeDtypeStruct(shape, BF16)),
+        in_specs=[in_smem()] + [in_vmem()] * (len(flat) + len(narrow)),
+        out_specs=(in_vmem(), in_vmem()),
+        scratch_shapes=[pltpu.VMEM((2, total, width), BF16), pltpu.VMEM((total, cols), BF16)],
         compiler_params=kernel_params(VMEM_LIMIT),
         cost_estimate=pl.CostEstimate(
-            flops=2 * n * rows * wide(a[0]) * wide(b[0]),
-            bytes_accessed=4 * wide(a[0]) * wide(b[0]),
-            transcendentals=0,
+            flops=4 * total * width * cols, bytes_accessed=6 * width * cols, transcendentals=0
         ),
         name="weight_grad",
-    )(*a, *b, *totals)
+    )(core, *flat, *narrow)
 
 
 def passed_along(x, axis, by):
@@ -406,6 +409,7 @@
     own = lax.dynamic_slice_in_dim(both, hi, 1, axis=0)[0]
     away = lax.dynamic_slice_in_dim(both, 1 - hi, 1, axis=0)[0]
     away = [away[j] for j in range(ntr)]
+    source, lengths, bounds, targets, away[0] = together(source, lengths, bounds, targets, away[0])
 
     def first(j):
         return own[j] + swapped(away[j], "dp", 2)
@@ -427,9 +431,11 @@
     spans = [jnp.where(section_at == n, lens[0], lens[1]).reshape(1) for n in range(nst + 1)]
     flags = [(section_at == s).astype(jnp.int32).reshape(1) for s in range(nst)]
     masks = [section_at == s for s in range(nst)]
-    quarter = peers // lax.axis_size("dp")
-    starts = [((rep ^ k) * quarter).astype(jnp.uint32) for k in range(4)]
+    half = peers // 2
+    mine_at = (hi * half).astype(jnp.uint32)
+    away_at = [((1 - hi) * half + n * half // 2).astype(jnp.uint32) for n in range(2)]
     block_at = tensor_at.astype(jnp.uint32)
+    core = core.astype(jnp.int32).reshape(1)
 
     def sum_of(got):
         return jnp.sum(got[:, :width].astype(F32), axis=0)
@@ -439,8 +445,8 @@
     for turn in range(nst):
         cur = first(turn) if turn < ntr else jnp.zeros((width, dsh), BF16)
         if turn == 0:
-            cur, factor, picks, hots, spans, flags, masks, starts, block_at = together(
-                cur, factor, picks, hots, spans, flags, masks, starts, block_at
+            cur, factor, picks, hots, spans, flags, masks, mine_at, away_at, block_at, core = together(
+                cur, factor, picks, hots, spans, flags, masks, mine_at, away_at, block_at, core
             )
         if arriving is not None:
             cur, arriving = together(cur, arriving)
@@ -458,6 +464,7 @@
         arriving = (cur.astype(F32) + sum_of(got)).astype(BF16)
         if turn == 0:
             away = [away[0], after(away[1], arriving)]
+        leaving = arriving
         arriving = passed_along(arriving, "section", 1)
 
     def end_cotangent(which, got, x):
@@ -465,11 +472,33 @@
 
     def own_block(blocks):
         return lax.dynamic_slice_in_dim(blocks, block_at, 1, axis=0)[0]
+
+    def chosen(choices, at=None, count=None):
+        if at is None:
+            return by_section(masks, choices)
+        return by_section(
+            masks, [lax.dynamic_slice_in_dim(x, at, count, axis=0) for x in choices]
+        )
+
+    def not_before(choices, mark):
+        return [after(x, mark) for x in choices]
+
+    seen = lambda name, which: [kept[s + which][name] for s in range(nst)]
+    back = lambda n, which: [taken[2 * nst - 1 - s + which][n] for s in range(nst)]
+
+    pieces = {}
+
+    def send_blocks(name, choices, n):
+        pieces[f"{name}.{n}"] = mirrored(chosen(choices, away_at[n], half // 2), 2)
+
+    def send_whole(name, choices):
+        pieces[name] = swapped(chosen(choices), "dp", 2)
 
     taken = {}
     g_top = end_cotangent(0, got, x)
     grad = own_block(g_top)
-    arriving, g_top, grad = together(arriving, g_top, grad)
+    send_blocks("h0", not_before(seen("h", 0), leaving), 0)
+    arriving, g_top, grad, pieces = together(arriving, g_top, grad, pieces)
     x = gathered(arriving)
     now = forward(spans[nst], x, weights, "ends", picks[1], nstep)
     d, dx = backward(
@@ -479,54 +508,21 @@
     kept.append(now)
     got = exchange(dx)
 
-    def chosen(choices, k=None):
-        if k is None:
-            return by_section(masks, choices)
-        cut = lambda x: lax.dynamic_slice_in_dim(x, starts[k], quarter, axis=0)
-        return by_section(masks, [cut(x) for x in choices])
-
-    def not_before(choices, mark):
-        return [after(x, mark) for x in choices]
-
-    seen = lambda name, which: [kept[s + which][name] for s in range(nst)]
-    back = lambda n, which: [taken[2 * nst - 1 - s + which][n] for s in range(nst)]
-
-    pieces = {}
-
-    def send_quarter(name, choices, k):
-        mine = chosen(choices, k)
-        if k:
-            mine = swapped(mine, "dp", k) if k == 1 else mirrored(mine, k)
-        pieces[name, k] = mine
-
-    def send_whole(name, choices):
-        mine = chosen(choices)
-        far = swapped(mine, "dp", 2)
-        pieces[name, 0], pieces[name, 2] = mine, far
-        pieces[name, 1], pieces[name, 3] = swapped(mine, "dp", 1), swapped(far, "dp", 1)
-
-    widths = (weights[0].shape[1], HEAD_DIM, HEAD_DIM)
-    wide_o = (quarter * dsh,)
-    of = lambda name: [pieces[name, k] for k in range(4)]
     for turn in range(nst + 1, 2 * nst + 1):
         grad = (grad.astype(F32) + sum_of(got)).astype(BF16)
         hs = [not_before(seen("h", w), grad) for w in range(ntr)]
         if turn == nst + 1:
             g_top = end_cotangent(1, got, x)
-            send_quarter("h0", hs[0], 2)
-        elif turn == nst + 2:
-            for name, which, k in (("h0", 0, 3), ("h0", 0, 1), ("h0", 0, 0), ("h1", 1, 2)):
-                send_quarter(name, hs[which], k)
-        elif turn == nst + 3:
-            for k in (3, 1, 0):
-                send_quarter("h1", hs[1], k)
-            for w in range(ntr):
-                send_whole(f"o{w}", not_before(seen("o", w), grad))
+            send_blocks("h0", hs[0], 1)
+        elif turn < 2 * nst:
+            n = turn - nst - 2
+            send_blocks("h1", hs[1], n)
+            send_whole(f"o{n}", not_before(seen("o", n), grad))
         else:
-            for k in range(4):
-                send_quarter("g0", not_before(back(1, 0), grad), k)
+            for n in range(2):
+                send_blocks("g0", not_before(back(1, 0), grad), n)
             send_whole("d0", not_before(back(0, 0), grad))
-        grad = after(passed_along(grad, "section", -1), *pieces.values())
+        grad, pieces = together(passed_along(grad, "section", -1), pieces)
         if turn == nst + 1:
             grad = jnp.where(masks[nst - 1], own_block(g_top), grad)
         g = gathered(grad)
@@ -538,17 +534,36 @@
             taken[turn] = (d, g)
             got = exchange(dx)
         else:
-            taken[turn] = (d, g)
-            for k in (2, 3, 1, 0):
-                send_quarter("g1", back(1, 1), k)
+            taken[turn] = (None, g)
+            for n in range(2):
+                send_blocks("g1", back(1, 1), n)
             (d,) = backward(flag, g, kept[early], kept[late], weights, False)
             taken[turn] = (d, g)
             send_whole("d1", back(0, 1))
 
-    total_qkv = rows_grad(of("h0"), of("d0"), widths)
-    total_o = rows_grad(of("o0"), of("g0"), wide_o)
-    (grad_o,) = rows_grad(of("o1"), of("g1"), wide_o, total_o)
-    grad_q, grad_k, grad_v = rows_grad(of("h1"), of("d1"), widths, total_qkv)
+    def wide(name, choices):
+        runs = []
+        for w in range(ntr):
+            runs.append((chosen(not_before(choices(w), g), mine_at, half),))
+            runs.append((pieces[f"{name}{w}.0"], pieces[f"{name}{w}.1"]))
+        return runs
+
+    def narrow(name, choices):
+        out = []
+        for w in range(ntr):
+            out += [chosen(not_before(choices(w), g)), pieces[f"{name}{w}"]]
+        return out
+
+    mine_o, give_o = weight_grad(
+        core, wide("g", lambda w: back(1, w)), narrow("o", lambda w: seen("o", w)), False
+    )
+    mine_d, give_d = weight_grad(
+        core, wide("h", lambda w: seen("h", w)), narrow("d", lambda w: back(0, w)), True
+    )
+    grad_o = mine_o + swapped(give_o, "dp", 1).astype(F32)
+    grad_d = mine_d + swapped(give_d, "dp", 1).astype(F32)
+    qcol = weights[0].shape[1]
+    grad_q, grad_k, grad_v = jnp.split(grad_d, (qcol, qcol + HEAD_DIM), axis=1)
     return (grad_q[None], grad_k[None], grad_v[None], grad_o[None])
 
 

time: 493 us -> 471 us (0.955)
  waiting for transfers between devices: 44.8 us -> 27 us
  blocking collectives: 262 us -> 248 us
  starting transfers between devices: 80.2 us -> 89 us
    ppermute x8, waiting for transfers between devices: 28 us -> 1.97 us  [mirrored(): return lax.ppermute(x, ('dp', 'tensor'), pairs)]
    all_to_all x17, blocking collectives: 262 us -> 248 us  [exchange(): lax.all_to_all(blocks, 'tensor', split_axis=0, concat_axis=0, tiled=True)]
    ppermute x19 -> x9, waiting for transfers between devices: 2.57 us -> 12 us  [swapped(): lax.ppermute(x, axis, [(i, i ^ mask) for i in range(lax.axis_size(axis))])]
    ppermute x19 -> x9, starting transfers between devices: 44.1 us -> 53.1 us  [swapped(): lax.ppermute(x, axis, [(i, i ^ mask) for i in range(lax.axis_size(axis))])]
  transfers between devices with their start and end apart: 36 -> 26, of which waited for: 16 -> 14; matrix products, arithmetic and copies ran while one was open for 2% -> 2% of each run, Pallas kernels for 3% -> 3%
where the time goes in v5:
time: 471 us; the launch traced here: 462 us
  blocking collectives  248 us (53%)
  starting transfers between devices  89 us (19%)
  Pallas kernels  50.6 us (11%)
  waiting for transfers between devices  27 us (6%)
  between operations  22.4 us (5%)
  local copies, waits for them, and re-layouts  16 us (3%)
  other arithmetic  8.58 us (2%)
    all_to_all x17, blocking collectives, exchange(): lax.all_to_all(blocks, 'tensor', split_axis=0, concat_axis=0, tiled=True)  248 us
    ppermute x9, starting transfers between devices, swapped(): lax.ppermute(x, axis, [(i, i ^ mask) for i in range(lax.axis_size(axis))])  53.1 us
    pallas_call x5, Pallas kernels, backward(): pl.pallas_call(functools.partial(backward_kernel, with_input, bool(ends))...  24.3 us
    ppermute x8, starting transfers between devices, passed_along(): return lax.ppermute(x, axis, pairs)  20.4 us
    pallas_call x5, Pallas kernels, forward(): pl.pallas_call(functools.partial(forward_kernel, mode, nstep), out_shape=...  16.5 us
    ppermute x8, starting transfers between devices, mirrored(): return lax.ppermute(x, ('dp', 'tensor'), pairs)  15.5 us
    ppermute x8, waiting for transfers between devices, passed_along(): return lax.ppermute(x, axis, pairs)  13 us
    ppermute x9, waiting for transfers between devices, swapped(): lax.ppermute(x, axis, [(i, i ^ mask) for i in range(lax.axis_size(axis))])  12 us
  transfers between devices with their start and end apart: 26, of which 14 were waited for; matrix products, arithmetic and copies ran while one was open for 2% of the time, Pallas kernels for 3%

profile of v5, /device:TPU:1, one launch (start us, length us, event | category | flops | bytes accessed | tf_op | source)
XLA Modules:
  0.0 462.1 jit_solution(1407478141696691466)
XLA Ops:
  16.6 2.8 collective-permute-start.1
  28.1 22.6 %all_to_all.85.x_ref = bf16[8,128,512]{2,1,0:T(8,128)(2,1)S(1)} all-to-all(bf16[8,128,512]{2,1,0:T(8,128)(2,1)S(1)} %broadcast_in_dim.134), channel_id=1, replica_groups=mesh['dp'=4,'section'=4,'tensor'=8] {'tensor'}, dimensions={0} | all-to-all | bytes 2097152 | tf_op jit(solution)/shard_map/all_to_all | solution.py:366
  50.7 2.2 copy-done.2
  52.9 2.2 copy-done.4
  55.1 3.0 forward_layer.5
  59.8 16.9 %all_to_all.86 = bf16[8,128,512]{2,1,0:T(8,128)(2,1)S(1)} all-to-all(bf16[8,128,512]{2,1,0:T(8,128)(2,1)} %copy-done.10), channel_id=1, replica_groups=mesh['dp'=4,'section'=4,'tensor'=8] {'tensor'}, dimensions={0} | all-to-all | bytes 2097152 | tf_op jit(solution)/shard_map/all_to_all | solution.py:366
  76.8 2.4 collective-permute-start.2
  79.2 3.3 collective-permute-start.3
  84.6 14.5 %all_to_all.87.x_ref = bf16[8,128,512]{2,1,0:T(8,128)(2,1)S(1)} all-to-all(bf16[8,128,512]{2,1,0:T(8,128)(2,1)S(1)} %broadcast_in_dim.135), channel_id=1, replica_groups=mesh['dp'=4,'section'=4,'tensor'=8] {'tensor'}, dimensions={0} | all-to-all | bytes 2097152 | tf_op jit(solution)/shard_map/all_to_all | solution.py:366
  99.1 2.2 copy-done.5
  101.3 3.0 forward_layer.6
  104.3 13.2 %all_to_all.88 = bf16[8,128,512]{2,1,0:T(8,128)(2,1)S(1)} all-to-all(bf16[8,128,512]{2,1,0:T(8,128)(2,1)S(1)} %get-tuple-element.177), channel_id=1, replica_groups=mesh['dp'=4,'section'=4,'tensor'=8] {'tensor'}, dimensions={0} | all-to-all | bytes 2097152 | tf_op jit(solution)/shard_map/all_to_all | solution.py:366
  117.7 4.1 collective-permute-start.4
  123.8 13.5 %all_to_all.89.x_ref = bf16[8,128,512]{2,1,0:T(8,128)(2,1)S(1)} all-to-all(bf16[8,128,512]{2,1,0:T(8,128)(2,1)S(1)} %broadcast_in_dim.136), channel_id=1, replica_groups=mesh['dp'=4,'section'=4,'tensor'=8] {'tensor'}, dimensions={0} | all-to-all | bytes 2097152 | tf_op jit(solution)/shard_map/all_to_all | solution.py:366
  137.4 3.0 forward_layer.7
  140.4 12.9 %all_to_all.90 = bf16[8,128,512]{2,1,0:T(8,128)(2,1)S(1)} all-to-all(bf16[8,128,512]{2,1,0:T(8,128)(2,1)S(1)} %get-tuple-element.183), channel_id=1, replica_groups=mesh['dp'=4,'section'=4,'tensor'=8] {'tensor'}, dimensions={0} | all-to-all | bytes 2097152 | tf_op jit(solution)/shard_map/all_to_all | solution.py:366
  153.5 3.6 collective-permute-start.5
  159.1 12.9 %all_to_all.91.x_ref = bf16[8,128,512]{2,1,0:T(8,128)(2,1)S(1)} all-to-all(bf16[8,128,512]{2,1,0:T(8,128)(2,1)S(1)} %broadcast_in_dim.137), channel_id=1, replica_groups=mesh['dp'=4,'section'=4,'tensor'=8] {'tensor'}, dimensions={0} | all-to-all | bytes 2097152 | tf_op jit(solution)/shard_map/all_to_all | solution.py:366
  172.0 4.3 forward_layer.8
  176.3 14.1 %all_to_all.92.got_ref = bf16[8,160,512]{2,1,0:T(8,128)(2,1)S(1)} all-to-all(bf16[8,160,512]{2,1,0:T(8,128)(2,1)S(1)} %get-tuple-element.188), channel_id=1, replica_groups=mesh['dp'=4,'section'=4,'tensor'=8] {'tensor'}, dimensions={0} | all-to-all | bytes 2621440 | tf_op jit(solution)/shard_map/all_to_all | solution.py:366
  190.7 3.2 collective-permute-start.7
  193.9 4.1 collective-permute-start.6
  198.0 3.2 step_end_grad.2.g_ref
  201.4 12.7 %all_to_all.93.x_ref = bf16[8,128,512]{2,1,0:T(8,128)(2,1)S(1)} all-to-all(bf16[8,128,512]{2,1,0:T(8,128)(2,1)S(1)} %broadcast_in_dim.138), channel_id=1, replica_groups=mesh['dp'=4,'section'=4,'tensor'=8] {'tensor'}, dimensions={0} | all-to-all | bytes 2097152 | tf_op jit(solution)/shard_map/all_to_all | solution.py:366
  214.1 3.1 forward_layer.9
  217.2 5.3 %backward_layer.4 = (bf16[128,768]{1,0:T(8,128)(2,1)S(1)}, bf16[8,160,512]{2,1,0:T(8,128)(2,1)S(1)}) custom-call(s32[1]{0:T(128)} %constant.61.clone.1.flag_ref, bf16[8,128,512]{2,1,0:T(8,128)(2,1)S(1)} %step_end_grad.2.g_ref, bf16[1280,128]{1,0:T(8,128)(2,1)S(1)} %get-tuple-element.202.pack0_ref.pack1_ref, ...), custom_call_target="tpu_custom_call" | custom-call | flops 1342177280 | bytes 10485760 | tf_op jit(solution)/shard_map/backward_layer/pallas_call | solution.py:274
  222.5 14.1 %all_to_all.94.got_ref = bf16[8,160,512]{2,1,0:T(8,128)(2,1)S(1)} all-to-all(bf16[8,160,512]{2,1,0:T(8,128)(2,1)S(1)} %get-tuple-element.208), channel_id=1, replica_groups=mesh['dp'=4,'section'=4,'tensor'=8] {'tensor'}, dimensions={0} | all-to-all | bytes 2621440 | tf_op jit(solution)/shard_map/all_to_all | solution.py:366
  238.5 3.2 step_end_grad.3
  243.8 12.8 %all_to_all.95.g_ref = bf16[8,128,512]{2,1,0:T(8,128)(2,1)S(1)} all-to-all(bf16[8,128,512]{2,1,0:T(8,128)(2,1)S(1)} %broadcast_in_dim.139), channel_id=1, replica_groups=mesh['dp'=4,'section'=4,'tensor'=8] {'tensor'}, dimensions={0} | all-to-all | bytes 2097152 | tf_op jit(solution)/shard_map/all_to_all | solution.py:366
  256.7 5.3 %backward_layer.5 = (bf16[128,768]{1,0:T(8,128)(2,1)S(1)}, bf16[8,128,512]{2,1,0:T(8,128)(2,1)S(1)}) custom-call(s32[1]{0:T(128)} %bitcast.19.flag_ref, bf16[8,128,512]{2,1,0:T(8,128)(2,1)S(1)} %all_to_all.95.g_ref, bf16[1280,128]{1,0:T(8,128)(2,1)S(1)} %get-tuple-element.219.pack0_ref.pack1_ref, bf16[1280,128]{1,0:T(8,128)(2,1)S(1)} %get-tuple-element.220.pack1_ref, ...), custom_call_target="tpu_custom_call" | custom-call | flops 1342177280 | bytes 10485760 | tf_op jit(solution)/shard_map/backward_layer/pallas_call | solution.py:274
  262.0 16.6 %all_to_all.96 = bf16[8,128,512]{2,1,0:T(8,128)(2,1)S(1)} all-to-all(bf16[8,128,512]{2,1,0:T(8,128)(2,1)S(1)} %get-tuple-element.224), channel_id=1, replica_groups=mesh['dp'=4,'section'=4,'tensor'=8] {'tensor'}, dimensions={0} | all-to-all | bytes 2097152 | tf_op jit(solution)/shard_map/all_to_all | solution.py:366
  278.9 2.0 collective-permute-start.11
  283.7 2.8 collective-permute-done.12.refs_7_
  288.2 13.8 %all_to_all.97.g_ref = bf16[8,128,512]{2,1,0:T(8,128)(2,1)S(1)} all-to-all(bf16[8,128,512]{2,1,0:T(8,128)(2,1)S(1)} %broadcast_in_dim.140), channel_id=1, replica_groups=mesh['dp'=4,'section'=4,'tensor'=8] {'tensor'}, dimensions={0} | all-to-all | bytes 2097152 | tf_op jit(solution)/shard_map/all_to_all | solution.py:366
  302.0 5.3 %backward_layer.6 = (bf16[128,768]{1,0:T(8,128)(2,1)S(1)}, bf16[8,128,512]{2,1,0:T(8,128)(2,1)S(1)}) custom-call(s32[1]{0:T(128)} %bitcast.18.flag_ref, bf16[8,128,512]{2,1,0:T(8,128)(2,1)S(1)} %all_to_all.97.g_ref, bf16[1280,128]{1,0:T(8,128)(2,1)S(1)} %get-tuple-element.241.pack0_ref.pack1_ref, ...), custom_call_target="tpu_custom_call" | custom-call | flops 1342177280 | bytes 10485760 | tf_op jit(solution)/shard_map/backward_layer/pallas_call | solution.py:274
  307.3 12.7 %all_to_all.98 = bf16[8,128,512]{2,1,0:T(8,128)(2,1)S(1)} all-to-all(bf16[8,128,512]{2,1,0:T(8,128)(2,1)S(1)} %get-tuple-element.243), channel_id=1, replica_groups=mesh['dp'=4,'section'=4,'tensor'=8] {'tensor'}, dimensions={0} | all-to-all | bytes 2097152 | tf_op jit(solution)/shard_map/all_to_all | solution.py:366
  320.3 4.7 %collective-permute-start.14 = (bf16[2,128,512]{2,1,0:T(8,128)(2,1)S(1)}, bf16[2,128,512]{2,1,0:T(8,128)(2,1)S(1)}, u32[]{:S(2)}, u32[]{:S(2)}) collective-permute-start(bf16[2,128,512]{2,1,0:T(8,128)(2,1)S(1)} %select_select_fusion.9), channel_id=1, source_target_pairs={{0,68},{1,69},{2,70},{3,71},{4,64},{5,65},{6,66},{7,67},{32,100},{... | collective-permute-start | bytes 786440 | tf_op jit(solution)/shard_map/ppermute | solution.py:362
  326.8 3.7 collective-permute-done.15.refs_9_
  331.4 16.6 %all_to_all.99.g_ref = bf16[8,128,512]{2,1,0:T(8,128)(2,1)S(1)} all-to-all(bf16[8,128,512]{2,1,0:T(8,128)(2,1)S(1)} %broadcast_in_dim.141), channel_id=1, replica_groups=mesh['dp'=4,'section'=4,'tensor'=8] {'tensor'}, dimensions={0} | all-to-all | bytes 2097152 | tf_op jit(solution)/shard_map/all_to_all | solution.py:366
  348.0 5.6 %backward_layer.7 = (bf16[128,768]{1,0:T(8,128)(2,1)S(1)}, bf16[8,128,512]{2,1,0:T(8,128)(2,1)S(1)}) custom-call(s32[1]{0:T(128)} %bitcast.17.flag_ref, bf16[8,128,512]{2,1,0:T(8,128)(2,1)S(1)} %all_to_all.99.g_ref, bf16[1280,128]{1,0:T(8,128)(2,1)S(1)} %get-tuple-element.259.pack0_ref, bf16[1280,128]{1,0:T(8,128)(2,1)S(1)} %get-tuple-element.219.pack0_ref.pack1_ref, ...), custom_call_target="tpu_custom_call" | custom-call | flops 1342177280 | bytes 10485760 | tf_op jit(solution)/shard_map/backward_layer/pallas_call | solution.py:274
  353.6 13.0 %all_to_all.100 = bf16[8,128,512]{2,1,0:T(8,128)(2,1)S(1)} all-to-all(bf16[8,128,512]{2,1,0:T(8,128)(2,1)S(1)} %get-tuple-element.261), channel_id=1, replica_groups=mesh['dp'=4,'section'=4,'tensor'=8] {'tensor'}, dimensions={0} | all-to-all | bytes 2097152 | tf_op jit(solution)/shard_map/all_to_all | solution.py:366
  366.9 2.0 collective-permute-start.19
  372.7 4.4 collective-permute-done.16
  378.4 15.4 %all_to_all.101.g_ref = bf16[8,128,512]{2,1,0:T(8,128)(2,1)S(1)} all-to-all(bf16[8,128,512]{2,1,0:T(8,128)(2,1)S(1)} %broadcast_in_dim.142), channel_id=1, replica_groups=mesh['dp'=4,'section'=4,'tensor'=8] {'tensor'}, dimensions={0} | all-to-all | bytes 2097152 | tf_op jit(solution)/shard_map/all_to_all | solution.py:366
  393.8 2.7 backward_heads.1
  404.7 38.1 %collective-permute-start.21 = (bf16[1024,768]{1,0:T(8,128)(2,1)S(1)}, bf16[1024,768]{1,0:T(8,128)(2,1)S(1)}, u32[]{:S(2)}, u32[]{:S(2)}) collective-permute-start(bf16[1024,768]{1,0:T(8,128)(2,1)S(1)} %get-tuple-element.299), channel_id=1, source_target_pairs={{0,32},{32,0},{64,96},{96,64},{1,33},{33,1},{65,97},{97,65},{2,34}... | collective-permute-start | bytes 4718600 | tf_op jit(solution)/shard_map/ppermute | solution.py:355
  444.4 3.4 collective-permute-start.24
  447.8 2.3 collective-permute-done.24
  (159 shorter events, 50.7 us)
Async XLA Ops:
  7.2 6.0 %copy-start = (s32[8]{0:T(128)S(1)}, s32[8]{0:T(128)}, u32[]{:S(2)}) copy-start(s32[8]{0:T(128)} %param.12) | copy-start | bytes 100
  7.2 5.9 %copy-start.21 = (s32[8]{0:T(128)S(1)}, s32[8]{0:T(128)}, u32[]{:S(2)}) copy-start(s32[8]{0:T(128)} %param.11) | copy-start | bytes 100
  7.2 8.1 %copy-start.20 = (s32[8,4]{0,1:T(4,128)S(1)}, s32[8,4]{0,1:T(4,128)}, u32[]{:S(2)}) copy-start(s32[8,4]{0,1:T(4,128)} %param.14) | copy-start | bytes 388
  7.2 7.3 %copy-start.19 = (s32[8,4]{0,1:T(4,128)S(1)}, s32[8,4]{0,1:T(4,128)}, u32[]{:S(2)}) copy-start(s32[8,4]{0,1:T(4,128)} %param.13) | copy-start | bytes 388
  7.2 52.5 %all-gather.2.cloned.1.call-start = ((), (), s32[]{:S(2)}) async-start(), calls=%async_computation.17 | async-start | bytes 1179648 | tf_op jit(solution)/shard_map/all_gather | solution.py:396
  9.2 3.0 collective-permute-start
  12.4 38.3 %copy-start.15 = (bf16[2,2,128,512]{3,2,1,0:T(8,128)(2,1)}, bf16[2,2,128,512]{3,2,1,0:T(8,128)(2,1)S(1)}, u32[]{:S(2)}) copy-start(bf16[2,2,128,512]{3,2,1,0:T(8,128)(2,1)S(1)} %select_add_fusion) | copy-start | bytes 1572868
  13.2 37.5 %copy-start.7 = (bf16[1,4096,128]{2,1,0:T(8,128)(2,1)S(1)}, bf16[1,4096,128]{2,1,0:T(8,128)(2,1)}, u32[]{:S(2)}) copy-start(bf16[1,4096,128]{2,1,0:T(8,128)(2,1)} %param.16) | copy-start | bytes 3145732
  13.2 37.5 %copy-start.8 = (bf16[1,4096,128]{2,1,0:T(8,128)(2,1)S(1)}, bf16[1,4096,128]{2,1,0:T(8,128)(2,1)}, u32[]{:S(2)}) copy-start(bf16[1,4096,128]{2,1,0:T(8,128)(2,1)} %param.17) | copy-start | bytes 3145732
  16.6 11.4 %collective-permute-start.1 = (bf16[128,512]{1,0:T(8,128)(2,1)S(1)}, bf16[128,512]{1,0:T(8,128)(2,1)S(1)}, u32[]{:S(2)}, u32[]{:S(2)}) collective-permute-start(bf16[128,512]{1,0:T(8,128)(2,1)S(1)} %get-tuple-element.160), channel_id=1, source_target_pairs={{0,64},{32,96},{64,0},{96,32},{1,65},{33,97},{65,1},{97,33},{2,66}... | collective-permute-start | bytes 393224 | tf_op jit(solution)/shard_map/ppermute | solution.py:355
  28.0 22.7 %copy-start.16 = (bf16[128,512]{1,0:T(8,128)(2,1)}, bf16[128,512]{1,0:T(8,128)(2,1)S(1)}, u32[]{:S(2)}) copy-start(bf16[128,512]{1,0:T(8,128)(2,1)S(1)} %fusion.1) | copy-start | bytes 393220
  50.7 2.2 copy-start.2
  52.9 2.2 copy-start.4
  58.1 1.0 copy-start.10
  59.1 0.6 copy-start.11
  59.8 17.0 %copy-start.17 = (bf16[128,512]{1,0:T(8,128)(2,1)S(1)}, bf16[128,512]{1,0:T(8,128)(2,1)}, u32[]{:S(2)}) copy-start(bf16[128,512]{1,0:T(8,128)(2,1)} %copy-done.16) | copy-start | bytes 393220
  59.8 17.1 %copy-start.18 = (bf16[128,512]{1,0:T(8,128)(2,1)S(1)}, bf16[128,512]{1,0:T(8,128)(2,1)}, u32[]{:S(2)}) copy-start(bf16[128,512]{1,0:T(8,128)(2,1)} %get-tuple-element.173) | copy-start | bytes 393220
  76.8 22.3 %copy-start.3 = (bf16[1,4096,512]{2,1,0:T(8,128)(2,1)S(1)}, bf16[1,4096,512]{2,1,0:T(8,128)(2,1)}, u32[]{:S(2)}) copy-start(bf16[1,4096,512]{2,1,0:T(8,128)(2,1)} %param.15) | copy-start | bytes 12582916
  76.8 5.7 %collective-permute-start.2 = (bf16[128,512]{1,0:T(8,128)(2,1)S(1)}, bf16[128,512]{1,0:T(8,128)(2,1)S(1)}, u32[]{:S(2)}, u32[]{:S(2)}) collective-permute-start(bf16[128,512]{1,0:T(8,128)(2,1)S(1)} %copy-done.18), channel_id=1, source_target_pairs={{0,64},{32,96},{64,0},{96,32},{1,65},{33,97},{65,1},{97,33},{2,66}... | collective-permute-start | bytes 393224 | tf_op jit(solution)/shard_map/ppermute | solution.py:355
  79.2 5.2 %collective-permute-start.3 = (bf16[128,512]{1,0:T(8,128)(2,1)S(1)}, bf16[128,512]{1,0:T(8,128)(2,1)S(1)}, u32[]{:S(2)}, u32[]{:S(2)}) collective-permute-start(bf16[128,512]{1,0:T(8,128)(2,1)S(1)} %add_convert_fusion.7), channel_id=1, source_target_pairs={{0,8},{8,16},{16,24},{1,9},{9,17},{17,25},{2,10},{10,18},{18,26},{... | collective-permute-start | bytes 393224 | tf_op jit(solution)/shard_map/ppermute | solution.py:351
  99.1 2.2 copy-start.5
  117.7 6.0 %collective-permute-start.4 = (bf16[128,512]{1,0:T(8,128)(2,1)S(1)}, bf16[128,512]{1,0:T(8,128)(2,1)S(1)}, u32[]{:S(2)}, u32[]{:S(2)}) collective-permute-start(bf16[128,512]{1,0:T(8,128)(2,1)S(1)} %add_convert_fusion.6), channel_id=1, source_target_pairs={{0,8},{8,16},{16,24},{1,9},{9,17},{17,25},{2,10},{10,18},{18,26},{... | collective-permute-start | bytes 393224 | tf_op jit(solution)/shard_map/ppermute | solution.py:351
  153.5 5.5 %collective-permute-start.5 = (bf16[128,512]{1,0:T(8,128)(2,1)S(1)}, bf16[128,512]{1,0:T(8,128)(2,1)S(1)}, u32[]{:S(2)}, u32[]{:S(2)}) collective-permute-start(bf16[128,512]{1,0:T(8,128)(2,1)S(1)} %add_convert_fusion.5), channel_id=1, source_target_pairs={{0,8},{8,16},{16,24},{1,9},{9,17},{17,25},{2,10},{10,18},{18,26},{... | collective-permute-start | bytes 393224 | tf_op jit(solution)/shard_map/ppermute | solution.py:351
  190.4 7.5 %copy-start.9 = (bf16[4096,128]{1,0:T(8,128)(2,1)S(1)}, bf16[4096,128]{1,0:T(8,128)(2,1)}, u32[]{:S(2)}) copy-start(bf16[4096,128]{1,0:T(8,128)(2,1)} %all-gather.2.cloned.1.call-done.class_ref) | copy-start | bytes 3145732
  190.4 7.6 %copy-start.14 = (f32[16,128]{1,0:T(8,128)S(1)}, f32[16,128]{1,0:T(8,128)}, u32[]{:S(2)}) copy-start(f32[16,128]{1,0:T(8,128)} %pad_convert_fusion.1.hot_ref) | copy-start | bytes 24580
  190.7 10.6 %collective-permute-start.7 = (bf16[2,128,512]{2,1,0:T(8,128)(2,1)S(1)}, bf16[2,128,512]{2,1,0:T(8,128)(2,1)S(1)}, u32[]{:S(2)}, u32[]{:S(2)}) collective-permute-start(bf16[2,128,512]{2,1,0:T(8,128)(2,1)S(1)} %select_select_fusion.12), channel_id=1, source_target_pairs={{0,68},{1,69},{2,70},{3,71},{4,64},{5,65},{6,66},{7,67},{32,100},{... | collective-permute-start | bytes 786440 | tf_op jit(solution)/shard_map/ppermute | solution.py:362
  193.9 7.4 %collective-permute-start.6 = (bf16[128,512]{1,0:T(8,128)(2,1)S(1)}, bf16[128,512]{1,0:T(8,128)(2,1)S(1)}, u32[]{:S(2)}, u32[]{:S(2)}) collective-permute-start(bf16[128,512]{1,0:T(8,128)(2,1)S(1)} %add_convert_fusion.4), channel_id=1, source_target_pairs={{0,8},{8,16},{16,24},{1,9},{9,17},{17,25},{2,10},{10,18},{18,26},{... | collective-permute-start | bytes 393224 | tf_op jit(solution)/shard_map/ppermute | solution.py:351
  198.0 16.1 %copy-start.6 = (bf16[1,512,4096]{2,1,0:T(8,128)(2,1)S(1)}, bf16[1,512,4096]{2,1,0:T(8,128)(2,1)}, u32[]{:S(2)}) copy-start(bf16[1,512,4096]{2,1,0:T(8,128)(2,1)} %param.18) | copy-start | bytes 12582916
  236.6 1.9 copy-start.13
  236.9 6.8 %collective-permute-start.9 = (bf16[2,128,512]{2,1,0:T(8,128)(2,1)S(1)}, bf16[2,128,512]{2,1,0:T(8,128)(2,1)S(1)}, u32[]{:S(2)}, u32[]{:S(2)}) collective-permute-start(bf16[2,128,512]{2,1,0:T(8,128)(2,1)S(1)} %select_select_fusion.11), channel_id=1, source_target_pairs={{0,68},{1,69},{2,70},{3,71},{4,64},{5,65},{6,66},{7,67},{32,100},{... | collective-permute-start | bytes 786440 | tf_op jit(solution)/shard_map/ppermute | solution.py:362
  237.0 6.0 %collective-permute-start.8 = (bf16[128,512]{1,0:T(8,128)(2,1)S(1)}, bf16[128,512]{1,0:T(8,128)(2,1)S(1)}, u32[]{:S(2)}, u32[]{:S(2)}) collective-permute-start(bf16[128,512]{1,0:T(8,128)(2,1)S(1)} %add_convert_fusion.3), channel_id=1, source_target_pairs={{8,0},{16,8},{24,16},{9,1},{17,9},{25,17},{10,2},{18,10},{26,18},{... | collective-permute-start | bytes 393224 | tf_op jit(solution)/shard_map/ppermute | solution.py:351
  278.6 2.3 copy-start.12
  278.9 9.2 %collective-permute-start.11 = (bf16[2,128,512]{2,1,0:T(8,128)(2,1)S(1)}, bf16[2,128,512]{2,1,0:T(8,128)(2,1)S(1)}, u32[]{:S(2)}, u32[]{:S(2)}) collective-permute-start(bf16[2,128,512]{2,1,0:T(8,128)(2,1)S(1)} %select_select_fusion.10), channel_id=1, source_target_pairs={{0,68},{1,69},{2,70},{3,71},{4,64},{5,65},{6,66},{7,67},{32,100},{... | collective-permute-start | bytes 786440 | tf_op jit(solution)/shard_map/ppermute | solution.py:362
  280.9 5.5 %collective-permute-start.12 = (bf16[128,512]{1,0:T(8,128)(2,1)S(1)}, bf16[128,512]{1,0:T(8,128)(2,1)S(1)}, u32[]{:S(2)}, u32[]{:S(2)}) collective-permute-start(bf16[128,512]{1,0:T(8,128)(2,1)S(1)} %select_select_fusion.20), channel_id=1, source_target_pairs={{0,64},{32,96},{64,0},{96,32},{1,65},{33,97},{65,1},{97,33},{2,66}... | collective-permute-start | bytes 393224 | tf_op jit(solution)/shard_map/ppermute | solution.py:355
  282.4 5.7 %collective-permute-start.10 = (bf16[128,512]{1,0:T(8,128)(2,1)S(1)}, bf16[128,512]{1,0:T(8,128)(2,1)S(1)}, u32[]{:S(2)}, u32[]{:S(2)}) collective-permute-start(bf16[128,512]{1,0:T(8,128)(2,1)S(1)} %add_convert_fusion.2), channel_id=1, source_target_pairs={{8,0},{16,8},{24,16},{9,1},{17,9},{25,17},{10,2},{18,10},{26,18},{... | collective-permute-start | bytes 393224 | tf_op jit(solution)/shard_map/ppermute | solution.py:351
  320.3 11.0 %collective-permute-start.14 = (bf16[2,128,512]{2,1,0:T(8,128)(2,1)S(1)}, bf16[2,128,512]{2,1,0:T(8,128)(2,1)S(1)}, u32[]{:S(2)}, u32[]{:S(2)}) collective-permute-start(bf16[2,128,512]{2,1,0:T(8,128)(2,1)S(1)} %select_select_fusion.9), channel_id=1, source_target_pairs={{0,68},{1,69},{2,70},{3,71},{4,64},{5,65},{6,66},{7,67},{32,100},{... | collective-permute-start | bytes 786440 | tf_op jit(solution)/shard_map/ppermute | solution.py:362
  325.0 5.4 %collective-permute-start.15 = (bf16[128,512]{1,0:T(8,128)(2,1)S(1)}, bf16[128,512]{1,0:T(8,128)(2,1)S(1)}, u32[]{:S(2)}, u32[]{:S(2)}) collective-permute-start(bf16[128,512]{1,0:T(8,128)(2,1)S(1)} %select_select_fusion.19), channel_id=1, source_target_pairs={{0,64},{32,96},{64,0},{96,32},{1,65},{33,97},{65,1},{97,33},{2,66}... | collective-permute-start | bytes 393224 | tf_op jit(solution)/shard_map/ppermute | solution.py:355
  325.5 5.8 %collective-permute-start.13 = (bf16[128,512]{1,0:T(8,128)(2,1)S(1)}, bf16[128,512]{1,0:T(8,128)(2,1)S(1)}, u32[]{:S(2)}, u32[]{:S(2)}) collective-permute-start(bf16[128,512]{1,0:T(8,128)(2,1)S(1)} %add_convert_fusion.1), channel_id=1, source_target_pairs={{8,0},{16,8},{24,16},{9,1},{17,9},{25,17},{10,2},{18,10},{26,18},{... | collective-permute-start | bytes 393224 | tf_op jit(solution)/shard_map/ppermute | solution.py:351
  366.9 10.2 %collective-permute-start.19 = (bf16[2,128,512]{2,1,0:T(8,128)(2,1)S(1)}, bf16[2,128,512]{2,1,0:T(8,128)(2,1)S(1)}, u32[]{:S(2)}, u32[]{:S(2)}) collective-permute-start(bf16[2,128,512]{2,1,0:T(8,128)(2,1)S(1)} %get-tuple-element.318), channel_id=1, source_target_pairs={{0,68},{1,69},{2,70},{3,71},{4,64},{5,65},{6,66},{7,67},{32,100},{... | collective-permute-start | bytes 786440 | tf_op jit(solution)/shard_map/ppermute | solution.py:362
  369.0 9.4 %collective-permute-start.18 = (bf16[2,128,512]{2,1,0:T(8,128)(2,1)S(1)}, bf16[2,128,512]{2,1,0:T(8,128)(2,1)S(1)}, u32[]{:S(2)}, u32[]{:S(2)}) collective-permute-start(bf16[2,128,512]{2,1,0:T(8,128)(2,1)S(1)} %get-tuple-element.319), channel_id=1, source_target_pairs={{0,68},{1,69},{2,70},{3,71},{4,64},{5,65},{6,66},{7,67},{32,100},{... | collective-permute-start | bytes 786440 | tf_op jit(solution)/shard_map/ppermute | solution.py:362
  369.7 7.4 %collective-permute-start.17 = (bf16[128,768]{1,0:T(8,128)(2,1)S(1)}, bf16[128,768]{1,0:T(8,128)(2,1)S(1)}, u32[]{:S(2)}, u32[]{:S(2)}) collective-permute-start(bf16[128,768]{1,0:T(8,128)(2,1)S(1)} %select_select_fusion.16), channel_id=1, source_target_pairs={{0,64},{32,96},{64,0},{96,32},{1,65},{33,97},{65,1},{97,33},{2,66}... | collective-permute-start | bytes 589832 | tf_op jit(solution)/shard_map/ppermute | solution.py:355
  371.4 5.7 %collective-permute-start.16 = (bf16[128,512]{1,0:T(8,128)(2,1)S(1)}, bf16[128,512]{1,0:T(8,128)(2,1)S(1)}, u32[]{:S(2)}, u32[]{:S(2)}) collective-permute-start(bf16[128,512]{1,0:T(8,128)(2,1)S(1)} %add_convert_fusion), channel_id=1, source_target_pairs={{8,0},{16,8},{24,16},{9,1},{17,9},{25,17},{10,2},{18,10},{26,18},{... | collective-permute-start | bytes 393224 | tf_op jit(solution)/shard_map/ppermute | solution.py:351
  396.5 6.2 %collective-permute-start.20 = (bf16[128,768]{1,0:T(8,128)(2,1)S(1)}, bf16[128,768]{1,0:T(8,128)(2,1)S(1)}, u32[]{:S(2)}, u32[]{:S(2)}) collective-permute-start(bf16[128,768]{1,0:T(8,128)(2,1)S(1)} %select_select_fusion.13), channel_id=1, source_target_pairs={{0,64},{32,96},{64,0},{96,32},{1,65},{33,97},{65,1},{97,33},{2,66}... | collective-permute-start | bytes 589832 | tf_op jit(solution)/shard_map/ppermute | solution.py:355
  397.9 45.0 %collective-permute-start.23 = (bf16[2,128,512]{2,1,0:T(8,128)(2,1)S(1)}, bf16[2,128,512]{2,1,0:T(8,128)(2,1)S(1)}, u32[]{:S(2)}, u32[]{:S(2)}) collective-permute-start(bf16[2,128,512]{2,1,0:T(8,128)(2,1)S(1)} %get-tuple-element.316), channel_id=1, source_target_pairs={{0,68},{1,69},{2,70},{3,71},{4,64},{5,65},{6,66},{7,67},{32,100},{... | collective-permute-start | bytes 786440 | tf_op jit(solution)/shard_map/ppermute | solution.py:362
  399.9 43.0 %collective-permute-start.22 = (bf16[2,128,512]{2,1,0:T(8,128)(2,1)S(1)}, bf16[2,128,512]{2,1,0:T(8,128)(2,1)S(1)}, u32[]{:S(2)}, u32[]{:S(2)}) collective-permute-start(bf16[2,128,512]{2,1,0:T(8,128)(2,1)S(1)} %get-tuple-element.317), channel_id=1, source_target_pairs={{0,68},{1,69},{2,70},{3,71},{4,64},{5,65},{6,66},{7,67},{32,100},{... | collective-permute-start | bytes 786440 | tf_op jit(solution)/shard_map/ppermute | solution.py:362
  404.7 47.1 %collective-permute-start.21 = (bf16[1024,768]{1,0:T(8,128)(2,1)S(1)}, bf16[1024,768]{1,0:T(8,128)(2,1)S(1)}, u32[]{:S(2)}, u32[]{:S(2)}) collective-permute-start(bf16[1024,768]{1,0:T(8,128)(2,1)S(1)} %get-tuple-element.299), channel_id=1, source_target_pairs={{0,32},{32,0},{64,96},{96,64},{1,33},{33,1},{65,97},{97,65},{2,34}... | collective-permute-start | bytes 4718600 | tf_op jit(solution)/shard_map/ppermute | solution.py:355
  444.4 5.7 %collective-permute-start.24 = (bf16[512,1024]{1,0:T(8,128)(2,1)S(1)}, bf16[512,1024]{1,0:T(8,128)(2,1)S(1)}, u32[]{:S(2)}, u32[]{:S(2)}) collective-permute-start(bf16[512,1024]{1,0:T(8,128)(2,1)S(1)} %get-tuple-element.315), channel_id=1, source_target_pairs={{0,32},{32,0},{64,96},{96,64},{1,33},{33,1},{65,97},{97,65},{2,34}... | collective-permute-start | bytes 3145736 | tf_op jit(solution)/shard_map/ppermute | solution.py:355
  452.1 2.7 copy-start.1
Sparse Core Ops, SparseCore 0:
  10.8 41.4 all-gather.1
